TPU v7x, 32 devices: a whole 2x2x4 slice. The times are simulated.
32 devices in a mesh: dp: 16 (over z, x, core), tensor: 2 (over y).
Axes of the slice: x: 2, y: 2, z: 4, core: 2. Of those that a mesh axis runs over, the one named last changes fastest.
Arguments:
- hidden: float32 [2, 4096, 2048], P(None, ('dp', 'tensor')), may hold values from -6 to 6
- cotangent: bfloat16 [2, 4096, 2048], P(None, ('dp', 'tensor')), may hold values from -6 to 6
- lengths: int32 [2, 16, 4], P(None, 'dp'), may hold values from 1 to 253, as said below
- order: int32 [2, 16, 4], P(None, 'dp'), may hold values from 0 to 3, each once within a row
- norm_gain: float32 [2048], P('dp'), may hold values from 0.5 to 1.5
- input_weight: bfloat16 [2048, 2, 4096], P('dp', None, 'tensor'), may hold values from -0.125 to 0.125
- conv_weight: float32 [4, 4096], P(None, ('tensor', 'dp')), may hold values from -3 to 3
- conv_bias: float32 [4096], P(('tensor', 'dp')), may hold values from -3 to 3
- select_weight: bfloat16 [4096, 160], P(('tensor', 'dp')), may hold values from -0.09375 to 0.09375
- step_weight: bfloat16 [128, 4096], P('dp', 'tensor'), may hold values from -0.5 to 0.5
- step_bias: float32 [4096], P(('tensor', 'dp')), may hold values from -7 to -2
- decay_log: float32 [16, 4096], P(None, ('tensor', 'dp')), may hold values from -1 to 2.8
- skip_gain: float32 [4096], P(('tensor', 'dp')), may hold values from 0.5 to 1.5
- output_weight: bfloat16 [4096, 2048], P('tensor', 'dp'), may hold values from -0.1875 to 0.1875
Outputs:
- layer_out: float32 [2, 4096, 2048], P(None, ('dp', 'tensor'))
- hidden_grad: float32 [2, 4096, 2048], P(None, ('dp', 'tensor'))
- norm_gain_grad: float32 [2048], P('dp')
- input_weight_grad: float32 [2048, 2, 4096], P('dp', None, 'tensor')
- conv_weight_grad: float32 [4, 4096], P(None, ('tensor', 'dp'))
- conv_bias_grad: float32 [4096], P(('tensor', 'dp'))
- select_weight_grad: float32 [4096, 160], P(('tensor', 'dp'))
- step_weight_grad: float32 [128, 4096], P('dp', 'tensor')
- step_bias_grad: float32 [4096], P(('tensor', 'dp'))
- decay_log_grad: float32 [16, 4096], P(None, ('tensor', 'dp'))
- skip_gain_grad: float32 [4096], P(('tensor', 'dp'))
- output_weight_grad: float32 [4096, 2048], P('tensor', 'dp')
Inputs may be any that keep to these rules, and one draw needn't show every extreme that they name: In each micro-batch and data index the 4 lengths sum to at most 256; the slots after their sum are padding.
All inputs are finite; a program needn't handle non-finite values.
Results may differ from a plain program's by a relative error of at most 0.0097.
Values may be sent and summed in bfloat16 or wider, within the bound.
No kernel may reach another device: no remote copies, remote signals or barrier semaphores. Data moves between devices by JAX's collectives and lax.ppermute only.
A program may use at most 384 MiB of HBM per device.

v0:
```python
import jax
import jax.numpy as jnp
from jax import lax
from jax.sharding import PartitionSpec as P

epsilon = 1e-05


def positions(length_row, order_row, slot_count):
    number = order_row.shape[0]
    picked = (order_row[:, None] == jnp.arange(number, dtype=jnp.int32)[None, :]).astype(jnp.int32)
    ordered = jnp.sum(picked * length_row[None, :], axis=1)
    seq_ends = jnp.cumsum(ordered)
    starts = jnp.concatenate([jnp.zeros((1,), jnp.int32), seq_ends])
    slot_ids = jnp.arange(slot_count, dtype=jnp.int32)
    seq_begin = jnp.max(jnp.where(starts[None, :] <= slot_ids[:, None], starts[None, :], 0), axis=1)
    return (slot_ids - seq_begin, (slot_ids < seq_ends[-1]).astype(jnp.float32))


def delayed(values, steps_back):
    if steps_back == 0:
        return values
    return jnp.concatenate(
        [jnp.zeros((steps_back,) + values.shape[1:], values.dtype), values[:-steps_back]], axis=0
    )


def advanced(values, steps_ahead):
    if steps_ahead == 0:
        return values
    return jnp.concatenate(
        [values[steps_ahead:], jnp.zeros((steps_ahead,) + values.shape[1:], values.dtype)], axis=0
    )


def decay_factor(step_blk, keep_blk, decay_rate):
    return jnp.exp(step_blk[:, None, :] * decay_rate[None]) * keep_blk[:, None, None]


def block_terms(step_blk, in_blk, act_blk, keep_blk, decay_rate):
    factor = decay_factor(step_blk, keep_blk, decay_rate)
    driven = (step_blk * act_blk)[:, None, :] * in_blk[:, :, None]
    return (factor, driven)


def run_block(start_state, factor, driven):

    def advance(state, parts):
        factor_row, driven_row = parts
        state = factor_row * state + driven_row
        return (state, state)

    _, states = lax.scan(advance, start_state, (factor, driven), unroll=8)
    return states


def adjoint_block(incoming, factor, emitted_grad):

    def retreat(carried, parts):
        factor_row, grad_row = parts
        adjoint_row = grad_row + carried
        return (factor_row * adjoint_row, adjoint_row)

    handed, adjoint = lax.scan(retreat, incoming, (factor, emitted_grad), reverse=True, unroll=8)
    return (handed, adjoint)


def on_device(
    hidden,
    cotangent,
    lengths,
    order,
    norm_gain,
    input_weight,
    conv_weight,
    conv_bias,
    select_weight,
    step_weight,
    step_bias,
    decay_log,
    skip_gain,
    output_weight,
):
    highest = lax.Precision.HIGHEST
    f32 = jnp.float32
    bf16 = jnp.bfloat16
    shard_rows = hidden.shape[1]
    group_tok = shard_rows * lax.axis_size("tensor")
    model_dim = hidden.shape[2]
    channels = input_weight.shape[2]
    block_len = min(128, group_tok)
    block_count = group_tok // block_len

    def to_blocks(values):
        return values.reshape((block_count, block_len) + values.shape[1:])

    summed = (
        jnp.zeros(input_weight.shape, f32),
        jnp.zeros(conv_weight.shape, f32),
        jnp.zeros(conv_bias.shape, f32),
        jnp.zeros(select_weight.shape, f32),
        jnp.zeros(step_weight.shape, f32),
        jnp.zeros(step_bias.shape, f32),
        jnp.zeros(decay_log.shape, f32),
        jnp.zeros(skip_gain.shape, f32),
        jnp.zeros(output_weight.shape, f32),
    )
    pending = None
    gain_acc = jnp.zeros((model_dim,), f32)
    layer_list = []
    grad_list = []
    for number in range(hidden.shape[0]):
        matrices = (
            lax.all_gather(input_weight, "dp", axis=0, tiled=True),
            lax.all_gather(select_weight, "dp", axis=0, tiled=True),
            lax.all_gather(step_weight, "dp", axis=0, tiled=True),
            lax.all_gather(output_weight, "dp", axis=1, tiled=True),
        )
        smaller = (
            lax.all_gather(norm_gain, "dp", axis=0, tiled=True),
            lax.all_gather(conv_weight, "dp", axis=1, tiled=True),
            lax.all_gather(conv_bias, "dp", axis=0, tiled=True),
            lax.all_gather(step_bias, "dp", axis=0, tiled=True),
            lax.all_gather(decay_log, "dp", axis=1, tiled=True),
            lax.all_gather(skip_gain, "dp", axis=0, tiled=True),
        )
        token_rows = hidden[number]
        cot_rows = cotangent[number]
        (w_in, w_sel, w_step, w_out), (gain_full, conv_w, conv_b, step_b, decay_lg, skip_g) = (
            matrices,
            smaller,
        )
        w_in_flat = w_in.reshape(model_dim, 2 * channels)
        rank_dim = w_step.shape[0]
        state_dim = decay_lg.shape[0]
        taps = conv_w.shape[0]
        position, live_mask = positions(lengths[number, 0], order[number, 0], group_tok)
        inverse_rms = lax.rsqrt(jnp.mean(token_rows * token_rows, axis=-1, keepdims=True) + epsilon)
        normal_rows = token_rows * inverse_rms
        normed_rows = (normal_rows * gain_full).astype(bf16)
        normed = lax.all_gather(normed_rows, "tensor", axis=0, tiled=True)
        projected = jnp.dot(normed, w_in_flat, preferred_element_type=f32)
        inner_part = projected[:, :channels]
        gate_part = projected[:, channels:]
        tap_masks = [
            (position >= taps - 1 - tap_index).astype(f32)[:, None] for tap_index in range(taps)
        ]
        convolved = jnp.zeros_like(inner_part) + conv_b
        for tap_index in range(taps):
            convolved = (
                convolved
                + conv_w[tap_index]
                * delayed(inner_part, taps - 1 - tap_index)
                * tap_masks[tap_index]
            )
        act_low = jax.nn.silu(convolved).astype(bf16)
        activated = act_low.astype(f32)
        selected = lax.psum(jnp.dot(act_low, w_sel, preferred_element_type=f32), "tensor")
        rank_low = selected[:, :rank_dim].astype(bf16)
        in_cols = selected[:, rank_dim : rank_dim + state_dim]
        out_cols = selected[:, rank_dim + state_dim :]
        pre_step = jnp.dot(rank_low, w_step, preferred_element_type=f32) + step_b
        step_size = jax.nn.softplus(pre_step)
        decay_rate = -jnp.exp(decay_lg)
        keep_mask = (position > 0).astype(f32)
        block_inputs = (
            to_blocks(step_size),
            to_blocks(in_cols),
            to_blocks(out_cols),
            to_blocks(activated),
            to_blocks(keep_mask),
        )

        def forward_block(carried, block_parts):
            step_blk, in_blk, out_blk, act_blk, keep_blk = block_parts
            factor, driven = block_terms(step_blk, in_blk, act_blk, keep_blk, decay_rate)
            states = run_block(carried, factor, driven)
            emitted = jnp.einsum("bs,bsc->bc", out_blk, states, precision=highest)
            return (states[-1], (carried, emitted, states))

        zero_state = jnp.zeros((state_dim, channels), f32)
        _, (block_starts, emitted, block_states) = lax.scan(forward_block, zero_state, block_inputs)
        scanned = emitted.reshape(group_tok, channels)
        branch_value = scanned + skip_g * activated
        gate_sig = jax.nn.sigmoid(gate_part)
        gate_act = gate_part * gate_sig
        gated_low = (branch_value * gate_act * live_mask[:, None]).astype(bf16)
        layer_rows = token_rows + lax.psum_scatter(
            jnp.dot(gated_low, w_out, preferred_element_type=f32).astype(jnp.bfloat16),
            "tensor",
            scatter_dimension=0,
            tiled=True,
        ).astype(jnp.float32)
        cot_full = lax.all_gather(cot_rows, "tensor", axis=0, tiled=True)
        out_grad = jnp.einsum("gc,gd->cd", gated_low, cot_full, preferred_element_type=f32)
        dgated = (
            jnp.einsum("gd,cd->gc", cot_full, w_out, preferred_element_type=f32)
            * live_mask[:, None]
        )
        dscan = dgated * gate_act
        dgate = dgated * branch_value * gate_sig * (1.0 + gate_part * (1.0 - gate_sig))
        skip_grad = jnp.sum(dscan * activated, axis=0)
        act_grad_sum = dscan * skip_g

        def backward_block(carried, block_parts):
            incoming, decay_acc = carried
            start_state, states, step_blk, in_blk, out_blk, act_blk, keep_blk, dscan_blk = (
                block_parts
            )
            factor = decay_factor(step_blk, keep_blk, decay_rate)
            previous = jnp.concatenate([start_state[None], states[:-1]], axis=0)
            emitted_grad = out_blk[:, :, None] * dscan_blk[:, None, :]
            handed, adjoint = adjoint_block(incoming, factor, emitted_grad)
            factor_grad = adjoint * previous * factor
            decay_acc = decay_acc + jnp.sum(factor_grad * step_blk[:, None, :], axis=0) * decay_rate
            input_sum = jnp.einsum("bsc,bs->bc", adjoint, in_blk, precision=highest)
            step_grad = jnp.sum(factor_grad * decay_rate[None], axis=1) + input_sum * act_blk
            act_grad = input_sum * step_blk
            in_grad = jnp.einsum("bsc,bc->bs", adjoint, step_blk * act_blk, precision=highest)
            out_col_grad = jnp.einsum("bc,bsc->bs", dscan_blk, states, precision=highest)
            return ((handed, decay_acc), (step_grad, act_grad, in_grad, out_col_grad))

        (_, decay_grad), (step_grads, act_grads, in_grads, out_col_grads) = lax.scan(
            backward_block,
            (zero_state, zero_state),
            (block_starts, block_states) + block_inputs + (to_blocks(dscan),),
            reverse=True,
        )
        act_grad_sum = act_grad_sum + act_grads.reshape(group_tok, channels)
        pre_grad_low = (step_grads.reshape(group_tok, channels) * jax.nn.sigmoid(pre_step)).astype(
            bf16
        )
        step_bias_grad = jnp.sum(pre_grad_low.astype(f32), axis=0)
        step_weight_grad = jnp.einsum(
            "gr,gc->rc", rank_low, pre_grad_low, preferred_element_type=f32
        )
        rank_grad = jnp.einsum("gc,rc->gr", pre_grad_low, w_step, preferred_element_type=f32)
        select_terms = jnp.concatenate(
            [
                rank_grad,
                in_grads.reshape(group_tok, state_dim),
                out_col_grads.reshape(group_tok, state_dim),
            ],
            axis=1,
        )
        select_low = lax.psum(select_terms, "tensor").astype(bf16)
        select_grad = jnp.einsum("gc,gk->ck", act_low, select_low, preferred_element_type=f32)
        act_grad_sum = act_grad_sum + jnp.einsum(
            "gk,ck->gc", select_low, w_sel, preferred_element_type=f32
        )
        conv_sig = jax.nn.sigmoid(convolved)
        dconv = act_grad_sum * conv_sig * (1.0 + convolved * (1.0 - conv_sig))
        conv_bias_grad = jnp.sum(dconv, axis=0)
        conv_rows = []
        dinner = jnp.zeros_like(inner_part)
        for tap_index in range(taps):
            delay_by = taps - 1 - tap_index
            masked_conv = dconv * tap_masks[tap_index]
            conv_rows.append(jnp.sum(masked_conv * delayed(inner_part, delay_by), axis=0))
            dinner = dinner + advanced(masked_conv, delay_by) * conv_w[tap_index]
        conv_weight_grad = jnp.stack(conv_rows, axis=0)
        dproj_low = jnp.concatenate([dinner, dgate], axis=1).astype(bf16)
        input_grad = jnp.einsum("gd,gk->dk", normed, dproj_low, preferred_element_type=f32).reshape(
            model_dim, 2, channels
        )
        dnormed = lax.psum_scatter(
            jnp.einsum("gk,dk->gd", dproj_low, w_in_flat, preferred_element_type=f32).astype(
                jnp.bfloat16
            ),
            "tensor",
            scatter_dimension=0,
            tiled=True,
        ).astype(jnp.float32)
        gain_part = jnp.sum(dnormed * normal_rows, axis=0)
        dnormal = dnormed * gain_full
        grad_rows = cot_rows.astype(f32) + inverse_rms * (
            dnormal - normal_rows * jnp.mean(dnormal * normal_rows, axis=-1, keepdims=True)
        )
        local_grads = (
            input_grad,
            conv_weight_grad,
            conv_bias_grad,
            select_grad,
            step_weight_grad,
            step_bias_grad,
            decay_grad,
            skip_grad,
            out_grad,
        )
        layer_rows, grad_rows, local_grads, gain_part = (
            layer_rows,
            grad_rows,
            local_grads,
            gain_part,
        )
        layer_list.append(layer_rows)
        grad_list.append(grad_rows)
        gain_acc = gain_acc + gain_part
        pending = local_grads if number == 0 else jax.tree.map(jnp.add, pending, local_grads)
    summed = (
        lax.psum_scatter(pending[0], "dp", scatter_dimension=0, tiled=True),
        lax.psum_scatter(pending[1], "dp", scatter_dimension=1, tiled=True),
        lax.psum_scatter(pending[2], "dp", scatter_dimension=0, tiled=True),
        lax.psum_scatter(pending[3], "dp", scatter_dimension=0, tiled=True),
        lax.psum_scatter(pending[4], "dp", scatter_dimension=0, tiled=True),
        lax.psum_scatter(pending[5], "dp", scatter_dimension=0, tiled=True),
        lax.psum_scatter(pending[6], "dp", scatter_dimension=1, tiled=True),
        lax.psum_scatter(pending[7], "dp", scatter_dimension=0, tiled=True),
        lax.psum_scatter(pending[8], "dp", scatter_dimension=1, tiled=True),
    )
    gain_total = lax.psum(gain_acc, ("dp", "tensor"))
    own_gain = lax.dynamic_slice_in_dim(
        gain_total, lax.axis_index("dp") * norm_gain.shape[0], norm_gain.shape[0]
    )
    return (
        jnp.stack(layer_list, axis=0),
        jnp.stack(grad_list, axis=0),
        own_gain,
        summed[0],
        summed[1],
        summed[2],
        summed[3],
        summed[4],
        summed[5],
        summed[6],
        summed[7],
        summed[8],
    )


def solution(mesh):
    in_specs = (
        P(None, ("dp", "tensor"), None),
        P(None, ("dp", "tensor"), None),
        P(None, "dp", None),
        P(None, "dp", None),
        P("dp"),
        P("dp", None, "tensor"),
        P(None, ("tensor", "dp")),
        P(("tensor", "dp")),
        P(("tensor", "dp"), None),
        P("dp", "tensor"),
        P(("tensor", "dp")),
        P(None, ("tensor", "dp")),
        P(("tensor", "dp")),
        P("tensor", "dp"),
    )
    out_specs = (
        P(None, ("dp", "tensor"), None),
        P(None, ("dp", "tensor"), None),
        P("dp"),
        P("dp", None, "tensor"),
        P(None, ("tensor", "dp")),
        P(("tensor", "dp")),
        P(("tensor", "dp"), None),
        P("dp", "tensor"),
        P(("tensor", "dp")),
        P(None, ("tensor", "dp")),
        P(("tensor", "dp")),
        P("tensor", "dp"),
    )
    return jax.shard_map(
        on_device, mesh=mesh, in_specs=in_specs, out_specs=out_specs, check_vma=False
    )
```

profile of v0, /device:TPU:0, one launch (start us, length us, event | category | flops | bytes accessed | tf_op | source)
XLA Modules:
  0.0 3187.7 jit_solution(3934016503548709411)
XLA Ops:
  120.9 26.4 all-gather.15.cloned.1.call-done
  215.2 80.1 %all-gather.17.cloned.1.call-done = bf16[2048,2048]{1,0:T(8,128)(2,1)} async-done(((bf16[2048,128]{1,0:T(8,128)(2,1)}), bf16[2048,2048]{1,0:T(8,128)(2,1)}) %all-gather.17.cloned.1.call-update) | async-done | bytes 8388624 | tf_op jit(solution)/shard_map/all_gather | solution.py:117
  418.9 373.6 %while.171 = (s32[]{:T(128)}, f32[16,2048]{1,0:T(8,128)S(1)}, f32[2,16,2048]{2,1,0:T(8,128)}, f32[2,128,2048]{2,1,0:T(8,128)}, f32[2,128,16,2048]{3,2,1,0:T(8,12...) while((s32[]{:T(128)}, f32[16,2048]{1,0:T(8,128)S(1)}, ...), condition=%wide.region_8.9_spmd, body=%wide.region_5.8_spmd.sunk | while | flops 63766536 | bytes 174412736 | solution.py:182
  436.4 147.8 %while.178 = (s32[]{:T(128)}, f32[16,2048]{1,0:T(8,128)S(1)}, f32[16,8,16,2048]{3,2,1,0:T(8,128)}, f32[16,8,16,2048]{3,2,1,0:T(8,128)}, f32[16,8,16,2048]{3,2,1,...) while((s32[]{:T(128)}, f32[16,2048]{1,0:T(8,128)S(1)}, ...), condition=%wide.region_7.7_spmd, body=%wide.region_6.6_spmd.sunk | while | flops 589832 | bytes 7471893 | solution.py:53
  623.3 147.8 %while.178 = (s32[]{:T(128)}, f32[16,2048]{1,0:T(8,128)S(1)}, f32[16,8,16,2048]{3,2,1,0:T(8,128)}, f32[16,8,16,2048]{3,2,1,0:T(8,128)}, f32[16,8,16,2048]{3,2,1,...) while((s32[]{:T(128)}, f32[16,2048]{1,0:T(8,128)S(1)}, ...), condition=%wide.region_7.7_spmd, body=%wide.region_6.6_spmd.sunk | while | flops 589832 | bytes 7471893 | solution.py:53
  796.9 421.4 %while.175 = (s32[]{:T(128)}, f32[16,2048]{1,0:T(8,128)S(1)}, f32[16,2048]{1,0:T(8,128)}, f32[2,128,2048]{2,1,0:T(8,128)}, f32[2,128,2048]{2,1,0:T(8,128)}, /*in...) while((s32[]{:T(128)}, f32[16,2048]{1,0:T(8,128)S(1)}, ...), condition=%wide.region_25.26_spmd.clone, body=%wide.region_20.25_spmd.clone.sunk | while | flops 215318544 | bytes 422883776 | solution.py:223
  824.4 76.1 %while.180 = (s32[]{:T(128)}, f32[16,2048]{1,0:T(8,128)S(1)}, f32[16,8,16,2048]{3,2,1,0:T(8,128)}, f32[16,8,16,2048]{3,2,1,0:T(8,128)}, f32[16,8,16,2048]{3,2,1,...) while((s32[]{:T(128)}, f32[16,2048]{1,0:T(8,128)S(1)}, ...), condition=%wide.region_22.22_spmd, body=%wide.region_21.21_spmd.sunk | while | flops 557065 | bytes 7602461 | solution.py:64
  956.0 23.9 fusion.274
  1030.6 76.1 %while.180 = (s32[]{:T(128)}, f32[16,2048]{1,0:T(8,128)S(1)}, f32[16,8,16,2048]{3,2,1,0:T(8,128)}, f32[16,8,16,2048]{3,2,1,0:T(8,128)}, f32[16,8,16,2048]{3,2,1,...) while((s32[]{:T(128)}, f32[16,2048]{1,0:T(8,128)S(1)}, ...), condition=%wide.region_22.22_spmd, body=%wide.region_21.21_spmd.sunk | while | flops 557065 | bytes 7602461 | solution.py:64
  1237.7 374.9 %while.173 = (s32[]{:T(128)}, f32[16,2048]{1,0:T(8,128)S(1)}, f32[2,16,2048]{2,1,0:T(8,128)}, f32[2,128,2048]{2,1,0:T(8,128)}, f32[2,128,16,2048]{3,2,1,0:T(8,12...) while((s32[]{:T(128)}, f32[16,2048]{1,0:T(8,128)S(1)}, ...), condition=%wide.region_18.19_spmd, body=%wide.region_15.18_spmd.sunk | while | flops 63766536 | bytes 173888432 | solution.py:182
  1255.9 147.8 %while.179 = (s32[]{:T(128)}, f32[16,2048]{1,0:T(8,128)S(1)}, f32[16,8,16,2048]{3,2,1,0:T(8,128)}, f32[16,8,16,2048]{3,2,1,0:T(8,128)}, f32[16,8,16,2048]{3,2,1,...) while((s32[]{:T(128)}, f32[16,2048]{1,0:T(8,128)S(1)}, ...), condition=%wide.region_17.17_spmd, body=%wide.region_16.16_spmd.sunk | while | flops 589832 | bytes 7471893 | solution.py:53
  1443.3 147.8 %while.179 = (s32[]{:T(128)}, f32[16,2048]{1,0:T(8,128)S(1)}, f32[16,8,16,2048]{3,2,1,0:T(8,128)}, f32[16,8,16,2048]{3,2,1,0:T(8,128)}, f32[16,8,16,2048]{3,2,1,...) while((s32[]{:T(128)}, f32[16,2048]{1,0:T(8,128)S(1)}, ...), condition=%wide.region_17.17_spmd, body=%wide.region_16.16_spmd.sunk | while | flops 589832 | bytes 7471893 | solution.py:53
  1617.1 438.6 %while.177 = (s32[]{:T(128)}, f32[16,2048]{1,0:T(8,128)S(1)}, f32[16,2048]{1,0:T(8,128)}, f32[2,128,2048]{2,1,0:T(8,128)}, f32[2,128,2048]{2,1,0:T(8,128)}, /*in...) while((s32[]{:T(128)}, f32[16,2048]{1,0:T(8,128)S(1)}, ...), condition=%wide.region_34.35_spmd.clone, body=%wide.region_29.34_spmd.clone.sunk | while | flops 215318544 | bytes 422351200 | solution.py:223
  1661.4 76.1 %while.181 = (s32[]{:T(128)}, f32[16,2048]{1,0:T(8,128)S(1)}, f32[16,8,16,2048]{3,2,1,0:T(8,128)}, f32[16,8,16,2048]{3,2,1,0:T(8,128)}, f32[16,8,16,2048]{3,2,1,...) while((s32[]{:T(128)}, f32[16,2048]{1,0:T(8,128)S(1)}, ...), condition=%wide.region_31.31_spmd, body=%wide.region_30.30_spmd.sunk | while | flops 557065 | bytes 7602461 | solution.py:64
  1867.7 76.1 %while.181 = (s32[]{:T(128)}, f32[16,2048]{1,0:T(8,128)S(1)}, f32[16,8,16,2048]{3,2,1,0:T(8,128)}, f32[16,8,16,2048]{3,2,1,0:T(8,128)}, f32[16,8,16,2048]{3,2,1,...) while((s32[]{:T(128)}, f32[16,2048]{1,0:T(8,128)S(1)}, ...), condition=%wide.region_31.31_spmd, body=%wide.region_30.30_spmd.sunk | while | flops 557065 | bytes 7602461 | solution.py:64
  2160.3 25.5 convolution_add_fusion
  2185.8 42.7 %add.571 = f32[2048,2,2048]{2,1,0:T(2,128)} reshape(f32[2048,4096]{1,0:T(8,128)} %convolution_add_fusion) | data formatting | bytes 67108864 | tf_op jit(solution)/shard_map/add | solution.py:299
  2252.0 61.0 %all-reduce.16 = (f32[2048]{0:T(1024)S(1)}, f32[2048]{0:T(1024)S(1)}, f32[2048]{0:T(1024)S(1)}) all-reduce(f32[2048]{0:T(1024)S(1)} %add.573, f32[2048]{0:T(1024)S(1)} %add.576, f32[2048]{0:T(1024)S(1)} %add.578), channel_id=10, replica_groups=mesh['dp'=16,'tensor'=2] {'dp'}, use_global_device_ids=true, to_apply=%region_53.54.clone | all-reduce | flops 6144 | bytes 49152
  2318.3 38.2 %psum.39 = f32[2048]{0:T(1024)S(1)} all-reduce(f32[2048]{0:T(1024)S(1)} %add.568), channel_id=1, replica_groups=mesh['dp'=16,'tensor'=2] {'dp','tensor'}, use_global_device_ids=true, to_apply=%region_40.41 | all-reduce | flops 2048 | bytes 16384 | tf_op jit(solution)/shard_map/psum | solution.py:311
  2362.4 457.7 %all-reduce.23.cloned.1.call-done = f32[2048,2,2048]{2,1,0:T(2,128)} async-done(((f32[2048,2,2048]{2,1,0:T(2,128)}), f32[2048,2,2048]{2,1,0:T(2,128)}) %all-reduce.23.cloned.1.call-update) | async-done | bytes 33554448
  2823.2 53.2 %reduce-scatter.24.cloned.1.call-done = f32[16,128]{1,0:T(8,128)} async-done(((f32[16,2048]{1,0:T(8,128)}), f32[16,128]{1,0:T(8,128)}) %reduce-scatter.24.cloned.1.call-update) | async-done | bytes 8208 | tf_op jit(solution)/shard_map/reduce_scatter | solution.py:307
  2876.4 60.5 %reduce-scatter.22.cloned.1.call-done = f32[8,2048]{1,0:T(8,128)} async-done(((f32[128,2048]{1,0:T(8,128)}), f32[8,2048]{1,0:T(8,128)}) %reduce-scatter.22.cloned.1.call-update) | async-done | bytes 65552 | tf_op jit(solution)/shard_map/reduce_scatter | solution.py:305
  2936.9 61.8 %reduce-scatter.20.cloned.1.call-done = f32[128,160]{0,1:T(8,128)} async-done(((f32[2048,160]{0,1:T(8,128)}), f32[128,160]{0,1:T(8,128)}) %reduce-scatter.20.cloned.1.call-update) | async-done | bytes 81936 | tf_op jit(solution)/shard_map/reduce_scatter | solution.py:304
  2998.7 182.3 %reduce-scatter.26.cloned.1.call-done = f32[2048,128]{1,0:T(8,128)} async-done(((f32[2048,2048]{1,0:T(8,128)}), f32[2048,128]{1,0:T(8,128)}) %reduce-scatter.26.cloned.1.call-update) | async-done | bytes 1048592 | tf_op jit(solution)/shard_map/reduce_scatter | solution.py:309
  (2036 shorter events, 2017.2 us)
Async XLA Ops:
  7.2 140.1 %all-gather.15.cloned.1.call-start = ((), (), s32[]{:S(2)}) async-start(), calls=%async_computation.10 | async-start | bytes 17825792 | tf_op jit(solution)/shard_map/all_gather | solution.py:114
  7.9 161.0 %all-gather.19.cloned.1.call-start = ((), (), s32[]{:S(2)}) async-start(), calls=%async_computation.13 | async-start | bytes 1572864 | tf_op jit(solution)/shard_map/all_gather | solution.py:141
  34.3 158.2 %all-gather.13.cloned.1.call-start = ((), (), s32[]{:S(2)}) async-start(), calls=%async_computation.9 | async-start | bytes 1572864 | tf_op jit(solution)/shard_map/all_gather | solution.py:141
  35.0 180.2 %all-gather.23.cloned.1.call-start = ((), (), s32[]{:S(2)}) async-start(), calls=%async_computation.22 | async-start | bytes 1572864 | tf_op jit(solution)/shard_map/all_gather | solution.py:194
  36.2 259.1 %all-gather.17.cloned.1.call-start = ((), (), s32[]{:S(2)}) async-start(), calls=%async_computation.11 | async-start | bytes 8912896 | tf_op jit(solution)/shard_map/all_gather | solution.py:117
  36.8 279.5 %all-gather.21.cloned.1.call-start = ((), (), s32[]{:S(2)}) async-start(), calls=%async_computation.21 | async-start | bytes 1572864 | tf_op jit(solution)/shard_map/all_gather | solution.py:194
  37.3 359.0 %all-reduce.25.cloned.1.call-start = ((), (), s32[]{:S(2)}) async-start(), calls=%async_computation.25 | async-start | bytes 655360 | tf_op jit(solution)/shard_map/psum | solution.py:158
  39.5 276.7 %copy-start.136 = (f32[256]{0:T(256)}, f32[256]{0:T(256)S(1)}, u32[]{:S(2)}) copy-start(f32[256]{0:T(256)S(1)} %get-tuple-element.1750) | copy-start | bytes 3076
  39.5 276.7 %copy-start.140 = (f32[256]{0:T(256)}, f32[256]{0:T(256)S(1)}, u32[]{:S(2)}) copy-start(f32[256]{0:T(256)S(1)} %get-tuple-element.1747) | copy-start | bytes 3076
  39.5 276.7 %copy-start.142 = (f32[256]{0:T(256)}, f32[256]{0:T(256)S(1)}, u32[]{:S(2)}) copy-start(f32[256]{0:T(256)S(1)} %get-tuple-element.1748) | copy-start | bytes 3076
  39.5 276.7 %copy-start.144 = (f32[256]{0:T(256)}, f32[256]{0:T(256)S(1)}, u32[]{:S(2)}) copy-start(f32[256]{0:T(256)S(1)} %get-tuple-element.1749) | copy-start | bytes 3076
  57.7 258.5 %copy-start.103 = (f32[1,2048]{1,0:T(1,128)}, f32[1,2048]{1,0:T(1,128)S(1)}, u32[]{:S(2)}) copy-start(f32[1,2048]{1,0:T(1,128)S(1)} %get-tuple-element.1741) | copy-start | bytes 24580
  57.8 258.5 %copy-start.105 = (f32[1,2048]{1,0:T(1,128)}, f32[1,2048]{1,0:T(1,128)S(1)}, u32[]{:S(2)}) copy-start(f32[1,2048]{1,0:T(1,128)S(1)} %get-tuple-element.1742) | copy-start | bytes 24580
  57.8 258.5 %copy-start.107 = (f32[1,2048]{1,0:T(1,128)}, f32[1,2048]{1,0:T(1,128)S(1)}, u32[]{:S(2)}) copy-start(f32[1,2048]{1,0:T(1,128)S(1)} %get-tuple-element.1743) | copy-start | bytes 24580
  331.6 1983.1 %reduce-scatter.28.cloned.1.call-start = ((), (), s32[]{:S(2)}) async-start(), calls=%async_computation.23 | async-start | bytes 1114112
  2103.6 212.7 %reduce-scatter.18.cloned.1.call-start = ((), (), s32[]{:S(2)}) async-start(), calls=%async_computation.16 | async-start | bytes 1572864 | tf_op jit(solution)/shard_map/reduce_scatter | solution.py:266
  2116.0 200.3 %reduce-scatter.16.cloned.1.call-start = ((), (), s32[]{:S(2)}) async-start(), calls=%async_computation.15 | async-start | bytes 1572864 | tf_op jit(solution)/shard_map/reduce_scatter | solution.py:266
  2128.1 228.9 %reduce-scatter.14.cloned.1.call-start = ((), (), s32[]{:S(2)}) async-start(), calls=%async_computation.14 | async-start | bytes 1572864 | tf_op jit(solution)/shard_map/reduce_scatter | solution.py:188
  2134.9 222.1 %reduce-scatter.12.cloned.1.call-start = ((), (), s32[]{:S(2)}) async-start(), calls=%async_computation.12 | async-start | bytes 1572864 | tf_op jit(solution)/shard_map/reduce_scatter | solution.py:188
  2142.5 677.6 %all-reduce.23.cloned.1.call-start = ((), (), s32[]{:S(2)}) async-start(), calls=%async_computation.24 | async-start | bytes 67108864
  2228.5 647.9 %reduce-scatter.24.cloned.1.call-start = ((), (), s32[]{:S(2)}) async-start(), calls=%async_computation.19 | async-start | bytes 139264 | tf_op jit(solution)/shard_map/reduce_scatter | solution.py:307
  2232.3 704.6 %reduce-scatter.22.cloned.1.call-start = ((), (), s32[]{:S(2)}) async-start(), calls=%async_computation.18 | async-start | bytes 1114112 | tf_op jit(solution)/shard_map/reduce_scatter | solution.py:305
  2235.3 763.4 %reduce-scatter.20.cloned.1.call-start = ((), (), s32[]{:S(2)}) async-start(), calls=%async_computation.17 | async-start | bytes 1392640 | tf_op jit(solution)/shard_map/reduce_scatter | solution.py:304
  2237.6 943.3 %reduce-scatter.26.cloned.1.call-start = ((), (), s32[]{:S(2)}) async-start(), calls=%async_computation.20 | async-start | bytes 17825792 | tf_op jit(solution)/shard_map/reduce_scatter | solution.py:309
  (236 other events, 4660.4 us)
Sparse Core Ops, SparseCore 0:
  10.2 137.0 all-gather.14
  149.4 19.5 all-gather.18
  171.1 21.2 all-gather.12
  193.8 21.2 all-gather.22
  217.2 78.0 all-gather.16
  296.7 19.4 all-gather.20
  331.7 24.4 all-reduce.24
  2103.7 54.6 reduce-scatter.27
  2160.6 19.3 reduce-scatter.17
  2182.8 20.3 reduce-scatter.15
  2205.4 20.2 reduce-scatter.13
  2227.9 20.3 reduce-scatter.11
  2252.4 567.6 all-reduce.22
  2824.3 52.0 reduce-scatter.23
  2880.4 56.4 reduce-scatter.21
  2941.4 57.2 reduce-scatter.19
  3003.2 177.6 reduce-scatter.25
where the time goes:
time: 3210 us; the launch traced here: 3190 us
  other arithmetic  1030 us (32%)
  waiting for transfers between devices  953 us (30%)
  matrix products  448 us (14%)
  local copies, waits for them, and re-layouts  421 us (13%)
  blocking collectives  276 us (9%)
  loops' own time  41.2 us (1%)
    while x516, other arithmetic  565 us
    unnamed x19, waiting for transfers between devices  460 us
    reduce_scatter x1, waiting for transfers between devices, on_device(): lax.psum_scatter(pending[8], 'dp', scatter_dimension=1, tiled=True)  182 us
    dynamic_update_slice x128, local copies, waits for them, and re-layouts, run_block(): _, states = lax.scan(advance, start_state, (factor, driven), unroll=8)  138 us
    dot_general x4, matrix products, backward_block(): jnp.einsum('bsc,bc->bs', adjoint, step_blk * act_blk, precision=highest)  95.8 us
    dot_general x4, matrix products, backward_block(): jnp.einsum('bc,bsc->bs', dscan_blk, states, precision=highest)  90.1 us
    all_gather x1, waiting for transfers between devices, on_device(): lax.all_gather(output_weight, 'dp', axis=1, tiled=True)  80.1 us
    mul x8, other arithmetic, decay_factor(): jnp.exp(step_blk[:, None, :] * decay_rate[None]) * keep_blk[:, None, None]  68.6 us
  transfers between devices with their start and end apart: 17, of which 11 were waited for; matrix products, arithmetic and copies ran while one was open for 7% of the time, Pallas kernels for 0%

commit v1 on v0

v1 whole, which is shorter than its diff:
```python
import functools

import jax
import jax.numpy as jnp
from jax import lax
from jax.experimental import pallas as pl
from jax.experimental.pallas import tpu as pltpu
from jax.sharding import PartitionSpec as P

epsilon = 1e-05
log2e = 1.4426950408889634
far = 1e6
chunk = 16
f32 = jnp.float32
bf16 = jnp.bfloat16
highest = lax.Precision.HIGHEST
last_dims = (((1,), (1,)), ((), ()))
first_dims = (((0,), (0,)), ((), ()))


def positions(length_row, order_row, slot_count):
    number = order_row.shape[0]
    picked = (order_row[:, None] == jnp.arange(number, dtype=jnp.int32)[None, :]).astype(jnp.int32)
    ordered = jnp.sum(picked * length_row[None, :], axis=1)
    seq_ends = jnp.cumsum(ordered)
    starts = jnp.concatenate([jnp.zeros((1,), jnp.int32), seq_ends])
    slot_ids = jnp.arange(slot_count, dtype=jnp.int32)
    seq_begin = jnp.max(jnp.where(starts[None, :] <= slot_ids[:, None], starts[None, :], 0), axis=1)
    return (slot_ids - seq_begin, (slot_ids < seq_ends[-1]).astype(jnp.float32))


def delayed(values, steps_back):
    if steps_back == 0:
        return values
    return jnp.pad(values[:, :-steps_back], ((0, 0), (steps_back, 0), (0, 0)))


def advanced(values, steps_ahead):
    if steps_ahead == 0:
        return values
    return jnp.pad(values[:, steps_ahead:], ((0, 0), (0, steps_ahead), (0, 0)))


def swapped(values, axis, bit):
    count = lax.axis_size(axis)
    return lax.ppermute(values, axis, [(i, i ^ bit) for i in range(count)])


def tensor_gather(values, axis):
    if lax.axis_size("tensor") != 2:
        return lax.all_gather(values, "tensor", axis=axis, tiled=True)
    other = swapped(values, "tensor", 1)
    mine_first = lax.axis_index("tensor") == 0
    low = jnp.where(mine_first, values, other)
    high = jnp.where(mine_first, other, values)
    return jnp.concatenate([low, high], axis=axis)


def tensor_sum(values):
    if lax.axis_size("tensor") != 2:
        return lax.psum(values, "tensor")
    return values + swapped(values, "tensor", 1)


def tensor_scatter_matmul(pairs, rows, micro):
    def product(picked):
        total = None
        for left, right, dims in pairs:
            part = left.reshape(micro, -1, left.shape[-1])
            if picked is not None:
                part = lax.dynamic_slice_in_dim(part, picked * rows, rows, 1)
            part = lax.dot_general(part.reshape(-1, part.shape[-1]), right, dims, preferred_element_type=f32)
            total = part if total is None else total + part
        return total.reshape(micro, -1, total.shape[-1])

    if lax.axis_size("tensor") != 2:
        return lax.psum_scatter(
            product(None).astype(bf16), "tensor", scatter_dimension=1, tiled=True
        ).astype(f32)
    here = lax.axis_index("tensor")
    away = swapped(product(1 - here).astype(bf16), "tensor", 1)
    return product(here) + away.astype(f32)


def moved(values, offset):
    count = lax.axis_size("dp")
    return lax.ppermute(values, "dp", [((i + 4 * offset) % count, i) for i in range(count)])


def reduce_scatter(values):
    count = lax.axis_size("dp")
    outer = count // 4
    kind = values.dtype
    here = lax.axis_index("dp")
    parts = values.reshape((outer, 2, 2, values.shape[0] // count) + values.shape[1:])
    core = here % 2
    cross = (here // 2) % 2
    place = here // 4
    kept = lax.dynamic_index_in_dim(parts, core, 2, False)
    sent = lax.dynamic_index_in_dim(parts, 1 - core, 2, False)
    parts = (kept.astype(f32) + swapped(sent, "dp", 1).astype(f32)).astype(kind)
    kept = lax.dynamic_index_in_dim(parts, cross, 1, False)
    sent = lax.dynamic_index_in_dim(parts, 1 - cross, 1, False)
    parts = (kept.astype(f32) + swapped(sent, "dp", 2).astype(f32)).astype(kind)
    total = lax.dynamic_index_in_dim(parts, place, 0, False).astype(f32)
    for offset in range(1, outer):
        sent = lax.dynamic_index_in_dim(parts, (place + outer - offset) % outer, 0, False)
        total = total + moved(sent, offset).astype(f32)
    return total


def scan_kernel(
    states,
    pre_ref,
    act_ref,
    gate_ref,
    dgated_ref,
    mask_ref,
    in_ref,
    out_ref,
    in_block_ref,
    out_block_ref,
    skip_ref,
    decay_ref,
    gated_ref,
    dgate_ref,
    dpre_ref,
    dact_ref,
    small_ref,
    decay_grad_ref,
    din_ref,
    dout_ref,
    step_s,
    drive_s,
    dscan_s,
    scanned_s,
    state_s,
    adjoint_s,
    rate_s,
    decay_s,
):
    tok, width = pre_ref.shape
    tiles = width // 128
    rows = chunk * states
    count = tok // chunk
    first = pl.program_id(1) == 0
    decay = -jnp.exp(decay_ref[...])
    decay_two = decay * log2e
    skip = skip_ref[0:1, :]
    row_ids = lax.broadcasted_iota(jnp.int32, (chunk, rows), 0)
    col_ids = lax.broadcasted_iota(jnp.int32, (chunk, rows), 1)
    ones_block = (lax.div(col_ids, states) == row_ids).astype(bf16)

    def spread(ref, at):
        one = ref[pl.ds(at, states), :]
        return jnp.concatenate([one] * tiles, axis=1) if tiles > 1 else one

    def softplus(v):
        return jnp.maximum(v, 0.0) + jnp.log1p(jnp.exp(-jnp.abs(v)))

    def forward(step, state):
        base = pl.multiple_of(step * chunk, chunk)
        cut = pl.ds(base, chunk)
        step_size = softplus(pre_ref[cut, :])
        keep = mask_ref[cut, 0:1]
        live = mask_ref[cut, 1:2]
        gate = gate_ref[cut, :]
        drive = step_size * act_ref[cut, :].astype(f32)
        dscan = dgated_ref[cut, :] * live * gate * jax.nn.sigmoid(gate)
        step_s[cut, :] = step_size + far * (1.0 - keep)
        drive_s[cut, :] = drive
        dscan_s[cut, :] = dscan
        for i in range(chunk):
            row = pl.ds(base + i, 1)
            at = pl.multiple_of((base + i) * states, states)
            factor = jnp.exp2(step_s[row, :] * decay_two)
            state = factor * state + drive_s[row, :] * spread(in_ref, at)
            state_s[pl.ds(at, states), :] = state
        start = pl.multiple_of(base * states, rows)
        low = state_s[pl.ds(start, rows), :].astype(bf16)
        scanned_s[cut, :] = jnp.dot(out_block_ref[cut, :], low, preferred_element_type=f32)
        part = lax.dot_general(dscan.astype(bf16), low, last_dims, preferred_element_type=f32)
        dout_ref[cut, :] = jnp.where(first, part, dout_ref[cut, :] + part)
        return state

    zero = jnp.zeros((states, width), f32)
    lax.fori_loop(0, count, forward, zero)
    decay_s[...] = zero

    def backward(back, carry):
        handed, skip_acc, bias_acc = carry
        step = count - 1 - back
        base = pl.multiple_of(step * chunk, chunk)
        cut = pl.ds(base, chunk)
        acc = decay_s[...]
        for i in reversed(range(chunk)):
            row = pl.ds(base + i, 1)
            at = pl.multiple_of((base + i) * states, states)
            step_row = step_s[row, :]
            adjoint = dscan_s[row, :] * spread(out_ref, at) + handed
            adjoint_s[pl.ds(i * states, states), :] = adjoint.astype(bf16)
            handed = jnp.exp2(step_row * decay_two) * adjoint
            if i == 0:
                before = pl.multiple_of(jnp.maximum(at - states, 0), states)
            else:
                before = pl.multiple_of((base + (i - 1)) * states, states)
            rate = handed * state_s[pl.ds(before, states), :] * decay
            rate_s[pl.ds(i * states, states), :] = rate.astype(bf16)
            acc = acc + rate * step_row
        decay_s[...] = acc
        low = adjoint_s[...]
        in_sum = jnp.dot(in_block_ref[cut, :], low, preferred_element_type=f32)
        rate_sum = jnp.dot(ones_block, rate_s[...], preferred_element_type=f32)
        part = lax.dot_general(drive_s[cut, :].astype(bf16), low, last_dims, preferred_element_type=f32)
        din_ref[cut, :] = jnp.where(first, part, din_ref[cut, :] + part)
        pre = pre_ref[cut, :]
        live = mask_ref[cut, 1:2]
        gate = gate_ref[cut, :]
        sig = jax.nn.sigmoid(gate)
        act = act_ref[cut, :].astype(f32)
        dscan = dscan_s[cut, :]
        dpre = ((rate_sum + in_sum * act) * jax.nn.sigmoid(pre)).astype(bf16)
        dpre_ref[cut, :] = dpre
        dact_ref[cut, :] = dscan * skip + in_sum * softplus(pre)
        branch = (scanned_s[cut, :] + skip * act) * live
        gated_ref[cut, :] = (branch * gate * sig).astype(bf16)
        dgate_ref[cut, :] = (dgated_ref[cut, :] * branch * sig * (1.0 + gate * (1.0 - sig))).astype(bf16)
        skip_acc = skip_acc + jnp.sum((dscan * act).reshape(chunk // 8, 8, width), axis=0)
        bias_acc = bias_acc + jnp.sum(dpre.astype(f32).reshape(chunk // 8, 8, width), axis=0)
        return handed, skip_acc, bias_acc

    eight = jnp.zeros((8, width), f32)
    _, skip_acc, bias_acc = lax.fori_loop(0, count, backward, (zero, eight, eight))
    decay_grad_ref[...] = decay_s[...]
    small_ref[0:8, :] = skip_acc
    small_ref[8:16, :] = bias_acc


def scan_both_ways(pre, act, gate, dgated, mask, in_cols, out_cols, skip, decay_log):
    micro, tok, chans = pre.shape
    states = decay_log.shape[0]
    rows = chunk * states
    width = min(512, chans)

    def lanes(cols):
        return jnp.broadcast_to(cols[..., None], cols.shape + (128,)).reshape(micro, tok * states, 128)

    same = jnp.arange(tok)[:, None] % chunk == jnp.arange(rows)[None, :] // states

    def blocked(cols):
        return jnp.where(same[None], jnp.tile(cols, (1, 1, chunk)), 0.0).astype(bf16)

    def whole(r, c):
        return pl.BlockSpec((None, r, c), lambda m, j: (m, 0, 0))

    def part(r):
        return pl.BlockSpec((None, r, width), lambda m, j: (m, 0, j))

    def param(r):
        return pl.BlockSpec((r, width), lambda m, j: (0, j))

    def shaped(r, c, kind):
        return jax.ShapeDtypeStruct((micro, r, c), kind)

    elements = micro * tok * chans * states
    gated, dgate, dpre, dact, small, decay_grad, din, dout = pl.pallas_call(
        functools.partial(scan_kernel, states),
        grid=(micro, chans // width),
        in_specs=[part(tok)] * 4
        + [whole(tok, 2)]
        + [whole(tok * states, 128)] * 2
        + [whole(tok, rows)] * 2
        + [param(1), param(states)],
        out_specs=[part(tok)] * 4 + [part(16), part(states), whole(tok, rows), whole(tok, rows)],
        out_shape=[shaped(tok, chans, bf16)] * 3
        + [shaped(tok, chans, f32), shaped(16, chans, f32), shaped(states, chans, f32)]
        + [shaped(tok, rows, f32)] * 2,
        scratch_shapes=[pltpu.VMEM((tok, width), f32)] * 4
        + [pltpu.VMEM((tok * states, width), f32)]
        + [pltpu.VMEM((rows, width), bf16)] * 2
        + [pltpu.VMEM((states, width), f32)],
        compiler_params=pltpu.CompilerParams(
            dimension_semantics=("arbitrary", "arbitrary"), vmem_limit_bytes=56 * 2**20
        ),
        cost_estimate=pl.CostEstimate(
            flops=30 * elements, bytes_accessed=24 * micro * tok * chans, transcendentals=2 * elements
        ),
    )(
        pre,
        act,
        gate,
        dgated,
        mask,
        lanes(in_cols),
        lanes(out_cols),
        blocked(in_cols),
        blocked(out_cols),
        skip[None],
        decay_log,
    )
    picks = (jnp.arange(rows)[:, None] % states == jnp.arange(states)[None, :]).astype(f32)

    def unblocked(full):
        return jnp.dot(jnp.where(same[None], full, 0.0), picks, precision=highest)

    skip_grad = jnp.sum(small[:, :8], axis=(0, 1))
    bias_grad = jnp.sum(small[:, 8:], axis=(0, 1))
    return gated, dgate, dpre, dact, skip_grad, bias_grad, jnp.sum(decay_grad, axis=0), unblocked(din), unblocked(dout)


def on_device(
    hidden,
    cotangent,
    lengths,
    order,
    norm_gain,
    input_weight,
    conv_weight,
    conv_bias,
    select_weight,
    step_weight,
    step_bias,
    decay_log,
    skip_gain,
    output_weight,
):
    micro, shard_rows, model_dim = hidden.shape
    count = lax.axis_size("dp")
    group_tok = shard_rows * lax.axis_size("tensor")
    tokens = micro * group_tok
    channels = input_weight.shape[2]
    taps = conv_weight.shape[0]
    states = decay_log.shape[0]
    own = conv_bias.shape[0]
    own_dim = norm_gain.shape[0]

    pieces = [norm_gain, conv_weight, conv_bias, step_bias, decay_log, skip_gain]
    packed = lax.all_gather(jnp.concatenate([v.reshape(-1) for v in pieces]), "dp", axis=0)
    full = []
    at = 0
    for v in pieces:
        part = packed[:, at : at + v.size]
        at += v.size
        if v.ndim == 2:
            part = part.reshape(count, v.shape[0], v.shape[1]).transpose(1, 0, 2).reshape(v.shape[0], -1)
        else:
            part = part.reshape(-1)
        full.append(part)
    gain_full, conv_w, conv_b, step_b, decay_lg, skip_g = full
    w_inner = lax.all_gather(input_weight[:, 0], "dp", axis=0, tiled=True)
    w_sel = lax.all_gather(select_weight, "dp", axis=0, tiled=True)
    w_step = lax.all_gather(step_weight, "dp", axis=0, tiled=True)
    w_gate = lax.all_gather(input_weight[:, 1], "dp", axis=0, tiled=True)
    w_out = lax.all_gather(output_weight.T, "dp", axis=0, tiled=True)
    rank_dim = w_step.shape[0]

    inverse_rms = lax.rsqrt(jnp.mean(hidden * hidden, axis=-1, keepdims=True) + epsilon)
    normal_rows = hidden * inverse_rms
    normed = tensor_gather((normal_rows * gain_full).astype(bf16), 1).reshape(tokens, model_dim)
    cot_full = tensor_gather(cotangent, 1).reshape(tokens, model_dim)

    position, live_mask = jax.vmap(lambda a, b: positions(a, b, group_tok))(lengths[:, 0], order[:, 0])
    mask = jnp.stack([(position > 0).astype(f32), live_mask], axis=2)

    inner = jnp.dot(normed, w_inner, preferred_element_type=f32).reshape(micro, group_tok, channels)
    tap_masks = [(position >= taps - 1 - t).astype(f32)[:, :, None] for t in range(taps)]
    convolved = jnp.zeros_like(inner) + conv_b
    for t in range(taps):
        convolved = convolved + conv_w[t] * delayed(inner, taps - 1 - t) * tap_masks[t]
    act_low = jax.nn.silu(convolved).astype(bf16)
    act_rows = act_low.reshape(tokens, channels)
    selected = tensor_sum(jnp.dot(act_rows, w_sel, preferred_element_type=f32))
    rank_low = selected[:, :rank_dim].astype(bf16)
    cols = selected[:, rank_dim:].reshape(micro, group_tok, 2 * states)
    pre_step = jnp.dot(rank_low, w_step, preferred_element_type=f32) + step_b
    gate = jnp.dot(normed, w_gate, preferred_element_type=f32)
    dgated = jnp.dot(cot_full, w_out, preferred_element_type=f32)

    def grouped(v):
        return v.reshape(micro, group_tok, channels)

    gated, dgate, dpre, dact, skip_grad, step_bias_grad, decay_grad, din, dout = scan_both_ways(
        grouped(pre_step),
        act_low,
        grouped(gate),
        grouped(dgated),
        mask,
        cols[..., :states],
        cols[..., states:],
        skip_g,
        decay_lg,
    )
    gated = gated.reshape(tokens, channels)
    dgate = dgate.reshape(tokens, channels)
    dpre = dpre.reshape(tokens, channels)

    out_grad = lax.dot_general(cot_full, gated, first_dims, preferred_element_type=f32).astype(bf16)
    out_grad = reduce_scatter(out_grad)
    gate_grad = lax.dot_general(normed, dgate, first_dims, preferred_element_type=f32).astype(bf16)
    gate_grad = reduce_scatter(gate_grad)
    layer_rows = hidden + tensor_scatter_matmul([(gated, w_out, last_dims)], shard_rows, micro)

    rank_grad = lax.dot_general(dpre, w_step, last_dims, preferred_element_type=f32)
    select_terms = jnp.concatenate(
        [rank_grad, din.reshape(tokens, states), dout.reshape(tokens, states)], axis=1
    )
    select_low = tensor_sum(select_terms).astype(bf16)
    step_weight_grad = lax.dot_general(rank_low, dpre, first_dims, preferred_element_type=f32)
    select_grad = lax.dot_general(select_low, act_rows, first_dims, preferred_element_type=f32)
    dact = dact + grouped(lax.dot_general(select_low, w_sel, last_dims, preferred_element_type=f32))
    conv_sig = jax.nn.sigmoid(convolved)
    dconv = dact * conv_sig * (1.0 + convolved * (1.0 - conv_sig))
    conv_bias_grad = jnp.sum(dconv, axis=(0, 1))
    conv_rows = []
    dinner = jnp.zeros_like(inner)
    for t in range(taps):
        masked = dconv * tap_masks[t]
        conv_rows.append(jnp.sum(masked * delayed(inner, taps - 1 - t), axis=(0, 1)))
        dinner = dinner + advanced(masked, taps - 1 - t) * conv_w[t]
    dinner = dinner.astype(bf16).reshape(tokens, channels)
    inner_grad = lax.dot_general(normed, dinner, first_dims, preferred_element_type=f32).astype(bf16)
    inner_grad = reduce_scatter(inner_grad)

    dnormed = tensor_scatter_matmul(
        [(dinner, w_inner, last_dims), (dgate, w_gate, last_dims)], shard_rows, micro
    )
    gain_part = jnp.sum(dnormed * normal_rows, axis=(0, 1))
    dnormal = dnormed * gain_full
    grad_rows = cotangent.astype(f32) + inverse_rms * (
        dnormal - normal_rows * jnp.mean(dnormal * normal_rows, axis=-1, keepdims=True)
    )

    vectors = jnp.concatenate(
        [jnp.stack(conv_rows + [conv_bias_grad, step_bias_grad, skip_grad]), decay_grad], axis=0
    )
    vectors = vectors.reshape(-1, count, own).transpose(1, 0, 2)
    vectors = reduce_scatter(vectors)[0]
    select_part = select_grad.astype(bf16).reshape(-1, count, own).transpose(1, 0, 2).reshape(count, -1)
    step_part = step_weight_grad.astype(bf16).reshape(count, -1)
    mixed = reduce_scatter(jnp.concatenate([select_part, step_part], axis=1))[0]
    gain_total = tensor_sum(reduce_scatter(gain_part.reshape(count, own_dim))[0])
    split = select_part.shape[1]
    return (
        layer_rows,
        grad_rows,
        gain_total,
        jnp.stack([inner_grad, gate_grad], axis=1),
        vectors[:taps],
        vectors[taps],
        mixed[:split].reshape(-1, own).T,
        mixed[split:].reshape(-1, channels),
        vectors[taps + 1],
        vectors[taps + 3 :],
        vectors[taps + 2],
        out_grad.T,
    )


def solution(mesh):
    in_specs = (
        P(None, ("dp", "tensor"), None),
        P(None, ("dp", "tensor"), None),
        P(None, "dp", None),
        P(None, "dp", None),
        P("dp"),
        P("dp", None, "tensor"),
        P(None, ("tensor", "dp")),
        P(("tensor", "dp")),
        P(("tensor", "dp"), None),
        P("dp", "tensor"),
        P(("tensor", "dp")),
        P(None, ("tensor", "dp")),
        P(("tensor", "dp")),
        P("tensor", "dp"),
    )
    out_specs = (
        P(None, ("dp", "tensor"), None),
        P(None, ("dp", "tensor"), None),
        P("dp"),
        P("dp", None, "tensor"),
        P(None, ("tensor", "dp")),
        P(("tensor", "dp")),
        P(("tensor", "dp"), None),
        P("dp", "tensor"),
        P(("tensor", "dp")),
        P(None, ("tensor", "dp")),
        P(("tensor", "dp")),
        P("tensor", "dp"),
    )
    return jax.shard_map(
        on_device, mesh=mesh, in_specs=in_specs, out_specs=out_specs, check_vma=False
    )
```

time: 3210 us -> 797 us (0.25)
  other arithmetic: 1030 us -> 63.6 us
  waiting for transfers between devices: 953 us -> 345 us
  matrix products: 448 us -> 89.6 us
  local copies, waits for them, and re-layouts: 421 us -> 67.1 us
  blocking collectives: 276 us -> 68.5 us
  Pallas kernels: 0 us -> 105 us
  loops' own time: 41.2 us -> 0 us
  starting transfers between devices: 1.48 us -> 35.7 us
    while x516 -> x0, other arithmetic: 565 us -> none
    unnamed x19 -> x3, waiting for transfers between devices: 460 us -> 0.05 us
    reduce_scatter x8 -> x0, waiting for transfers between devices: 358 us -> none  [the longest x1 182 us: on_device(): lax.psum_scatter(pending[8], 'dp', scatter_dimension=1, tiled=True)]
    dot_general x38 -> x19, matrix products: 441 us -> 86.9 us  [the longest x6 31.5 us: product(): lax.dot_general(part.reshape(-1, part.shape[-1]), right, dims, preferred_...]
    ppermute x0 -> x37, waiting for transfers between devices: none -> 229 us  [the longest x19 143 us: swapped(): return lax.ppermute(values, axis, [(i, i ^ bit) for i in range(count)])]
    mul x88 -> x0, other arithmetic: 195 us -> none  [the longest x8 68.6 us: decay_factor(): jnp.exp(step_blk[:, None, :] * decay_rate[None]) * keep_blk[:, None, None]]
    dynamic_update_slice x148 -> x0, local copies, waits for them, and re-layouts: 168 us -> none  [the longest x128 138 us: run_block(): _, states = lax.scan(advance, start_state, (factor, driven), unroll=8)]
    concatenate x135 -> x1, other arithmetic: 158 us -> 0.79 us  [on_device(): jnp.concatenate([rank_grad, din.reshape(tokens, states), dout.reshape(tok...]
  transfers between devices with their start and end apart: 17 -> 40, of which waited for: 11 -> 15; matrix products, arithmetic and copies ran while one was open for 7% -> 23% of each run, Pallas kernels for 0% -> 0%
where the time goes in v1:
time: 797 us; the launch traced here: 790 us
  waiting for transfers between devices  345 us (43%)
  Pallas kernels  105 us (13%)
  matrix products  89.6 us (11%)
  blocking collectives  68.5 us (9%)
  local copies, waits for them, and re-layouts  67.1 us (8%)
  other arithmetic  63.6 us (8%)
  starting transfers between devices  35.7 us (4%)
  between operations  15.3 us (2%)
    ppermute x19, waiting for transfers between devices, swapped(): return lax.ppermute(values, axis, [(i, i ^ bit) for i in range(count)])  143 us
    pallas_call x1, Pallas kernels, scan_both_ways(): pl.pallas_call(functools.partial(scan_kernel, states), grid=(micro, chans...  105 us
    ppermute x18, waiting for transfers between devices, moved(): lax.ppermute(values, 'dp', [((i + 4 * offset) % count, i) for i in range(...  86.4 us
    all_gather x1, waiting for transfers between devices, on_device(): w_out = lax.all_gather(output_weight.T, 'dp', axis=0, tiled=True)  65.3 us
    all_gather x1, waiting for transfers between devices, on_device(): w_gate = lax.all_gather(input_weight[:, 1], 'dp', axis=0, tiled=True)  50.7 us
    dot_general x6, matrix products, product(): lax.dot_general(part.reshape(-1, part.shape[-1]), right, dims, preferred_...  31.5 us
    all_gather x1, blocking collectives, on_device(): lax.all_gather(jnp.concatenate([v.reshape(-1) for v in pieces]), 'dp', ax...  24.3 us
    all_gather x1, blocking collectives, on_device(): w_sel = lax.all_gather(select_weight, 'dp', axis=0, tiled=True)  23.3 us
  transfers between devices with their start and end apart: 40, of which 15 were waited for; matrix products, arithmetic and copies ran while one was open for 23% of the time, Pallas kernels for 0%

profile of v1, /device:TPU:0, one launch (start us, length us, event | category | flops | bytes accessed | tf_op | source)
XLA Modules:
  0.0 789.8 jit_solution(3600354776223113894)
XLA Ops:
  15.2 24.3 %all-gather = f32[49152]{0:T(1024)S(1)} all-gather(f32[3072]{0:T(1024)S(1)} %constant_dynamic-update-slice_fusion.11), channel_id=2, replica_groups=mesh['dp'=16,'tensor'=2] {'dp'}, dimensions={0}, use_global_device_ids=true | all-gather | bytes 208896 | tf_op jit(solution)/shard_map/all_gather | solution.py:338
  46.6 20.9 %all_gather.25 = bf16[128,2048]{1,0:T(8,128)(2,1)S(1)} all-gather(bf16[8,2048]{1,0:T(8,128)(2,1)S(1)} %copy-done.25), channel_id=1, replica_groups=mesh['dp'=16,'tensor'=2] {'dp'}, dimensions={0}, use_global_device_ids=true | all-gather | bytes 557056 | tf_op jit(solution)/shard_map/all_gather | solution.py:352
  67.5 23.3 %all_gather.24 = bf16[2048,160]{0,1:T(8,128)(2,1)S(1)} all-gather(bf16[128,160]{0,1:T(8,128)(2,1)S(1)} %copy-done.24), channel_id=1, replica_groups=mesh['dp'=16,'tensor'=2] {'dp'}, dimensions={0}, use_global_device_ids=true | all-gather | bytes 696320 | tf_op jit(solution)/shard_map/all_gather | solution.py:351
  97.0 7.5 fusion.15
  104.5 16.3 %multiply_convert_fusion = (bf16[2,256,2048]{2,1,0:T(8,128)(2,1)S(1)}, f32[2,256,2048]{2,1,0:T(8,128)}) fusion(f32[2,256]{1,0:T(2,128)S(1)} %get-tuple-element.187, f32[2,256,2048]{2,1,0:T(8,128)S(1)} %fusion.15, f32[2048]{0:T(1024)S(1)} %bitcast.336, f32[2,256]{1,0:T(2,128)S(1)} %get-tuple-element.186, f32[2,255,2048]{2,1,0:T(8,128)S(1)} %bitcast.297, ...), kind=kLoop, calls=%fused_computation.43 | loop fusion | flops 17825792 | bytes 23019520 | tf_op jit(solution)/shard_map/convert_element_type | solution.py:370
  123.7 50.7 %all-gather.11.cloned.1.call-done = bf16[2048,1,2048]{2,0,1:T(8,128)(2,1)} async-done(((bf16[128,1,2048]{2,0,1:T(8,128)(2,1)}), bf16[2048,1,2048]{2,0,1:T(8,128)(2,1)}) %all-gather.11.cloned.1.call-update) | async-done | bytes 8388624 | tf_op jit(solution)/shard_map/all_gather | solution.py:353
  174.4 10.6 %fusion.9.gate_ref = f32[2,256,2048]{2,1,0:T(8,128)} fusion(bf16[2048,1,2048]{2,0,1:T(8,128)(2,1)} %all-gather.11.cloned.1.call-done, bf16[2,128,2048]{2,1,0:T(8,128)(2,1)} %get-tuple-element.153, bf16[2,128,2048]{2,1,0:T(8,128)(2,1)} %get-tuple-element.152), kind=kOutput, calls=%fused_computation.15 | convolution fusion | flops 4299161600 | bytes 14680064 | tf_op jit(solution)/shard_map/dot_general | solution.py:376
  185.0 65.3 %all-gather.7.cloned.1.call-done = bf16[2048,2048]{1,0:T(8,128)(2,1)} async-done(((bf16[128,2048]{1,0:T(8,128)(2,1)}), bf16[2048,2048]{1,0:T(8,128)(2,1)}) %all-gather.7.cloned.1.call-update) | async-done | bytes 8388624 | tf_op jit(solution)/shard_map/all_gather | solution.py:354
  250.3 10.5 %fusion.7.dgated_ref = f32[2,256,2048]{2,1,0:T(8,128)} fusion(bf16[2048,2048]{1,0:T(8,128)(2,1)} %all-gather.7.cloned.1.call-done, bf16[2,128,2048]{2,1,0:T(8,128)(2,1)} %get-tuple-element.151, bf16[2,128,2048]{2,1,0:T(8,128)(2,1)} %get-tuple-element.150), kind=kOutput, calls=%fused_computation.13 | convolution fusion | flops 4299161600 | bytes 14680064 | tf_op jit(solution)/shard_map/dot_general | solution.py:377
  271.6 104.9 %shard_map.229 = (bf16[2,256,2048]{2,1,0:T(8,128)(2,1)}, bf16[2,256,2048]{2,1,0:T(8,128)(2,1)}, bf16[2,256,2048]{2,1,0:T(8,128)(2,1)}, f32[2,256,2048]{2,1,0:T(8...) custom-call(f32[2,256,2048]{2,1,0:T(8,128)} %bitcast.311, ...), custom_call_target="tpu_custom_call" | custom-call | flops 503316480 | bytes 25165824 | tf_op jit(solution)/shard_map/pallas_call | solution.py:266
  396.8 6.7 copy.241
  407.1 6.8 bitcast_convert_fusion.1
  421.1 7.0 fusion.33
  448.6 7.0 bitcast_convert_fusion.2
  474.6 6.8 constant_dynamic-slice_fusion.11
  491.3 18.5 %collective-permute-done.3 = bf16[2,128,2048]{2,1,0:T(8,128)(2,1)S(1)} collective-permute-done((bf16[2,128,2048]{2,1,0:T(8,128)(2,1)S(1)}, bf16[2,128,2048]{2,1,0:T(8,128)(2,1)S(1)}, u32[]{:S(2)}, u32[]{:S(2)}) %collective-permute-start.3) | collective-permute-done | bytes 1048608 | tf_op jit(solution)/shard_map/ppermute | solution.py:46
  509.8 7.1 add_add_fusion
  517.8 12.6 %collective-permute-done.5 = bf16[2,128,2048]{2,1,0:T(8,128)(2,1)S(1)} collective-permute-done((bf16[2,128,2048]{2,1,0:T(8,128)(2,1)S(1)}, bf16[2,128,2048]{2,1,0:T(8,128)(2,1)S(1)}, u32[]{:S(2)}, u32[]{:S(2)}) %collective-permute-start.5) | collective-permute-done | bytes 1048608 | tf_op jit(solution)/shard_map/ppermute | solution.py:46
  538.6 9.8 %collective-permute-done.30 = bf16[1,36864]{1,0:T(2,128)(2,1)S(1)} collective-permute-done((bf16[1,36864]{1,0:T(2,128)(2,1)S(1)}, bf16[1,36864]{1,0:T(2,128)(2,1)S(1)}, u32[]{:S(2)}, u32[]{:S(2)}) %collective-permute-start.30) | collective-permute-done | bytes 73760 | tf_op jit(solution)/shard_map/ppermute | solution.py:87
  586.8 30.8 %collective-permute-done.33 = bf16[4,128,2048]{1,2,0:T(8,128)(2,1)} collective-permute-done((bf16[4,128,2048]{1,2,0:T(8,128)(2,1)}, bf16[4,128,2048]{1,2,0:T(8,128)(2,1)}, u32[]{:S(2)}, u32[]{:S(2)}) %collective-permute-start.33) | collective-permute-done | bytes 2097184 | tf_op jit(solution)/shard_map/ppermute | solution.py:46
  621.9 40.5 %collective-permute-done.18 = bf16[4,128,2048]{2,1,0:T(8,128)(2,1)S(1)} collective-permute-done((bf16[4,128,2048]{2,1,0:T(8,128)(2,1)}, bf16[4,128,2048]{2,1,0:T(8,128)(2,1)S(1)}, u32[]{:S(2)}, u32[]{:S(2)}) %collective-permute-start.18) | collective-permute-done | bytes 2097184 | tf_op jit(solution)/shard_map/ppermute | solution.py:46
  664.5 38.3 %collective-permute-done.13 = bf16[4,128,2048]{2,1,0:T(8,128)(2,1)S(1)} collective-permute-done((bf16[4,128,2048]{2,1,0:T(8,128)(2,1)S(1)}, bf16[4,128,2048]{2,1,0:T(8,128)(2,1)S(1)}, u32[]{:S(2)}, u32[]{:S(2)}) %collective-permute-start.13) | collective-permute-done | bytes 2097184 | tf_op jit(solution)/shard_map/ppermute | solution.py:46
  710.4 29.1 %collective-permute-done.20 = bf16[128,2048]{1,0:T(8,128)(2,1)S(1)} collective-permute-done((bf16[128,2048]{1,0:T(8,128)(2,1)S(1)}, bf16[128,2048]{1,0:T(8,128)(2,1)S(1)}, u32[]{:S(2)}, u32[]{:S(2)}) %collective-permute-start.20) | collective-permute-done | bytes 524320 | tf_op jit(solution)/shard_map/ppermute | solution.py:87
  739.8 39.7 %collective-permute-done.15 = bf16[128,2048]{1,0:T(8,128)(2,1)S(1)} collective-permute-done((bf16[128,2048]{1,0:T(8,128)(2,1)S(1)}, bf16[128,2048]{1,0:T(8,128)(2,1)S(1)}, u32[]{:S(2)}, u32[]{:S(2)}) %collective-permute-start.15) | collective-permute-done | bytes 524320 | tf_op jit(solution)/shard_map/ppermute | solution.py:87
  (311 shorter events, 179.6 us)
Async XLA Ops:
  7.2 89.7 %all-gather.9.cloned.1.call-start = ((), (), s32[]{:S(2)}) async-start(), calls=%async_computation.1 | async-start | bytes 8912896 | tf_op jit(solution)/shard_map/all_gather | solution.py:350
  11.7 162.7 %all-gather.11.cloned.1.call-start = ((), (), s32[]{:S(2)}) async-start(), calls=%async_computation.2 | async-start | bytes 8912896 | tf_op jit(solution)/shard_map/all_gather | solution.py:353
  12.9 237.4 %all-gather.7.cloned.1.call-start = ((), (), s32[]{:S(2)}) async-start(), calls=%async_computation | async-start | bytes 8912896 | tf_op jit(solution)/shard_map/all_gather | solution.py:354
  41.6 52.2 %collective-permute-start = (bf16[2,128,2048]{2,1,0:T(8,128)(2,1)}, bf16[2,128,2048]{2,1,0:T(8,128)(2,1)}, u32[]{:S(2)}, u32[]{:S(2)}) collective-permute-start(bf16[2,128,2048]{2,1,0:T(8,128)(2,1)} %multiply_convert_fusion.1), channel_id=1, source_target_pairs={{0,1},{1,0},{2,3},{3,2},{4,5},{5,4},{6,7},{7,6},{8,9},{9,8},{10,11... | collective-permute-start | bytes 3145736 | tf_op jit(solution)/shard_map/ppermute | solution.py:46
  43.0 47.8 %collective-permute-start.2 = (bf16[2,128,2048]{2,1,0:T(8,128)(2,1)}, bf16[2,128,2048]{2,1,0:T(8,128)(2,1)}, u32[]{:S(2)}, u32[]{:S(2)}) collective-permute-start(bf16[2,128,2048]{2,1,0:T(8,128)(2,1)} %param.15), channel_id=1, source_target_pairs={{0,1},{1,0},{2,3},{3,2},{4,5},{5,4},{6,7},{7,6},{8,9},{9,8},{10,11... | collective-permute-start | bytes 3145736 | tf_op jit(solution)/shard_map/ppermute | solution.py:46
  122.4 138.4 %collective-permute-start.1 = (f32[512,160]{0,1:T(8,128)}, f32[512,160]{0,1:T(8,128)}, u32[]{:S(2)}, u32[]{:S(2)}) collective-permute-start(f32[512,160]{0,1:T(8,128)} %fusion.99), channel_id=1, source_target_pairs={{0,1},{1,0},{2,3},{3,2},{4,5},{5,4},{6,7},{7,6},{8,9},{9,8},{10,11... | collective-permute-start | bytes 983048 | tf_op jit(solution)/shard_map/ppermute | solution.py:46
  396.5 166.1 %collective-permute-start.32 = (bf16[4,2,128,2048]{2,3,0,1:T(8,128)(2,1)}, bf16[4,2,128,2048]{2,3,0,1:T(8,128)(2,1)}, u32[]{:S(2)}, u32[]{:S(2)}) collective-permute-start(bf16[4,2,128,2048]{2,3,0,1:T(8,128)(2,1)} %bitcast.312), channel_id=1, source_target_pairs={{0,2},{2,0},{4,6},{6,4},{8,10},{10,8},{12,14},{14,12},{16,18},{18,... | collective-permute-start | bytes 12582920 | tf_op jit(solution)/shard_map/ppermute | solution.py:46
  405.1 30.5 %collective-permute-start.4 = (f32[512,160]{0,1:T(8,128)}, f32[512,160]{0,1:T(8,128)}, u32[]{:S(2)}, u32[]{:S(2)}) collective-permute-start(f32[512,160]{0,1:T(8,128)} %pad_maximum_fusion.5), channel_id=1, source_target_pairs={{0,1},{1,0},{2,3},{3,2},{4,5},{5,4},{6,7},{7,6},{8,9},{9,8},{10,11... | collective-permute-start | bytes 983048 | tf_op jit(solution)/shard_map/ppermute | solution.py:46
  419.5 150.6 %collective-permute-start.17 = (bf16[4,2,128,2048]{3,2,0,1:T(8,128)(2,1)}, bf16[4,2,128,2048]{3,2,0,1:T(8,128)(2,1)}, u32[]{:S(2)}, u32[]{:S(2)}) collective-permute-start(bf16[4,2,128,2048]{3,2,0,1:T(8,128)(2,1)} %bitcast.288), channel_id=1, source_target_pairs={{0,2},{2,0},{4,6},{6,4},{8,10},{10,8},{12,14},{14,12},{16,18},{18,... | collective-permute-start | bytes 12582920 | tf_op jit(solution)/shard_map/ppermute | solution.py:46
  484.3 46.1 %collective-permute-start.5 = (bf16[2,128,2048]{2,1,0:T(8,128)(2,1)S(1)}, bf16[2,128,2048]{2,1,0:T(8,128)(2,1)S(1)}, u32[]{:S(2)}, u32[]{:S(2)}) collective-permute-start(bf16[2,128,2048]{2,1,0:T(8,128)(2,1)S(1)} %bitcast.352), channel_id=1, source_target_pairs={{0,1},{1,0},{2,3},{3,2},{4,5},{5,4},{6,7},{7,6},{8,9},{9,8},{10,11... | collective-permute-start | bytes 3145736 | tf_op jit(solution)/shard_map/ppermute | solution.py:46
  489.9 27.0 %collective-permute-start.28 = (bf16[4,1,36864]{2,1,0:T(2,128)(2,1)S(1)}, bf16[4,1,36864]{2,1,0:T(2,128)(2,1)S(1)}, u32[]{:S(2)}, u32[]{:S(2)}) collective-permute-start(bf16[4,1,36864]{2,1,0:T(2,128)(2,1)S(1)} %dynamic-slice_bitcast_fusion.4), channel_id=1, source_target_pairs={{0,4},{2,6},{4,0},{6,2},{8,12},{10,14},{12,8},{14,10},{16,20},{18,... | collective-permute-start | bytes 884744 | tf_op jit(solution)/shard_map/ppermute | solution.py:46
  538.6 38.4 %collective-permute-start.12 = (bf16[4,2,128,2048]{3,2,0,1:T(8,128)(2,1)}, bf16[4,2,128,2048]{3,2,0,1:T(8,128)(2,1)}, u32[]{:S(2)}, u32[]{:S(2)}) collective-permute-start(bf16[4,2,128,2048]{3,2,0,1:T(8,128)(2,1)} %bitcast.289), channel_id=1, source_target_pairs={{0,2},{2,0},{4,6},{6,4},{8,10},{10,8},{12,14},{14,12},{16,18},{18,... | collective-permute-start | bytes 12582920 | tf_op jit(solution)/shard_map/ppermute | solution.py:46
  568.7 48.9 %collective-permute-start.33 = (bf16[4,128,2048]{1,2,0:T(8,128)(2,1)}, bf16[4,128,2048]{1,2,0:T(8,128)(2,1)}, u32[]{:S(2)}, u32[]{:S(2)}) collective-permute-start(bf16[4,128,2048]{1,2,0:T(8,128)(2,1)} %dynamic-slice_bitcast_fusion), channel_id=1, source_target_pairs={{0,4},{2,6},{4,0},{6,2},{8,12},{10,14},{12,8},{14,10},{16,20},{18,... | collective-permute-start | bytes 6291464 | tf_op jit(solution)/shard_map/ppermute | solution.py:46
  575.7 86.7 %collective-permute-start.18 = (bf16[4,128,2048]{2,1,0:T(8,128)(2,1)}, bf16[4,128,2048]{2,1,0:T(8,128)(2,1)S(1)}, u32[]{:S(2)}, u32[]{:S(2)}) collective-permute-start(bf16[4,128,2048]{2,1,0:T(8,128)(2,1)} %dynamic-slice_bitcast_fusion.1), channel_id=1, source_target_pairs={{0,4},{2,6},{4,0},{6,2},{8,12},{10,14},{12,8},{14,10},{16,20},{18,... | collective-permute-start | bytes 6291464 | tf_op jit(solution)/shard_map/ppermute | solution.py:46
  581.5 121.3 %collective-permute-start.13 = (bf16[4,128,2048]{2,1,0:T(8,128)(2,1)S(1)}, bf16[4,128,2048]{2,1,0:T(8,128)(2,1)S(1)}, u32[]{:S(2)}, u32[]{:S(2)}) collective-permute-start(bf16[4,128,2048]{2,1,0:T(8,128)(2,1)S(1)} %dynamic-slice_bitcast_fusion.2), channel_id=1, source_target_pairs={{0,4},{2,6},{4,0},{6,2},{8,12},{10,14},{12,8},{14,10},{16,20},{18,... | collective-permute-start | bytes 6291464 | tf_op jit(solution)/shard_map/ppermute | solution.py:46
  619.8 84.3 %collective-permute-start.34 = (bf16[128,2048]{0,1:T(8,128)(2,1)S(1)}, bf16[128,2048]{0,1:T(8,128)(2,1)S(1)}, u32[]{:S(2)}, u32[]{:S(2)}) collective-permute-start(bf16[128,2048]{0,1:T(8,128)(2,1)S(1)} %get-tuple-element.137), channel_id=1, source_target_pairs={{8,0},{10,2},{12,4},{14,6},{16,8},{18,10},{20,12},{22,14},{24,16},... | collective-permute-start | bytes 1572872 | tf_op jit(solution)/shard_map/ppermute | solution.py:87
  620.8 84.9 %collective-permute-start.35 = (bf16[128,2048]{0,1:T(8,128)(2,1)S(1)}, bf16[128,2048]{0,1:T(8,128)(2,1)S(1)}, u32[]{:S(2)}, u32[]{:S(2)}) collective-permute-start(bf16[128,2048]{0,1:T(8,128)(2,1)S(1)} %get-tuple-element.139), channel_id=1, source_target_pairs={{16,0},{18,2},{20,4},{22,6},{24,8},{26,10},{28,12},{30,14},{0,16},... | collective-permute-start | bytes 1572872 | tf_op jit(solution)/shard_map/ppermute | solution.py:87
  620.8 87.3 %collective-permute-start.36 = (bf16[128,2048]{0,1:T(8,128)(2,1)S(1)}, bf16[128,2048]{0,1:T(8,128)(2,1)S(1)}, u32[]{:S(2)}, u32[]{:S(2)}) collective-permute-start(bf16[128,2048]{0,1:T(8,128)(2,1)S(1)} %get-tuple-element.138), channel_id=1, source_target_pairs={{24,0},{26,2},{28,4},{30,6},{0,8},{2,10},{4,12},{6,14},{8,16},{10,... | collective-permute-start | bytes 1572872 | tf_op jit(solution)/shard_map/ppermute | solution.py:87
  663.5 45.5 %collective-permute-start.19 = (bf16[128,2048]{1,0:T(8,128)(2,1)S(1)}, bf16[128,2048]{1,0:T(8,128)(2,1)S(1)}, u32[]{:S(2)}, u32[]{:S(2)}) collective-permute-start(bf16[128,2048]{1,0:T(8,128)(2,1)S(1)} %get-tuple-element.143), channel_id=1, source_target_pairs={{8,0},{10,2},{12,4},{14,6},{16,8},{18,10},{20,12},{22,14},{24,16},... | collective-permute-start | bytes 1572872 | tf_op jit(solution)/shard_map/ppermute | solution.py:87
  702.9 36.7 %collective-permute-start.20 = (bf16[128,2048]{1,0:T(8,128)(2,1)S(1)}, bf16[128,2048]{1,0:T(8,128)(2,1)S(1)}, u32[]{:S(2)}, u32[]{:S(2)}) collective-permute-start(bf16[128,2048]{1,0:T(8,128)(2,1)S(1)} %get-tuple-element.145), channel_id=1, source_target_pairs={{16,0},{18,2},{20,4},{22,6},{24,8},{26,10},{28,12},{30,14},{0,16},... | collective-permute-start | bytes 1572872 | tf_op jit(solution)/shard_map/ppermute | solution.py:87
  704.1 35.4 %collective-permute-start.21 = (bf16[128,2048]{1,0:T(8,128)(2,1)S(1)}, bf16[128,2048]{1,0:T(8,128)(2,1)S(1)}, u32[]{:S(2)}, u32[]{:S(2)}) collective-permute-start(bf16[128,2048]{1,0:T(8,128)(2,1)S(1)} %get-tuple-element.144), channel_id=1, source_target_pairs={{24,0},{26,2},{28,4},{30,6},{0,8},{2,10},{4,12},{6,14},{8,16},{10,... | collective-permute-start | bytes 1572872 | tf_op jit(solution)/shard_map/ppermute | solution.py:87
  705.8 34.1 %collective-permute-start.14 = (bf16[128,2048]{1,0:T(8,128)(2,1)S(1)}, bf16[128,2048]{1,0:T(8,128)(2,1)S(1)}, u32[]{:S(2)}, u32[]{:S(2)}) collective-permute-start(bf16[128,2048]{1,0:T(8,128)(2,1)S(1)} %get-tuple-element.140), channel_id=1, source_target_pairs={{8,0},{10,2},{12,4},{14,6},{16,8},{18,10},{20,12},{22,14},{24,16},... | collective-permute-start | bytes 1572872 | tf_op jit(solution)/shard_map/ppermute | solution.py:87
  708.1 71.4 %collective-permute-start.15 = (bf16[128,2048]{1,0:T(8,128)(2,1)S(1)}, bf16[128,2048]{1,0:T(8,128)(2,1)S(1)}, u32[]{:S(2)}, u32[]{:S(2)}) collective-permute-start(bf16[128,2048]{1,0:T(8,128)(2,1)S(1)} %get-tuple-element.142), channel_id=1, source_target_pairs={{16,0},{18,2},{20,4},{22,6},{24,8},{26,10},{28,12},{30,14},{0,16},... | collective-permute-start | bytes 1572872 | tf_op jit(solution)/shard_map/ppermute | solution.py:87
  709.0 70.6 %collective-permute-start.16 = (bf16[128,2048]{1,0:T(8,128)(2,1)S(1)}, bf16[128,2048]{1,0:T(8,128)(2,1)S(1)}, u32[]{:S(2)}, u32[]{:S(2)}) collective-permute-start(bf16[128,2048]{1,0:T(8,128)(2,1)S(1)} %get-tuple-element.141), channel_id=1, source_target_pairs={{24,0},{26,2},{28,4},{30,6},{0,8},{2,10},{4,12},{6,14},{8,16},{10,... | collective-permute-start | bytes 1572872 | tf_op jit(solution)/shard_map/ppermute | solution.py:87
  (62 other events, 890.4 us)
Sparse Core Ops, SparseCore 0:
  11.8 84.4 all-gather.8
  99.0 75.3 all-gather.10
  177.1 73.1 all-gather.6

commit v2 on v1

v2 whole, which is shorter than its diff:
```python
import functools

import jax
import jax.numpy as jnp
from jax import lax
from jax.experimental import pallas as pl
from jax.experimental.pallas import tpu as pltpu
from jax.sharding import PartitionSpec as P

epsilon = 1e-05
log2e = 1.4426950408889634
far = 1e6
chunk = 16
f32 = jnp.float32
bf16 = jnp.bfloat16
highest = lax.Precision.HIGHEST
small_cost = pl.CostEstimate(flops=1, bytes_accessed=1, transcendentals=0)
last_dims = (((1,), (1,)), ((), ()))
first_dims = (((0,), (0,)), ((), ()))


def positions(length_row, order_row, slot_count):
    number = order_row.shape[0]
    picked = (order_row[:, None] == jnp.arange(number, dtype=jnp.int32)[None, :]).astype(jnp.int32)
    ordered = jnp.sum(picked * length_row[None, :], axis=1)
    seq_ends = jnp.cumsum(ordered)
    starts = jnp.concatenate([jnp.zeros((1,), jnp.int32), seq_ends])
    slot_ids = jnp.arange(slot_count, dtype=jnp.int32)
    seq_begin = jnp.max(jnp.where(starts[None, :] <= slot_ids[:, None], starts[None, :], 0), axis=1)
    return (slot_ids - seq_begin, (slot_ids < seq_ends[-1]).astype(jnp.float32))


def swapped(values, axis, bit):
    count = lax.axis_size(axis)
    return lax.ppermute(values, axis, [(i, i ^ bit) for i in range(count)])


def tensor_gather(values, axis):
    if lax.axis_size("tensor") != 2:
        return lax.all_gather(values, "tensor", axis=axis, tiled=True)
    other = swapped(values, "tensor", 1)
    mine_first = lax.axis_index("tensor") == 0
    low = jnp.where(mine_first, values, other)
    high = jnp.where(mine_first, other, values)
    return jnp.concatenate([low, high], axis=axis)


def tensor_sum(values):
    if lax.axis_size("tensor") != 2:
        return lax.psum(values, "tensor")
    return values + swapped(values, "tensor", 1)


def moved(values, offset):
    count = lax.axis_size("dp")
    return lax.ppermute(values, "dp", [((i + 4 * offset) % count, i) for i in range(count)])


def reduce_scatter(values):
    count = lax.axis_size("dp")
    outer = count // 4
    kind = values.dtype
    here = lax.axis_index("dp")
    parts = values.reshape((outer, 2, 2, values.shape[0] // count) + values.shape[1:])
    core = here % 2
    cross = (here // 2) % 2
    place = here // 4
    kept = lax.dynamic_index_in_dim(parts, core, 2, False)
    sent = lax.dynamic_index_in_dim(parts, 1 - core, 2, False)
    parts = (kept.astype(f32) + swapped(sent, "dp", 1).astype(f32)).astype(kind)
    kept = lax.dynamic_index_in_dim(parts, cross, 1, False)
    sent = lax.dynamic_index_in_dim(parts, 1 - cross, 1, False)
    parts = (kept.astype(f32) + swapped(sent, "dp", 2).astype(f32)).astype(kind)
    total = lax.dynamic_index_in_dim(parts, place, 0, False).astype(f32)
    for offset in range(1, outer):
        sent = lax.dynamic_index_in_dim(parts, (place + outer - offset) % outer, 0, False)
        total = total + moved(sent, offset).astype(f32)
    return total


def scan_kernel(
    states,
    pre_ref,
    act_ref,
    normed_ref,
    cot_ref,
    gate_weight_ref,
    out_weight_ref,
    rank_ref,
    step_weight_ref,
    mask_ref,
    in_ref,
    out_ref,
    in_block_ref,
    out_block_ref,
    skip_ref,
    decay_ref,
    gated_ref,
    dgate_ref,
    dact_ref,
    step_grad_ref,
    sums_ref,
    rank_grad_ref,
    din_ref,
    dout_ref,
    gate_s,
    dgated_s,
    step_s,
    drive_s,
    dscan_s,
    scanned_s,
    dpre_s,
    state_s,
    power_s,
    odd_s,
    even_s,
    odd_rate_s,
    even_rate_s,
    decay_s,
):
    tok, width = pre_ref.shape
    tiles = width // 128
    rows = chunk * states
    count = tok // chunk
    first = pl.program_id(1) == 0
    decay = -jnp.exp(decay_ref[...])
    decay_two = decay * log2e
    skip = skip_ref[0:1, :]
    row_ids = lax.broadcasted_iota(jnp.int32, (chunk, rows), 0)
    col_ids = lax.broadcasted_iota(jnp.int32, (chunk, rows), 1)
    ones_block = (lax.div(col_ids, states) == row_ids).astype(bf16)
    gate_s[...] = jnp.dot(normed_ref[...], gate_weight_ref[...], preferred_element_type=f32)
    dgated_s[...] = jnp.dot(cot_ref[...], out_weight_ref[...], preferred_element_type=f32)

    def spread(ref, at):
        one = ref[pl.ds(at, states), :]
        return jnp.concatenate([one] * tiles, axis=1) if tiles > 1 else one

    def softplus(v):
        return jnp.maximum(v, 0.0) + jnp.log1p(jnp.exp(-jnp.abs(v)))

    def run_forward(step, state, low_s):
        base = pl.multiple_of(step * chunk, chunk)
        cut = pl.ds(base, chunk)
        step_size = softplus(pre_ref[cut, :])
        keep = mask_ref[cut, 1:2]
        live = mask_ref[cut, 0:1]
        gate = gate_s[cut, :]
        step_s[cut, :] = step_size + far * (1.0 - keep)
        drive_s[cut, :] = step_size * act_ref[cut, :].astype(f32)
        dscan_s[cut, :] = dgated_s[cut, :] * live * gate * jax.nn.sigmoid(gate)
        for i in range(chunk):
            row = pl.ds(base + i, 1)
            at = pl.multiple_of((base + i) * states, states)
            power = step_s[row, :] * decay_two
            power_s[pl.ds(at, states), :] = power
            state = jnp.exp2(power) * state + drive_s[row, :] * spread(in_ref, at)
            state_s[pl.ds(at, states), :] = state
            low_s[pl.ds(i * states, states), :] = state.astype(bf16)
        return state

    def sum_forward(step, low_s):
        cut = pl.ds(pl.multiple_of(step * chunk, chunk), chunk)
        low = low_s[...]
        scanned_s[cut, :] = jnp.dot(out_block_ref[cut, :], low, preferred_element_type=f32)
        dout_ref[cut, :] = lax.dot_general(dscan_s[cut, :].astype(bf16), low, last_dims, preferred_element_type=f32)

    def forward(pair, state):
        sum_forward(jnp.maximum(2 * pair - 1, 0), odd_s)
        state = run_forward(2 * pair, state, even_s)
        sum_forward(2 * pair, even_s)
        return run_forward(2 * pair + 1, state, odd_s)

    zero = jnp.zeros((states, width), f32)
    odd_s[...] = jnp.zeros_like(odd_s)
    lax.fori_loop(0, count // 2, forward, zero)
    sum_forward(count - 1, odd_s)
    decay_s[...] = zero

    def run_backward(step, handed, low_s, rate_s):
        base = pl.multiple_of(step * chunk, chunk)
        acc = decay_s[...]
        for i in reversed(range(chunk)):
            row = pl.ds(base + i, 1)
            at = pl.multiple_of((base + i) * states, states)
            power = power_s[pl.ds(at, states), :]
            adjoint = dscan_s[row, :] * spread(out_ref, at) + handed
            low_s[pl.ds(i * states, states), :] = adjoint.astype(bf16)
            handed = jnp.exp2(power) * adjoint
            if i == 0:
                before = pl.multiple_of(jnp.maximum(at - states, 0), states)
            else:
                before = pl.multiple_of((base + (i - 1)) * states, states)
            rate = handed * state_s[pl.ds(before, states), :]
            rate_s[pl.ds(i * states, states), :] = (rate * decay).astype(bf16)
            acc = acc + rate * power
        decay_s[...] = acc
        return handed

    def sum_backward(step, low_s, rate_s, accs):
        skip_acc, bias_acc = accs
        cut = pl.ds(pl.multiple_of(step * chunk, chunk), chunk)
        low = low_s[...]
        in_sum = jnp.dot(in_block_ref[cut, :], low, preferred_element_type=f32)
        rate_sum = jnp.dot(ones_block, rate_s[...], preferred_element_type=f32)
        din_ref[cut, :] = lax.dot_general(drive_s[cut, :].astype(bf16), low, last_dims, preferred_element_type=f32)
        pre = pre_ref[cut, :]
        live = mask_ref[cut, 0:1]
        gate = gate_s[cut, :]
        sig = jax.nn.sigmoid(gate)
        act = act_ref[cut, :].astype(f32)
        dscan = dscan_s[cut, :]
        dpre = ((rate_sum + in_sum * act) * jax.nn.sigmoid(pre)).astype(bf16)
        dpre_s[cut, :] = dpre
        dact_ref[cut, :] = dscan * skip + in_sum * softplus(pre)
        branch = (scanned_s[cut, :] + skip * act) * live
        gated_ref[cut, :] = (branch * gate * sig).astype(bf16)
        dgate_ref[cut, :] = (dgated_s[cut, :] * branch * sig * (1.0 + gate * (1.0 - sig))).astype(bf16)
        skip_acc = skip_acc + jnp.sum((dscan * act).reshape(chunk // 8, 8, width), axis=0)
        bias_acc = bias_acc + jnp.sum(dpre.astype(f32).reshape(chunk // 8, 8, width), axis=0)
        return skip_acc, bias_acc

    eight = jnp.zeros((8, width), f32)
    last = count - 1
    handed = run_backward(last, zero, odd_s, odd_rate_s)

    def backward(pair, carry):
        handed, accs = carry
        step = last - 2 * pair
        accs = sum_backward(step, odd_s, odd_rate_s, accs)
        handed = run_backward(step - 1, handed, even_s, even_rate_s)
        accs = sum_backward(step - 1, even_s, even_rate_s, accs)
        handed = run_backward(step - 2, handed, odd_s, odd_rate_s)
        return handed, accs

    handed, accs = lax.fori_loop(0, count // 2 - 1, backward, (handed, (eight, eight)))
    accs = sum_backward(1, odd_s, odd_rate_s, accs)
    run_backward(0, handed, even_s, even_rate_s)
    skip_acc, bias_acc = sum_backward(0, even_s, even_rate_s, accs)
    rank_grad_ref[...] = lax.dot_general(dpre_s[...], step_weight_ref[...], last_dims, preferred_element_type=f32)
    step_part = lax.dot_general(rank_ref[...], dpre_s[...], first_dims, preferred_element_type=f32)
    small = jnp.concatenate(
        [jnp.sum(skip_acc, axis=0, keepdims=True), jnp.sum(bias_acc, axis=0, keepdims=True), jnp.zeros((6, width), f32)],
        axis=0,
    )

    @pl.when(first)
    def _():
        step_grad_ref[...] = step_part
        sums_ref[0:8, :] = small
        sums_ref[8:, :] = decay_s[...] * (1.0 / log2e)

    @pl.when(jnp.logical_not(first))
    def _():
        step_grad_ref[...] += step_part
        sums_ref[0:8, :] += small
        sums_ref[8:, :] += decay_s[...] * (1.0 / log2e)


def scan_both_ways(start, blocks, width, pre, act, normed, cot, weights, rank_low, step_weight, mask, tables, skip, decay_log):
    micro, tok, chans = pre.shape
    dim = normed.shape[2]
    states = decay_log.shape[0]
    rows = chunk * states
    rank = rank_low.shape[2]
    inside = start % (weights.shape[2] // width)

    def whole(r, c):
        return pl.BlockSpec((None, r, c), lambda j, m: (m, 0, 0))

    def each(r, c):
        return pl.BlockSpec((None, None, r, c), lambda j, m: (j, m, 0, 0))

    def part(r):
        return pl.BlockSpec((None, r, width), lambda j, m: (m, 0, j))

    def later(r):
        return pl.BlockSpec((None, r, width), lambda j, m: (m, 0, j + start))

    def param(r, at):
        return pl.BlockSpec((r, width), lambda j, m: (0, j + at))

    def shaped(*dims, kind=f32):
        return jax.ShapeDtypeStruct(dims, kind)

    total = blocks * width
    return pl.pallas_call(
        functools.partial(scan_kernel, states),
        grid=(blocks, micro),
        in_specs=[later(tok)] * 2
        + [whole(tok, dim)] * 2
        + [pl.BlockSpec((None, dim, width), lambda j, m, k=k: (k, 0, j + inside)) for k in range(2)]
        + [whole(tok, rank), param(rank, start), whole(tok, mask.shape[2])]
        + [whole(tok * states, 128)] * 2
        + [whole(tok, rows)] * 2
        + [param(1, start), param(states, start)],
        out_specs=[part(tok)] * 3
        + [param(rank, 0), param(8 + states, 0), each(tok, rank), each(tok, rows), each(tok, rows)],
        out_shape=[shaped(micro, tok, total, kind=bf16)] * 2
        + [shaped(micro, tok, total), shaped(rank, total), shaped(8 + states, total)]
        + [shaped(blocks, micro, tok, rank), shaped(blocks, micro, tok, rows), shaped(blocks, micro, tok, rows)],
        scratch_shapes=[pltpu.VMEM((tok, width), f32)] * 6
        + [pltpu.VMEM((tok, width), bf16)]
        + [pltpu.VMEM((tok * states, width), f32)] * 2
        + [pltpu.VMEM((rows, width), bf16)] * 4
        + [pltpu.VMEM((states, width), f32)],
        compiler_params=pltpu.CompilerParams(
            dimension_semantics=("arbitrary", "arbitrary"), vmem_limit_bytes=58 * 2**20
        ),
        cost_estimate=small_cost,
    )(pre, act, normed, cot, weights, weights, rank_low, step_weight, mask, *tables, skip[None], decay_log)


def halves(values):
    high = values.astype(bf16)
    return high, (values - high.astype(f32)).astype(bf16)


def middle_kernel(states, selected_ref, weight_ref, bias_ref, pre_ref, rank_ref, in_ref, out_ref, in_block_ref, out_block_ref):
    tokens = selected_ref.shape[0]
    rank = weight_ref.shape[0]
    rows = chunk * states
    selected = selected_ref[...]
    low = selected[:, :rank].astype(bf16)
    rank_ref[...] = low
    pre_ref[...] = jnp.dot(low, weight_ref[...], preferred_element_type=f32) + bias_ref[...]
    state_ids = lax.broadcasted_iota(jnp.int32, (states, rows), 0)
    col_ids = lax.broadcasted_iota(jnp.int32, (states, rows), 1)
    spreading = (lax.rem(col_ids, states) == state_ids).astype(bf16)
    row_ids = lax.broadcasted_iota(jnp.int32, (chunk, rows), 0)
    chunk_cols = lax.broadcasted_iota(jnp.int32, (chunk, rows), 1)
    same = lax.div(chunk_cols, states) == row_ids
    ones = jnp.ones((2 * chunk, 128), bf16)
    for at, lanes_ref, block_ref in ((rank, in_ref, in_block_ref), (rank + states, out_ref, out_block_ref)):
        tiled = [
            jnp.dot(v, spreading, preferred_element_type=f32) for v in halves(selected[:, at : at + states])
        ]
        for i in range(tokens // chunk):
            cut = slice(i * chunk, (i + 1) * chunk)
            high, rest = [jnp.where(same, v[cut], 0.0).astype(bf16) for v in tiled]
            block_ref[cut, :] = high
            lanes_ref[i * rows : (i + 1) * rows, :] = lax.dot_general(
                jnp.concatenate([high, rest], axis=0), ones, first_dims, preferred_element_type=f32
            )


def middle(selected, weight, bias, states):
    tokens, picked = selected.shape
    rank, channels = weight.shape
    rows = chunk * states
    cut = min(128, tokens)

    def fixed(r, c):
        return pl.BlockSpec((r, c), lambda i: (0, 0))

    def part(r, c):
        return pl.BlockSpec((r, c), lambda i: (i, 0))

    def shaped(r, c, kind):
        return jax.ShapeDtypeStruct((r, c), kind)

    return pl.pallas_call(
        functools.partial(middle_kernel, states),
        grid=(tokens // cut,),
        in_specs=[part(cut, picked), fixed(rank, channels), fixed(1, channels)],
        out_specs=[part(cut, channels), part(cut, rank)]
        + [part(cut * states, 128)] * 2
        + [part(cut, rows)] * 2,
        out_shape=[shaped(tokens, channels, f32), shaped(tokens, rank, bf16)]
        + [shaped(tokens * states, 128, f32)] * 2
        + [shaped(tokens, rows, bf16)] * 2,
        compiler_params=pltpu.CompilerParams(dimension_semantics=("arbitrary",), vmem_limit_bytes=48 * 2**20),
    )(selected, weight, bias[None])


def unblocked(fulls, states):
    tok, rows = fulls[0].shape[2:]
    same = jnp.arange(tok)[:, None] % chunk == jnp.arange(rows)[None, :] // states
    picks = (jnp.arange(rows)[:, None] % states == jnp.arange(states)[None, :]).astype(f32)
    full = sum(v[j] for v in fulls for j in range(v.shape[0]))
    return jnp.dot(jnp.where(same[None], full, 0.0), picks, precision=highest)


def behind(values, steps):
    return values if steps == 0 else pltpu.roll(values, steps, 0)


def ahead(values, steps):
    return values if steps == 0 else pltpu.roll(values, values.shape[0] - steps, 0)


def convolve(inner, mask_ref, weight_ref, bias_ref):
    taps = weight_ref.shape[0]
    total = bias_ref[...] + weight_ref[taps - 1 : taps, :] * inner
    for back in range(1, taps):
        tap = taps - 1 - back
        total = total + weight_ref[tap : tap + 1, :] * behind(inner, back) * mask_ref[:, back : back + 1]
    return total


def inner_kernel(normed_ref, weight_ref, mask_ref, conv_ref, bias_ref, select_ref, inner_ref, act_ref, selected_ref):
    inner = jnp.dot(normed_ref[...], weight_ref[...], preferred_element_type=f32)
    inner_ref[...] = inner
    convolved = convolve(inner, mask_ref, conv_ref, bias_ref)
    act = (convolved * jax.nn.sigmoid(convolved)).astype(bf16)
    act_ref[...] = act
    part = jnp.dot(act, select_ref[...], preferred_element_type=f32)
    selected_ref[...] = jnp.where(pl.program_id(0) == 0, part, selected_ref[...] + part)


def inner_forward(normed, weight, mask, conv_w, conv_b, select):
    tokens, dim = normed.shape
    channels = weight.shape[1]
    width = min(256, channels)
    taps = conv_w.shape[0]
    picked = select.shape[1]

    def fixed(r, c):
        return pl.BlockSpec((r, c), lambda j: (0, 0))

    def part(r):
        return pl.BlockSpec((r, width), lambda j: (0, j))

    return pl.pallas_call(
        inner_kernel,
        grid=(channels // width,),
        in_specs=[
            fixed(tokens, dim),
            part(dim),
            fixed(tokens, mask.shape[1]),
            part(taps),
            part(1),
            pl.BlockSpec((width, picked), lambda j: (j, 0)),
        ],
        out_specs=[part(tokens), part(tokens), fixed(tokens, picked)],
        out_shape=[
            jax.ShapeDtypeStruct((tokens, channels), f32),
            jax.ShapeDtypeStruct((tokens, channels), bf16),
            jax.ShapeDtypeStruct((tokens, picked), f32),
        ],
        compiler_params=pltpu.CompilerParams(dimension_semantics=("arbitrary",), vmem_limit_bytes=48 * 2**20),
        cost_estimate=small_cost,
    )(normed, weight, mask, conv_w, conv_b[None], select)


def inner_back_kernel(bounds, places_ref, *refs):
    *dact_refs, dsel_ref, select_ref, inner_ref, act_ref, mask_ref, conv_ref, bias_ref, left_ref = refs[:-6]
    dinner_ref, sums_ref, select_grad_ref, sent_ref, kept_ref, dact_s = refs[-6:]
    taps = conv_ref.shape[0]
    tile = pl.program_id(0)
    for ref, low, high in zip(dact_refs, bounds[:-1], bounds[1:]):

        @pl.when(jnp.logical_and(tile >= low, tile < high))
        def _(ref=ref):
            dact_s[...] = ref[...]

    inner = inner_ref[...]
    dsel = dsel_ref[...]
    convolved = convolve(inner, mask_ref, conv_ref, bias_ref)
    sig = jax.nn.sigmoid(convolved)
    dact = dact_s[...] + lax.dot_general(dsel, select_ref[...], last_dims, preferred_element_type=f32)
    dconv = dact * sig * (1.0 + convolved * (1.0 - sig))
    dinner = conv_ref[taps - 1 : taps, :] * dconv
    sums_ref[taps : taps + 1, :] = jnp.sum(dconv, axis=0, keepdims=True)
    sums_ref[taps - 1 : taps, :] = jnp.sum(dconv * inner, axis=0, keepdims=True)
    for back in range(1, taps):
        tap = taps - 1 - back
        masked = dconv * mask_ref[:, back : back + 1]
        sums_ref[tap : tap + 1, :] = jnp.sum(masked * behind(inner, back), axis=0, keepdims=True)
        dinner = dinner + conv_ref[tap : tap + 1, :] * ahead(masked, back)
    low = dinner.astype(bf16)
    dinner_ref[...] = low
    select_grad_ref[...] = lax.dot_general(
        dsel, act_ref[...], first_dims, preferred_element_type=f32
    ).astype(bf16)
    outer, own = kept_ref.shape[1], kept_ref.shape[3]
    for core, out_ref in ((1, sent_ref), (0, kept_ref)):
        for cross in range(2):
            at = (2 * core + cross) * outer
            rows = [
                left_ref[pl.ds(pl.multiple_of(places_ref[at + j] * own, own), own), :] for j in range(outer)
            ]
            full = jnp.dot(jnp.concatenate(rows, axis=0), low, preferred_element_type=f32).astype(bf16)
            for j in range(outer):
                out_ref[cross, j, 0] = full[j * own : (j + 1) * own]


def inner_backward(places, dacts, dsel, select, inner, act, mask, conv_w, conv_b, left):
    tokens, channels = inner.shape
    count = places.shape[0]
    outer, own = count // 4, left.shape[0] // count
    width = min([256] + [v.shape[1] for v in dacts])
    taps = conv_w.shape[0]
    picked = select.shape[1]
    bounds = [0]
    for v in dacts:
        bounds.append(bounds[-1] + v.shape[1] // width)

    def fixed(r, c):
        return pl.BlockSpec((r, c), lambda j, _: (0, 0))

    def part(r):
        return pl.BlockSpec((r, width), lambda j, _: (0, j))

    def held(low, high):
        return pl.BlockSpec((tokens, width), lambda j, _: (0, jnp.clip(j - low, 0, high - low - 1)))

    parts = pl.BlockSpec((2, outer, 1, own, width), lambda j, _: (0, 0, 0, 0, j))
    return pl.pallas_call(
        functools.partial(inner_back_kernel, tuple(bounds)),
        grid_spec=pltpu.PrefetchScalarGridSpec(
            num_scalar_prefetch=1,
            grid=(channels // width,),
            in_specs=[held(low, high) for low, high in zip(bounds[:-1], bounds[1:])]
            + [
                fixed(tokens, picked),
                pl.BlockSpec((width, picked), lambda j, _: (j, 0)),
                part(tokens),
                part(tokens),
                fixed(tokens, mask.shape[1]),
                part(taps),
                part(1),
                fixed(*left.shape),
            ],
            out_specs=[part(tokens), part(8), part(picked), parts, parts],
            scratch_shapes=[pltpu.VMEM((tokens, width), f32)],
        ),
        out_shape=[
            jax.ShapeDtypeStruct((tokens, channels), bf16),
            jax.ShapeDtypeStruct((8, channels), f32),
            jax.ShapeDtypeStruct((picked, channels), bf16),
        ]
        + [jax.ShapeDtypeStruct((2, outer, 1, own, channels), bf16)] * 2,
        compiler_params=pltpu.CompilerParams(dimension_semantics=("arbitrary",), vmem_limit_bytes=52 * 2**20),
        cost_estimate=small_cost,
    )(places, *dacts, dsel, select, inner, act, mask, conv_w, conv_b[None], left)


def project_kernel(micro, count, where_ref, *refs):
    lefts, rights = refs[:count], refs[count : 2 * count]
    here_ref, away_ref, total_s = refs[2 * count :]
    total = None
    for left, right in zip(lefts, rights):
        part = lax.dot_general(left[...], right[...], last_dims, preferred_element_type=f32)
        total = part if total is None else total + part
    total_s[...] = total
    group = total.shape[0] // micro
    rows = here_ref.shape[1]
    here = where_ref[0] * rows
    for m in range(micro):
        here_ref[m] = total_s[pl.ds(pl.multiple_of(m * group + here, rows), rows), :]
        away_ref[m] = total_s[pl.ds(pl.multiple_of(m * group + (group - rows) - here, rows), rows), :].astype(bf16)


def project(lefts, rights, places, micro, shard_rows):
    tokens = lefts[0].shape[0]
    dim = rights[0].shape[1]
    width = min(256, dim)
    where = lax.axis_index("tensor").astype(jnp.int32)[None]

    def column(plane, at, wide):
        return pl.BlockSpec((None, width, wide), lambda i, _: (plane, i, at))

    return pl.pallas_call(
        functools.partial(project_kernel, micro, len(lefts)),
        grid_spec=pltpu.PrefetchScalarGridSpec(
            num_scalar_prefetch=1,
            grid=(dim // width,),
            in_specs=[pl.BlockSpec(v.shape, lambda i, _: (0, 0)) for v in lefts]
            + [column(*at, v.shape[1]) for at, v in zip(places, lefts)],
            out_specs=[pl.BlockSpec((micro, shard_rows, width), lambda i, _: (0, 0, i))] * 2,
            scratch_shapes=[pltpu.VMEM((tokens, width), f32)],
        ),
        out_shape=[
            jax.ShapeDtypeStruct((micro, shard_rows, dim), f32),
            jax.ShapeDtypeStruct((micro, shard_rows, dim), bf16),
        ],
        compiler_params=pltpu.CompilerParams(dimension_semantics=("arbitrary",), vmem_limit_bytes=48 * 2**20),
        cost_estimate=small_cost,
    )(where, *lefts, *rights)


def spread_sum(lefts, rights, places, micro, shard_rows):
    if lax.axis_size("tensor") == 2:
        here, away = project(lefts, rights, places, micro, shard_rows)
        return here, swapped(away, "tensor", 1)
    total = 0.0
    for left, right, (plane, at) in zip(lefts, rights, places):
        wide = left.shape[1]
        total = total + lax.dot_general(
            left, right[plane, :, at * wide : (at + 1) * wide], last_dims, preferred_element_type=f32
        )
    total = total.reshape(micro, -1, total.shape[1])
    away = lax.psum_scatter(total.astype(bf16), "tensor", scatter_dimension=1, tiled=True)
    return jnp.zeros(away.shape, f32), away


def parts_kernel(kinds, outer, places_ref, *refs):
    out_ref = refs[-1]
    own = refs[0].shape[0]
    for kind in range(kinds):
        left = jnp.concatenate([r[...] for r in refs[kind * outer : (kind + 1) * outer]], axis=0)
        full = jnp.dot(left, refs[kinds * outer + kind][...], preferred_element_type=f32).astype(bf16)
        for j in range(outer):
            out_ref[j, kind] = full[j * own : (j + 1) * own]


def grad_parts(places, near, lefts, rights):
    kinds = len(lefts)
    count = places.shape[0]
    outer = count // 4
    own = lefts[0].shape[0] // count
    tokens = lefts[0].shape[1]
    width = rights[0].shape[1]
    offset = 0 if near else 2 * outer

    def left_spec(j):
        return pl.BlockSpec((own, tokens), lambda q, where: (where[offset + q * outer + j], 0))

    return pl.pallas_call(
        functools.partial(parts_kernel, kinds, outer),
        grid_spec=pltpu.PrefetchScalarGridSpec(
            num_scalar_prefetch=1,
            grid=(2,),
            in_specs=[left_spec(j) for _ in range(kinds) for j in range(outer)]
            + [pl.BlockSpec(v.shape, lambda q, where: (0, 0)) for v in rights],
            out_specs=pl.BlockSpec((None, outer, kinds, own, width), lambda q, where: (q, 0, 0, 0, 0)),
        ),
        out_shape=jax.ShapeDtypeStruct((2, outer, kinds, own, width), bf16),
        compiler_params=pltpu.CompilerParams(dimension_semantics=("arbitrary",), vmem_limit_bytes=48 * 2**20),
        cost_estimate=small_cost,
    )(places, *[v for v in lefts for _ in range(outer)], *rights)


def join(*trees):
    return lax.optimization_barrier(trees)


def summed(first, second, *more):
    total = first.astype(f32) + second.astype(f32)
    for v in more:
        total = total + v.astype(f32)
    return total


def sums_kernel(crosses, alongs, outer, *refs):
    given = iter(refs[: 2 * crosses + 3 * alongs])
    outs = iter(refs[2 * crosses + 3 * alongs :])
    for _ in range(crosses):
        kept, got = next(given), next(given)
        next(outs)[...] = (kept[...].astype(f32) + got[...].astype(f32)).astype(bf16)
    for _ in range(alongs):
        kept, got, across = next(given), next(given), next(given)
        next(outs)[...] = kept[0].astype(f32) + got[0].astype(f32) + across[0].astype(f32)
        for j in range(1, outer):
            next(outs)[...] = (kept[j].astype(f32) + got[j].astype(f32) + across[j].astype(f32)).astype(bf16)


def step_sums(crosses, alongs):
    cuts = 4
    in_specs, out_specs, out_shape, given = [], [], [], []
    outer = (crosses + alongs)[0][0].shape[1]

    def taken(shape, first, at, wide):
        block = (None,) + shape[1:-2] + (shape[-2] // cuts, wide)
        return pl.BlockSpec(block, lambda i: (first,) + (0,) * (len(shape) - 3) + (i, at))

    def plain(shape):
        return pl.BlockSpec(shape[:-2] + (shape[-2] // cuts, shape[-1]), lambda i: (0,) * (len(shape) - 2) + (i, 0))

    for kept, got, (at, wide) in crosses:
        shape = kept.shape
        in_specs += [taken(shape, 1, at, wide)] * 2
        given += [kept, got]
        out = shape[1:-1] + (wide,)
        out_specs.append(plain(out))
        out_shape.append(jax.ShapeDtypeStruct(out, bf16))
    for kept, got, across, (at, wide) in alongs:
        shape = kept.shape
        in_specs += [taken(shape, 0, at, wide)] * 2 + [plain(across.shape)]
        given += [kept, got, across]
        out = shape[2:-1] + (wide,)
        out_specs += [plain(out)] * outer
        out_shape += [jax.ShapeDtypeStruct(out, f32 if j == 0 else bf16) for j in range(outer)]
    outs = pl.pallas_call(
        functools.partial(sums_kernel, len(crosses), len(alongs), outer),
        grid=(cuts,),
        in_specs=in_specs,
        out_specs=out_specs,
        out_shape=out_shape,
        compiler_params=pltpu.CompilerParams(dimension_semantics=("arbitrary",), vmem_limit_bytes=48 * 2**20),
        cost_estimate=small_cost,
    )(*given)
    outs = list(outs)
    first, rest = outs[: len(crosses)], outs[len(crosses) :]
    return first, [rest[i * outer : (i + 1) * outer] for i in range(len(alongs))]


def along_moves(rows):
    count = lax.axis_size("dp")
    return rows[:1] + [
        lax.ppermute(v, "dp", [(i, (i + 4 * (j + 1)) % count) for i in range(count)])
        for j, v in enumerate(rows[1:])
    ]


def final_kernel(kinds, *refs):
    *terms, out_ref = refs[: len(refs) - kinds + 1]
    outs = (out_ref,) + refs[len(refs) - kinds + 1 :]
    total = terms[0][...]
    for ref in terms[1:]:
        total = total + ref[...].astype(f32)
    outs[0][...] = total[0]
    if kinds == 2:
        outs[1][...] = total[1].T


def final_sum(terms):
    kinds, own, width = terms[0].shape
    return pl.pallas_call(
        functools.partial(final_kernel, kinds),
        out_shape=[jax.ShapeDtypeStruct((own, width), f32), jax.ShapeDtypeStruct((width, own), f32)][:kinds],
        compiler_params=pltpu.CompilerParams(vmem_limit_bytes=48 * 2**20),
        cost_estimate=small_cost,
    )(*terms)


def doubled(values):
    count = lax.axis_size("dp")
    here = lax.axis_index("dp")
    values = values[None]
    bit = 1
    while bit < count:
        other = swapped(values, "dp", bit)
        low = (here & bit) == 0
        values = jnp.concatenate([jnp.where(low, values, other), jnp.where(low, other, values)], axis=0)
        bit *= 2
    return values


def on_device(
    hidden,
    cotangent,
    lengths,
    order,
    norm_gain,
    input_weight,
    conv_weight,
    conv_bias,
    select_weight,
    step_weight,
    step_bias,
    decay_log,
    skip_gain,
    output_weight,
):
    micro, shard_rows, model_dim = hidden.shape
    count = lax.axis_size("dp")
    outer = count // 4
    group_tok = shard_rows * lax.axis_size("tensor")
    tokens = micro * group_tok
    channels = input_weight.shape[2]
    taps = conv_weight.shape[0]
    states = decay_log.shape[0]
    own = conv_bias.shape[0]
    own_dim = norm_gain.shape[0]
    half = channels // 2
    quarter = channels // 4
    here = lax.axis_index("dp")
    ids = jnp.arange(count, dtype=jnp.int32)
    place, cross, core = here // 4, (here // 2) % 2, here % 2
    places = ((place + ids % outer) % outer) * 4 + (cross ^ (ids // outer) % 2) * 2 + (core ^ ids // (2 * outer))
    places = places.astype(jnp.int32)

    pieces = [norm_gain, conv_weight, conv_bias, step_bias, decay_log, skip_gain]
    packed = doubled(jnp.concatenate([v.reshape(-1) for v in pieces]))
    picked = select_weight.shape[1]
    narrow, packed = join(jnp.concatenate([select_weight.T, step_weight.reshape(-1, own)], axis=0), packed)
    full = []
    at = 0
    for v in pieces:
        part = packed[:, at : at + v.size]
        at += v.size
        if v.ndim == 2:
            part = part.reshape(count, v.shape[0], v.shape[1]).transpose(1, 0, 2).reshape(v.shape[0], -1)
        else:
            part = part.reshape(-1)
        full.append(part)
    gain_full, conv_w, conv_b, step_b, decay_lg, skip_g = full
    narrow = doubled(narrow)
    w_sel = narrow[:, :picked].transpose(0, 2, 1).reshape(channels, picked)
    w_step = narrow[:, picked:].reshape(-1, channels)

    w_inner = lax.all_gather(input_weight[:, 0], "dp", axis=0, tiled=True)
    out_shard = output_weight.T
    weights = []
    for number in range(2):
        cut = slice(number * half, (number + 1) * half)
        both = jnp.stack([input_weight[:, 1, cut], out_shard[:, cut]])
        weights.append(lax.all_gather(both, "dp", axis=1, tiled=True))

    inverse_rms = lax.rsqrt(jnp.mean(hidden * hidden, axis=-1, keepdims=True) + epsilon)
    normal_rows = hidden * inverse_rms
    normed = tensor_gather((normal_rows * gain_full).astype(bf16), 1).reshape(tokens, model_dim)
    normed, cot_rows = join(normed, cotangent)
    cot_full = tensor_gather(cot_rows, 1).reshape(tokens, model_dim)

    position, live_mask = jax.vmap(lambda a, b: positions(a, b, group_tok))(lengths[:, 0], order[:, 0])
    mask = jnp.stack([live_mask] + [(position >= back).astype(f32) for back in range(1, taps)], axis=2)
    flat_mask = mask.reshape(tokens, taps)

    def grouped(v):
        return v.reshape(micro, group_tok, v.shape[-1])

    inner, act, selected = inner_forward(normed, w_inner, flat_mask, conv_w, conv_b, w_sel)
    selected = tensor_sum(selected)
    lefts = (normed.T, cot_full.T)
    pre_step, rank_low, *tables = middle(selected, w_step, step_b, states)
    tables = tuple(grouped(v) if v.shape[0] == tokens else v.reshape(micro, -1, v.shape[-1]) for v in tables)
    rank_rows = grouped(rank_low)

    gated, dgate, dact, step_grads, sums, rank_grads, dins, douts = [[] for _ in range(8)]
    rows_now = (grouped(normed), grouped(cot_full))
    kept, got, across, total = {}, {}, {}, {}
    stages = ((0, 2), (2, 1), (3, 1))

    def whole(piece):
        return kept[piece], got[piece], (0, kept[piece].shape[-1])

    def whole_across(piece):
        return kept[piece], got[piece], across[piece], (0, kept[piece].shape[-1])

    for number, (start, blocks) in enumerate(stages):
        cross, along = (), ()
        if number > 0:
            cross, along = step_sums(
                [whole(number - 1)], [whole_across(number - 2)] if number > 1 else []
            )
        rows_now, cross, along = join(rows_now, cross, along)
        cross = [swapped(v, "dp", 2) for v in cross]
        along = [along_moves(v) for v in along]
        results = scan_both_ways(
            start,
            blocks,
            quarter,
            grouped(pre_step),
            grouped(act),
            *rows_now,
            weights[start // 2],
            rank_rows,
            w_step,
            mask,
            tables,
            skip_g,
            decay_lg,
        )
        results, cross, along = join(results, cross, along)
        if number > 0:
            across[number - 1] = cross[0]
        if number > 1:
            total[number - 2] = along[0]
        for held, v in zip((gated, dgate, dact), results[:3]):
            held.append(v.reshape(tokens, -1))
        for held, v in zip((step_grads, sums, rank_grads, dins, douts), results[3:]):
            held.append(v)
        if number == 2:
            break
        rights = (dgate[number], gated[number])
        sent = grad_parts(places, False, lefts, rights)
        sent, lefts = join(sent, lefts)
        got[number] = swapped(sent, "dp", 1)
        kept[number] = grad_parts(places, True, lefts, rights)
        rows_now, kept[number] = join(rows_now, kept[number])

    rank_grad = sum(v[j] for v in rank_grads for j in range(v.shape[0]))
    select_terms = jnp.concatenate([rank_grad, unblocked(dins, states), unblocked(douts, states)], axis=2)
    select_terms = select_terms.reshape(tokens, -1)
    select_terms, gated[2], dgate[2], lefts = join(select_terms, gated[2], dgate[2], lefts)
    select_terms = tensor_sum(select_terms)
    sent = grad_parts(places, False, lefts, (dgate[2], gated[2]))
    sent, lefts = join(sent, lefts)
    got[2] = swapped(sent, "dp", 1)
    kept[2] = grad_parts(places, True, lefts, (dgate[2], gated[2]))
    got[2], kept[2], select_terms = join(got[2], kept[2], select_terms)
    select_low = select_terms.astype(bf16)
    cross, along = step_sums([whole(2)], [whole_across(1)])
    cross, along, select_low = join(cross, along, select_low)
    across[2] = swapped(cross[0], "dp", 2)
    along = along_moves(along[0])
    dinner, conv_sums, select_grad, sent, kept[3] = inner_backward(
        places, dact, select_low, w_sel, inner, act, flat_mask, conv_w, conv_b, lefts[0]
    )
    across[2], along, dinner, conv_sums, select_grad, sent, kept[3] = join(
        across[2], along, dinner, conv_sums, select_grad, sent, kept[3]
    )
    total[1] = along

    got[3] = swapped(sent, "dp", 1)
    mixed_select = select_grad.reshape(-1, count, own).transpose(1, 0, 2).reshape(count, own_dim, -1)
    mixed_step = jnp.concatenate(step_grads, axis=1).astype(bf16).reshape(count, own_dim, -1)
    split = mixed_select.shape[2]
    mixed = jnp.take(jnp.concatenate([mixed_select, mixed_step], axis=2), places, axis=0)
    mixed = mixed.reshape((2, 2, outer, 1) + mixed.shape[1:])
    kept[4] = mixed[0]
    got[4] = swapped(mixed[1], "dp", 1)
    _, along = step_sums([], [whole_across(2)])
    got[3], along, kept[4], got[4] = join(got[3], along, kept[4], got[4])
    along = along_moves(along[0])
    cross, _ = step_sums([(kept[3], got[3], (0, half)), (kept[3], got[3], (1, half)), whole(4)], [])
    first, second = swapped(cross[0], "dp", 2), cross[1]
    across[4] = swapped(cross[2], "dp", 2)
    norm_here, norm_away = spread_sum(
        dgate + [dinner],
        [weights[0], weights[1], weights[1], w_inner[None]],
        [(0, 0), (0, 0), (0, 1), (0, 0)],
        micro,
        shard_rows,
    )
    first, across[4], along, second, norm_here = join(first, across[4], along, second, norm_here)
    total[2] = along
    _, along = step_sums([], [(kept[3], got[3], first, (0, half)), whole_across(4)])
    second, along, gated = join(second, along, gated)
    second = swapped(second, "dp", 2)
    along = [along_moves(v) for v in along]
    layer_here, layer_away = spread_sum(
        gated, [weights[0], weights[1], weights[1]], [(1, 0), (1, 0), (1, 1)], micro, shard_rows
    )
    dnormed = norm_here + norm_away.astype(f32)
    gain_part = jnp.sum(dnormed * normal_rows, axis=(0, 1))
    vectors = jnp.concatenate([conv_sums[: taps + 1], jnp.concatenate(sums, axis=1)], axis=0)
    vectors = vectors.reshape(-1, count, own).transpose(1, 0, 2).reshape(count, -1)
    vectors = jnp.concatenate([gain_part.reshape(count, own_dim), vectors], axis=1)
    second, along, layer_here, vectors = join(second, along, layer_here, vectors)
    total[3], total[4] = along
    _, along = step_sums([], [(kept[3], got[3], second, (1, half))])
    along, vectors = join(along, vectors)
    total[5] = along_moves(along[0])
    vectors = reduce_scatter(vectors)[0]
    gain_total = tensor_sum(vectors[:own_dim])
    vectors = vectors[own_dim:].reshape(-1, own)

    layer_rows = hidden + (layer_here + layer_away.astype(f32))
    dnormal = dnormed * gain_full
    grad_rows = cotangent.astype(f32) + inverse_rms * (
        dnormal - normal_rows * jnp.mean(dnormal * normal_rows, axis=-1, keepdims=True)
    )
    sums_of = [final_sum(total[n]) for n in range(6)]
    gate_grad = jnp.concatenate([v[0] for v in sums_of[:3]], axis=1)
    out_grad = jnp.concatenate([v[1] for v in sums_of[:3]], axis=0)
    inner_grad = jnp.concatenate([sums_of[3][0], sums_of[5][0]], axis=1)
    mixed = sums_of[4][0]
    return (
        layer_rows,
        grad_rows,
        gain_total,
        jnp.stack([inner_grad, gate_grad], axis=1),
        vectors[:taps],
        vectors[taps],
        mixed[:, :split].reshape(-1, own).T,
        mixed[:, split:].reshape(-1, channels),
        vectors[taps + 2],
        vectors[taps + 9 :],
        vectors[taps + 1],
        out_grad,
    )


def solution(mesh):
    in_specs = (
        P(None, ("dp", "tensor"), None),
        P(None, ("dp", "tensor"), None),
        P(None, "dp", None),
        P(None, "dp", None),
        P("dp"),
        P("dp", None, "tensor"),
        P(None, ("tensor", "dp")),
        P(("tensor", "dp")),
        P(("tensor", "dp"), None),
        P("dp", "tensor"),
        P(("tensor", "dp")),
        P(None, ("tensor", "dp")),
        P(("tensor", "dp")),
        P("tensor", "dp"),
    )
    out_specs = (
        P(None, ("dp", "tensor"), None),
        P(None, ("dp", "tensor"), None),
        P("dp"),
        P("dp", None, "tensor"),
        P(None, ("tensor", "dp")),
        P(("tensor", "dp")),
        P(("tensor", "dp"), None),
        P("dp", "tensor"),
        P(("tensor", "dp")),
        P(None, ("tensor", "dp")),
        P(("tensor", "dp")),
        P("tensor", "dp"),
    )
    return jax.shard_map(
        on_device, mesh=mesh, in_specs=in_specs, out_specs=out_specs, check_vma=False
    )
```

time: 797 us -> 607 us (0.76)
  waiting for transfers between devices: 345 us -> 156 us
  Pallas kernels: 105 us -> 232 us
  matrix products: 89.6 us -> 4.05 us
  blocking collectives: 68.5 us -> 0 us
  starting transfers between devices: 35.7 us -> 81.8 us
  other arithmetic: 63.6 us -> 33.6 us
  local copies, waits for them, and re-layouts: 67.1 us -> 76.8 us
    pallas_call x1 -> x27, Pallas kernels: 105 us -> 232 us  [the longest x3 117 us: scan_both_ways(): pl.pallas_call(functools.partial(scan_kernel, states), grid=(blocks, micr...]
    dot_general x18 -> x0, matrix products: 88.9 us -> none  [the longest x6 31.5 us: product(): lax.dot_general(part.reshape(-1, part.shape[-1]), right, dims, preferred_...]
    all_gather x2, waiting for transfers between devices: 116 us -> 32.6 us  [on_device(): weights.append(lax.all_gather(both, 'dp', axis=1, tiled=True))]
    ppermute x18 -> x3, waiting for transfers between devices: 86.4 us -> 4.04 us  [moved(): lax.ppermute(values, 'dp', [((i + 4 * offset) % count, i) for i in range(...]
    all_gather x3 -> x0, blocking collectives: 68.5 us -> none  [the longest x1 24.3 us: on_device(): lax.all_gather(jnp.concatenate([v.reshape(-1) for v in pieces]), 'dp', ax...]
    ppermute x0 -> x18, starting transfers between devices: none -> 46.3 us  [along_moves(): lax.ppermute(v, 'dp', [(i, (i + 4 * (j + 1)) % count) for i in range(coun...]
    convert_element_type x13 -> x0, other arithmetic: 40 us -> none  [the longest x1 16.3 us: on_device(): act_low = jax.nn.silu(convolved).astype(bf16)]
    ppermute x19 -> x28, waiting for transfers between devices: 143 us -> 106 us  [swapped(): return lax.ppermute(values, axis, [(i, i ^ bit) for i in range(count)])]
  transfers between devices with their start and end apart: 40 -> 52, of which waited for: 15 -> 21; matrix products, arithmetic and copies ran while one was open for 23% -> 10% of each run, Pallas kernels for 0% -> 35%
where the time goes in v2:
time: 607 us; the launch traced here: 600 us
  Pallas kernels  232 us (38%)
  waiting for transfers between devices  156 us (26%)
  starting transfers between devices  81.8 us (13%)
  local copies, waits for them, and re-layouts  76.8 us (13%)
  other arithmetic  33.6 us (6%)
  between operations  15.6 us (3%)
    pallas_call x3, Pallas kernels, scan_both_ways(): pl.pallas_call(functools.partial(scan_kernel, states), grid=(blocks, micr...  117 us
    ppermute x28, waiting for transfers between devices, swapped(): return lax.ppermute(values, axis, [(i, i ^ bit) for i in range(count)])  106 us
    unnamed x237, local copies, waits for them, and re-layouts  48.3 us
    ppermute x18, starting transfers between devices, along_moves(): lax.ppermute(v, 'dp', [(i, (i + 4 * (j + 1)) % count) for i in range(coun...  46.3 us
    ppermute x28, starting transfers between devices, swapped(): return lax.ppermute(values, axis, [(i, i ^ bit) for i in range(count)])  33.2 us
    all_gather x2, waiting for transfers between devices, on_device(): weights.append(lax.all_gather(both, 'dp', axis=1, tiled=True))  32.6 us
    pallas_call x7, Pallas kernels, step_sums(): pl.pallas_call(functools.partial(sums_kernel, len(crosses), len(alongs),...  27.4 us
    pallas_call x2, Pallas kernels, project(): pl.pallas_call(functools.partial(project_kernel, micro, len(lefts)), grid...  24.9 us
  transfers between devices with their start and end apart: 52, of which 21 were waited for; matrix products, arithmetic and copies ran while one was open for 10% of the time, Pallas kernels for 35%

profile of v2, /device:TPU:0, one launch (start us, length us, event | category | flops | bytes accessed | tf_op | source)
XLA Modules:
  0.0 600.4 jit_solution(2331170220740725472)
XLA Ops:
  28.3 9.8 %collective-permute-done.3 = f32[8,3072]{1,0:T(8,128)S(1)} collective-permute-done((f32[8,3072]{1,0:T(8,128)S(1)}, f32[8,3072]{1,0:T(8,128)S(1)}, u32[]{:S(2)}, u32[]{:S(2)}) %collective-permute-start.3) | collective-permute-done | bytes 98336 | tf_op jit(solution)/shard_map/ppermute | solution.py:35
  47.5 12.2 %collective-permute-done.7 = bf16[4,288,128]{2,1,0:T(8,128)(2,1)S(1)} collective-permute-done((bf16[4,288,128]{2,1,0:T(8,128)(2,1)S(1)}, bf16[4,288,128]{2,1,0:T(8,128)(2,1)S(1)}, u32[]{:S(2)}, u32[]{:S(2)}) %collective-permute-start.7) | collective-permute-done | bytes 294944 | tf_op jit(solution)/shard_map/ppermute | solution.py:35
  73.7 39.1 %collective-permute-done.8 = bf16[8,288,128]{2,1,0:T(8,128)(2,1)} collective-permute-done((bf16[8,288,128]{2,1,0:T(8,128)(2,1)}, bf16[8,288,128]{2,1,0:T(8,128)(2,1)}, u32[]{:S(2)}, u32[]{:S(2)}) %collective-permute-start.8) | collective-permute-done | bytes 589856 | tf_op jit(solution)/shard_map/ppermute | solution.py:35
  124.5 11.8 %shard_map.229 = (f32[512,2048]{1,0:T(8,128)}, bf16[512,2048]{1,0:T(8,128)(2,1)S(1)}, f32[512,160]{1,0:T(8,128)S(1)}) custom-call(bf16[512,2048]{1,0:T(8,128)(2,1)S(1)} %bitcast.196, bf16[2048,2048]{1,0:T(8,128)(2,1)} %bitcast.271, f32[512,4]{1,0:T(8,128)S(1)} %stack.35.mask_ref.refs_7_, f32[4,2048]{1,0:T(4,128)S(1)} %bitcast.234, f32[1,2048]{1,0:T(1,128)S(1)} %bitcast.236, ...), custom_call_target="tpu_custom_call" | custom-call | flops 1 | bytes 1 | tf_op jit(solution)/shard_map/pallas_call | solution.py:424
  148.2 5.0 shard_map.230
  157.3 32.6 %all-gather.5.cloned.1.call-done.gate_weight_ref.out_weight_ref.refs_4_.refs_3_ = bf16[2,2048,1024]{2,1,0:T(8,128)(2,1)} async-done(((bf16[2,128,1024]{2,1,0:T(8,128)(2,1)}), bf16[2,2048,1024]{2,1,0:T(8,128)(2,1)}) %all-gather.5.cloned.1.call-update) | async-done | bytes 8388624 | tf_op jit(solution)/shard_map/all_gather | solution.py:800
  189.9 54.5 %shard_map.231 = (bf16[2,256,1024]{2,1,0:T(8,128)(2,1)}, bf16[2,256,1024]{2,1,0:T(8,128)(2,1)}, f32[2,256,1024]{2,1,0:T(8,128)}, f32[128,1024]{1,0:T(8,128)}, f3...) custom-call(f32[2,256,2048]{2,1,0:T(8,128)} %bitcast.197, ...), custom_call_target="tpu_custom_call" | custom-call | flops 1 | bytes 1 | tf_op jit(solution)/shard_map/pallas_call | solution.py:287
  246.9 5.6 shard_map.232
  252.7 5.6 shard_map.233.refs_0_.refs_2_
  262.9 4.4 shard_map.234
  267.9 31.2 %shard_map.235 = (bf16[2,256,512]{2,1,0:T(8,128)(2,1)}, bf16[2,256,512]{2,1,0:T(8,128)(2,1)}, f32[2,256,512]{2,1,0:T(8,128)}, f32[128,512]{1,0:T(8,128)}, f32[24...) custom-call(f32[2,256,2048]{2,1,0:T(8,128)} %bitcast.198, ...), custom_call_target="tpu_custom_call" | custom-call | flops 1 | bytes 1 | tf_op jit(solution)/shard_map/pallas_call | solution.py:287
  299.0 16.3 %collective-permute-done.12.refs_4_ = bf16[4,2,128,1024]{3,2,1,0:T(8,128)(2,1)} collective-permute-done((bf16[4,2,128,1024]{3,2,1,0:T(8,128)(2,1)}, bf16[4,2,128,1024]{3,2,1,0:T(8,128)(2,1)}, u32[]{:S(2)}, u32[]{:S(2)}) %collective-permute-start.12) | collective-permute-done | bytes 2097184 | tf_op jit(solution)/shard_map/ppermute | solution.py:35
  326.4 5.2 shard_map.238
  337.8 31.2 %shard_map.239 = (bf16[2,256,512]{2,1,0:T(8,128)(2,1)}, bf16[2,256,512]{2,1,0:T(8,128)(2,1)}, f32[2,256,512]{2,1,0:T(8,128)}, f32[128,512]{1,0:T(8,128)}, f32[24...) custom-call(f32[2,256,2048]{2,1,0:T(8,128)} %bitcast.199, ...), custom_call_target="tpu_custom_call" | custom-call | flops 1 | bytes 1 | tf_op jit(solution)/shard_map/pallas_call | solution.py:287
  383.9 9.5 %collective-permute-done.19 = f32[512,160]{1,0:T(8,128)S(1)} collective-permute-done((f32[512,160]{1,0:T(8,128)S(1)}, f32[512,160]{1,0:T(8,128)S(1)}, u32[]{:S(2)}, u32[]{:S(2)}) %collective-permute-start.19) | collective-permute-done | bytes 327712 | tf_op jit(solution)/shard_map/ppermute | solution.py:35
  399.5 10.6 %collective-permute-start.21 = (bf16[2,128,512]{2,1,0:T(8,128)(2,1)S(1)}, bf16[2,128,512]{2,1,0:T(8,128)(2,1)S(1)}, u32[]{:S(2)}, u32[]{:S(2)}) collective-permute-start(bf16[2,128,512]{2,1,0:T(8,128)(2,1)S(1)} %get-tuple-element.301), channel_id=1, source_target_pairs={{0,8},{2,10},{4,12},{6,14},{8,16},{10,18},{12,20},{14,22},{16,24},... | collective-permute-start | bytes 786440 | tf_op jit(solution)/shard_map/ppermute | solution.py:702
  412.4 19.4 %shard_map.243 = (bf16[512,2048]{1,0:T(8,128)(2,1)}, f32[8,2048]{1,0:T(8,128)S(1)}, bf16[160,2048]{1,0:T(8,128)(2,1)S(1)}, bf16[2,4,1,128,2048]{4,3,2,1,0:T(8,128)(2,1)}, bf16[2,4,1,128,2048]{4,3,2,1,0:T(8,128)(2,1)}) custom-call(s32[16]{0:T(128)S(1)} %get-tuple-element.481.places_ref, f32[512,1024]{1,0:T(8,128)} %bitcast.281, f32[512,512]{1,0:T(8,128)} %bitcast.286, ...), custom_call_target="tpu_custom_call" | custom-call | flops 1 | bytes 1 | tf_op jit(solution)/shard_map/pallas_call | solution.py:509
  457.4 4.6 shard_map.245
  463.5 14.9 %shard_map.246 = (f32[2,128,2048]{2,1,0:T(8,128)S(1)}, bf16[2,128,2048]{2,1,0:T(8,128)(2,1)}) custom-call(s32[1]{0:T(128)} %bitcast.52.where_ref, bf16[512,1024]{1,0:T(8,128)(2,1)S(1)} %bitcast.208, bf16[512,512]{1,0:T(8,128)(2,1)S(1)} %bitcast.215, bf16[512,512]{1,0:T(8,128)(2,1)S(1)} %bitcast.218, bf16[512,2048]{1,0:T(8,128)(2,1)} %get-tuple-element.335.refs_3_, ...), custom_call_target="tpu_custom_call" | custom-call | flops 1 | bytes 1 | tf_op jit(solution)/shard_map/pallas_call | solution.py:564
  483.7 7.4 %collective-permute-done.28.refs_1_ = bf16[2,128,512]{2,1,0:T(8,128)(2,1)S(1)} collective-permute-done((bf16[2,128,512]{2,1,0:T(8,128)(2,1)S(1)}, bf16[2,128,512]{2,1,0:T(8,128)(2,1)S(1)}, u32[]{:S(2)}, u32[]{:S(2)}) %collective-permute-start.28) | collective-permute-done | bytes 262176 | tf_op jit(solution)/shard_map/ppermute | solution.py:702
  509.7 5.2 collective-permute-start.35
  529.3 8.8 %collective-permute-start.37 = (bf16[1,128,288]{2,1,0:T(8,128)(2,1)S(1)}, bf16[1,128,288]{2,1,0:T(8,128)(2,1)S(1)}, u32[]{:S(2)}, u32[]{:S(2)}) collective-permute-start(bf16[1,128,288]{2,1,0:T(8,128)(2,1)S(1)} %get-tuple-element.356), channel_id=1, source_target_pairs={{0,24},{2,26},{4,28},{6,30},{8,0},{10,2},{12,4},{14,6},{16,8},{18,... | collective-permute-start | bytes 221192 | tf_op jit(solution)/shard_map/ppermute | solution.py:702
  539.2 10.0 %shard_map.248 = (f32[2,128,2048]{2,1,0:T(8,128)S(1)}, bf16[2,128,2048]{2,1,0:T(8,128)(2,1)}) custom-call(s32[1]{0:T(128)} %bitcast.52.where_ref, bf16[512,1024]{1,0:T(8,128)(2,1)S(1)} %bitcast.205, bf16[512,512]{1,0:T(8,128)(2,1)S(1)} %bitcast.221, bf16[512,512]{1,0:T(8,128)(2,1)S(1)} %bitcast.224, ...), custom_call_target="tpu_custom_call" | custom-call | flops 1 | bytes 1 | tf_op jit(solution)/shard_map/pallas_call | solution.py:564
  568.3 5.8 multiply_add_fusion
  (450 shorter events, 224.2 us)
Async XLA Ops:
  7.2 114.3 %all-gather.9.cloned.1.call-start = ((), (), s32[]{:S(2)}) async-start(), calls=%async_computation.2 | async-start | bytes 8912896 | tf_op jit(solution)/shard_map/all_gather | solution.py:794
  9.7 180.2 %all-gather.5.cloned.1.call-start = ((), (), s32[]{:S(2)}) async-start(), calls=%async_computation | async-start | bytes 8912896 | tf_op jit(solution)/shard_map/all_gather | solution.py:800
  12.2 255.6 %all-gather.7.cloned.1.call-start = ((), (), s32[]{:S(2)}) async-start(), calls=%async_computation.1 | async-start | bytes 8912896 | tf_op jit(solution)/shard_map/all_gather | solution.py:800
  41.3 25.0 %collective-permute-start.4 = (bf16[2,128,2048]{2,1,0:T(8,128)(2,1)S(1)}, bf16[2,128,2048]{2,1,0:T(8,128)(2,1)S(1)}, u32[]{:S(2)}, u32[]{:S(2)}) collective-permute-start(bf16[2,128,2048]{2,1,0:T(8,128)(2,1)S(1)} %multiply_convert_fusion), channel_id=1, source_target_pairs={{0,1},{1,0},{2,3},{3,2},{4,5},{5,4},{6,7},{7,6},{8,9},{9,8},{10,11... | collective-permute-start | bytes 3145736 | tf_op jit(solution)/shard_map/ppermute | solution.py:35
  60.6 52.2 %collective-permute-start.8 = (bf16[8,288,128]{2,1,0:T(8,128)(2,1)}, bf16[8,288,128]{2,1,0:T(8,128)(2,1)}, u32[]{:S(2)}, u32[]{:S(2)}) collective-permute-start(bf16[8,288,128]{2,1,0:T(8,128)(2,1)} %pad_maximum_fusion.5), channel_id=1, source_target_pairs={{0,16},{2,18},{4,20},{6,22},{8,24},{10,26},{12,28},{14,30},{16,0},... | collective-permute-start | bytes 1769480 | tf_op jit(solution)/shard_map/ppermute | solution.py:35
  68.4 69.6 %collective-permute-start.10 = (bf16[2,128,2048]{2,1,0:T(8,128)(2,1)}, bf16[2,128,2048]{2,1,0:T(8,128)(2,1)}, u32[]{:S(2)}, u32[]{:S(2)}) collective-permute-start(bf16[2,128,2048]{2,1,0:T(8,128)(2,1)} %param.15), channel_id=1, source_target_pairs={{0,1},{1,0},{2,3},{3,2},{4,5},{5,4},{6,7},{7,6},{8,9},{9,8},{10,11... | collective-permute-start | bytes 3145736 | tf_op jit(solution)/shard_map/ppermute | solution.py:35
  267.3 48.0 %collective-permute-start.12 = (bf16[4,2,128,1024]{3,2,1,0:T(8,128)(2,1)}, bf16[4,2,128,1024]{3,2,1,0:T(8,128)(2,1)}, u32[]{:S(2)}, u32[]{:S(2)}) collective-permute-start(bf16[4,2,128,1024]{3,2,1,0:T(8,128)(2,1)} %shard_map.234), channel_id=1, source_target_pairs={{0,4},{2,6},{4,0},{6,2},{8,12},{10,14},{12,8},{14,10},{16,20},{18,... | collective-permute-start | bytes 6291464 | tf_op jit(solution)/shard_map/ppermute | solution.py:35
  332.6 38.9 %collective-permute-start.14 = (bf16[4,2,128,512]{3,2,1,0:T(8,128)(2,1)S(1)}, bf16[4,2,128,512]{3,2,1,0:T(8,128)(2,1)S(1)}, u32[]{:S(2)}, u32[]{:S(2)}) collective-permute-start(bf16[4,2,128,512]{3,2,1,0:T(8,128)(2,1)S(1)} %get-tuple-element.268), channel_id=1, source_target_pairs={{0,4},{2,6},{4,0},{6,2},{8,12},{10,14},{12,8},{14,10},{16,20},{18,... | collective-permute-start | bytes 3145736 | tf_op jit(solution)/shard_map/ppermute | solution.py:35
  333.1 36.0 %collective-permute-start.15 = (bf16[2,128,1024]{2,1,0:T(8,128)(2,1)}, bf16[2,128,1024]{2,1,0:T(8,128)(2,1)S(1)}, u32[]{:S(2)}, u32[]{:S(2)}) collective-permute-start(bf16[2,128,1024]{2,1,0:T(8,128)(2,1)} %get-tuple-element.270), channel_id=1, source_target_pairs={{0,8},{2,10},{4,12},{6,14},{8,16},{10,18},{12,20},{14,22},{16,24},... | collective-permute-start | bytes 1572872 | tf_op jit(solution)/shard_map/ppermute | solution.py:702
  333.3 38.2 %collective-permute-start.16 = (bf16[2,128,1024]{2,1,0:T(8,128)(2,1)}, bf16[2,128,1024]{2,1,0:T(8,128)(2,1)S(1)}, u32[]{:S(2)}, u32[]{:S(2)}) collective-permute-start(bf16[2,128,1024]{2,1,0:T(8,128)(2,1)} %get-tuple-element.271), channel_id=1, source_target_pairs={{0,16},{2,18},{4,20},{6,22},{8,24},{10,26},{12,28},{14,30},{16,0},... | collective-permute-start | bytes 1572872 | tf_op jit(solution)/shard_map/ppermute | solution.py:702
  334.8 36.7 %collective-permute-start.17 = (bf16[2,128,1024]{2,1,0:T(8,128)(2,1)}, bf16[2,128,1024]{2,1,0:T(8,128)(2,1)S(1)}, u32[]{:S(2)}, u32[]{:S(2)}) collective-permute-start(bf16[2,128,1024]{2,1,0:T(8,128)(2,1)} %get-tuple-element.272), channel_id=1, source_target_pairs={{0,24},{2,26},{4,28},{6,30},{8,0},{10,2},{12,4},{14,6},{16,8},{18,... | collective-permute-start | bytes 1572872 | tf_op jit(solution)/shard_map/ppermute | solution.py:702
  397.9 36.7 %collective-permute-start.20 = (bf16[4,2,128,512]{3,2,1,0:T(8,128)(2,1)S(1)}, bf16[4,2,128,512]{3,2,1,0:T(8,128)(2,1)S(1)}, u32[]{:S(2)}, u32[]{:S(2)}) collective-permute-start(bf16[4,2,128,512]{3,2,1,0:T(8,128)(2,1)S(1)} %get-tuple-element.299), channel_id=1, source_target_pairs={{0,4},{2,6},{4,0},{6,2},{8,12},{10,14},{12,8},{14,10},{16,20},{18,... | collective-permute-start | bytes 3145736 | tf_op jit(solution)/shard_map/ppermute | solution.py:35
  399.5 33.0 %collective-permute-start.21 = (bf16[2,128,512]{2,1,0:T(8,128)(2,1)S(1)}, bf16[2,128,512]{2,1,0:T(8,128)(2,1)S(1)}, u32[]{:S(2)}, u32[]{:S(2)}) collective-permute-start(bf16[2,128,512]{2,1,0:T(8,128)(2,1)S(1)} %get-tuple-element.301), channel_id=1, source_target_pairs={{0,8},{2,10},{4,12},{6,14},{8,16},{10,18},{12,20},{14,22},{16,24},... | collective-permute-start | bytes 786440 | tf_op jit(solution)/shard_map/ppermute | solution.py:702
  410.1 23.2 %collective-permute-start.22 = (bf16[2,128,512]{2,1,0:T(8,128)(2,1)S(1)}, bf16[2,128,512]{2,1,0:T(8,128)(2,1)S(1)}, u32[]{:S(2)}, u32[]{:S(2)}) collective-permute-start(bf16[2,128,512]{2,1,0:T(8,128)(2,1)S(1)} %get-tuple-element.302), channel_id=1, source_target_pairs={{0,16},{2,18},{4,20},{6,22},{8,24},{10,26},{12,28},{14,30},{16,0},... | collective-permute-start | bytes 786440 | tf_op jit(solution)/shard_map/ppermute | solution.py:702
  410.9 23.1 %collective-permute-start.23 = (bf16[2,128,512]{2,1,0:T(8,128)(2,1)S(1)}, bf16[2,128,512]{2,1,0:T(8,128)(2,1)S(1)}, u32[]{:S(2)}, u32[]{:S(2)}) collective-permute-start(bf16[2,128,512]{2,1,0:T(8,128)(2,1)S(1)} %get-tuple-element.303), channel_id=1, source_target_pairs={{0,24},{2,26},{4,28},{6,30},{8,0},{10,2},{12,4},{14,6},{16,8},{18,... | collective-permute-start | bytes 786440 | tf_op jit(solution)/shard_map/ppermute | solution.py:702
  463.0 42.0 %collective-permute-start.26 = (bf16[4,1,128,1024]{3,2,1,0:T(8,128)(2,1)}, bf16[4,1,128,1024]{3,2,1,0:T(8,128)(2,1)}, u32[]{:S(2)}, u32[]{:S(2)}) collective-permute-start(bf16[4,1,128,1024]{3,2,1,0:T(8,128)(2,1)} %get-tuple-element.328), channel_id=1, source_target_pairs={{0,4},{2,6},{4,0},{6,2},{8,12},{10,14},{12,8},{14,10},{16,20},{18,... | collective-permute-start | bytes 3145736 | tf_op jit(solution)/shard_map/ppermute | solution.py:35
  478.4 42.0 %collective-permute-start.38 = (bf16[2,128,2048]{2,1,0:T(8,128)(2,1)}, bf16[2,128,2048]{2,1,0:T(8,128)(2,1)}, u32[]{:S(2)}, u32[]{:S(2)}) collective-permute-start(bf16[2,128,2048]{2,1,0:T(8,128)(2,1)} %get-tuple-element.362), channel_id=1, source_target_pairs={{0,1},{1,0},{2,3},{3,2},{4,5},{5,4},{6,7},{7,6},{8,9},{9,8},{10,11... | collective-permute-start | bytes 3145736 | tf_op jit(solution)/shard_map/ppermute | solution.py:35
  480.3 23.9 %collective-permute-start.27 = (bf16[4,1,128,288]{3,2,1,0:T(8,128)(2,1)}, bf16[4,1,128,288]{3,2,1,0:T(8,128)(2,1)S(1)}, u32[]{:S(2)}, u32[]{:S(2)}) collective-permute-start(bf16[4,1,128,288]{3,2,1,0:T(8,128)(2,1)} %get-tuple-element.329), channel_id=1, source_target_pairs={{0,4},{2,6},{4,0},{6,2},{8,12},{10,14},{12,8},{14,10},{16,20},{18,... | collective-permute-start | bytes 884744 | tf_op jit(solution)/shard_map/ppermute | solution.py:35
  519.0 31.6 %collective-permute-start.32 = (bf16[1,128,1024]{2,1,0:T(8,128)(2,1)S(1)}, bf16[1,128,1024]{2,1,0:T(8,128)(2,1)S(1)}, u32[]{:S(2)}, u32[]{:S(2)}) collective-permute-start(bf16[1,128,1024]{2,1,0:T(8,128)(2,1)S(1)} %get-tuple-element.350), channel_id=1, source_target_pairs={{0,8},{2,10},{4,12},{6,14},{8,16},{10,18},{12,20},{14,22},{16,24},... | collective-permute-start | bytes 786440 | tf_op jit(solution)/shard_map/ppermute | solution.py:702
  519.0 31.5 %collective-permute-start.33 = (bf16[1,128,1024]{2,1,0:T(8,128)(2,1)S(1)}, bf16[1,128,1024]{2,1,0:T(8,128)(2,1)S(1)}, u32[]{:S(2)}, u32[]{:S(2)}) collective-permute-start(bf16[1,128,1024]{2,1,0:T(8,128)(2,1)S(1)} %get-tuple-element.351), channel_id=1, source_target_pairs={{0,16},{2,18},{4,20},{6,22},{8,24},{10,26},{12,28},{14,30},{16,0},... | collective-permute-start | bytes 786440 | tf_op jit(solution)/shard_map/ppermute | solution.py:702
  520.4 30.2 %collective-permute-start.31 = (bf16[4,1,128,1024]{3,2,1,0:T(8,128)(2,1)S(1)}, bf16[4,1,128,1024]{3,2,1,0:T(8,128)(2,1)S(1)}, u32[]{:S(2)}, u32[]{:S(2)}) collective-permute-start(bf16[4,1,128,1024]{3,2,1,0:T(8,128)(2,1)S(1)} %copy-done.71), channel_id=1, source_target_pairs={{0,4},{2,6},{4,0},{6,2},{8,12},{10,14},{12,8},{14,10},{16,20},{18,... | collective-permute-start | bytes 3145736 | tf_op jit(solution)/shard_map/ppermute | solution.py:35
  523.6 27.0 %collective-permute-start.34 = (bf16[1,128,1024]{2,1,0:T(8,128)(2,1)S(1)}, bf16[1,128,1024]{2,1,0:T(8,128)(2,1)S(1)}, u32[]{:S(2)}, u32[]{:S(2)}) collective-permute-start(bf16[1,128,1024]{2,1,0:T(8,128)(2,1)S(1)} %get-tuple-element.352), channel_id=1, source_target_pairs={{0,24},{2,26},{4,28},{6,30},{8,0},{10,2},{12,4},{14,6},{16,8},{18,... | collective-permute-start | bytes 786440 | tf_op jit(solution)/shard_map/ppermute | solution.py:702
  560.2 27.2 %collective-permute-start.46 = (bf16[1,128,1024]{2,1,0:T(8,128)(2,1)}, bf16[1,128,1024]{2,1,0:T(8,128)(2,1)}, u32[]{:S(2)}, u32[]{:S(2)}) collective-permute-start(bf16[1,128,1024]{2,1,0:T(8,128)(2,1)} %get-tuple-element.381), channel_id=1, source_target_pairs={{0,8},{2,10},{4,12},{6,14},{8,16},{10,18},{12,20},{14,22},{16,24},... | collective-permute-start | bytes 786440 | tf_op jit(solution)/shard_map/ppermute | solution.py:702
  560.2 27.2 %collective-permute-start.47 = (bf16[1,128,1024]{2,1,0:T(8,128)(2,1)}, bf16[1,128,1024]{2,1,0:T(8,128)(2,1)}, u32[]{:S(2)}, u32[]{:S(2)}) collective-permute-start(bf16[1,128,1024]{2,1,0:T(8,128)(2,1)} %get-tuple-element.382), channel_id=1, source_target_pairs={{0,16},{2,18},{4,20},{6,22},{8,24},{10,26},{12,28},{14,30},{16,0},... | collective-permute-start | bytes 786440 | tf_op jit(solution)/shard_map/ppermute | solution.py:702
  (136 other events, 1242.1 us)
Sparse Core Ops, SparseCore 0:
  10.2 104.4 all-gather.8
  116.9 72.9 all-gather.4
  192.1 73.2 all-gather.6

commit v3 on v2

--- a/solution.py
+++ b/solution.py
@@ -45,10 +45,10 @@
     return jnp.concatenate([low, high], axis=axis)
 
 
-def tensor_sum(values):
+def tensor_sum(values, kind=f32):
     if lax.axis_size("tensor") != 2:
         return lax.psum(values, "tensor")
-    return values + swapped(values, "tensor", 1)
+    return values + swapped(values.astype(kind), "tensor", 1).astype(f32)
 
 
 def moved(values, offset):
@@ -263,7 +263,6 @@
     states = decay_log.shape[0]
     rows = chunk * states
     rank = rank_low.shape[2]
-    inside = start % (weights.shape[2] // width)
 
     def whole(r, c):
         return pl.BlockSpec((None, r, c), lambda j, m: (m, 0, 0))
@@ -289,7 +288,7 @@
         grid=(blocks, micro),
         in_specs=[later(tok)] * 2
         + [whole(tok, dim)] * 2
-        + [pl.BlockSpec((None, dim, width), lambda j, m, k=k: (k, 0, j + inside)) for k in range(2)]
+        + [pl.BlockSpec((None, dim, width), lambda j, m, k=k, at=at: (k, 0, j + at)) for _, k, at in weights]
         + [whole(tok, rank), param(rank, start), whole(tok, mask.shape[2])]
         + [whole(tok * states, 128)] * 2
         + [whole(tok, rows)] * 2
@@ -308,7 +307,7 @@
             dimension_semantics=("arbitrary", "arbitrary"), vmem_limit_bytes=58 * 2**20
         ),
         cost_estimate=small_cost,
-    )(pre, act, normed, cot, weights, weights, rank_low, step_weight, mask, *tables, skip[None], decay_log)
+    )(pre, act, normed, cot, *[v for v, _, _ in weights], rank_low, step_weight, mask, *tables, skip[None], decay_log)
 
 
 def halves(values):
@@ -398,22 +397,31 @@
     return total
 
 
-def inner_kernel(normed_ref, weight_ref, mask_ref, conv_ref, bias_ref, select_ref, inner_ref, act_ref, selected_ref):
-    inner = jnp.dot(normed_ref[...], weight_ref[...], preferred_element_type=f32)
-    inner_ref[...] = inner
-    convolved = convolve(inner, mask_ref, conv_ref, bias_ref)
+def inner_kernel(bounds, normed_ref, *refs):
+    *weight_refs, mask_ref, conv_ref, bias_ref, select_ref, inner_ref, act_ref, selected_ref = refs
+    tile = pl.program_id(0)
+    for ref, low, high in zip(weight_refs, bounds[:-1], bounds[1:]):
+
+        @pl.when(jnp.logical_and(tile >= low, tile < high))
+        def _(ref=ref):
+            inner_ref[...] = jnp.dot(normed_ref[...], ref[...], preferred_element_type=f32)
+
+    convolved = convolve(inner_ref[...], mask_ref, conv_ref, bias_ref)
     act = (convolved * jax.nn.sigmoid(convolved)).astype(bf16)
     act_ref[...] = act
     part = jnp.dot(act, select_ref[...], preferred_element_type=f32)
-    selected_ref[...] = jnp.where(pl.program_id(0) == 0, part, selected_ref[...] + part)
-
-
-def inner_forward(normed, weight, mask, conv_w, conv_b, select):
+    selected_ref[...] = jnp.where(tile == 0, part, selected_ref[...] + part)
+
+
+def inner_forward(normed, weights, mask, conv_w, conv_b, select):
     tokens, dim = normed.shape
-    channels = weight.shape[1]
-    width = min(256, channels)
+    channels = sum(v.shape[1] for v in weights)
+    width = min([256] + [v.shape[1] for v in weights])
     taps = conv_w.shape[0]
     picked = select.shape[1]
+    bounds = [0]
+    for v in weights:
+        bounds.append(bounds[-1] + v.shape[1] // width)
 
     def fixed(r, c):
         return pl.BlockSpec((r, c), lambda j: (0, 0))
@@ -421,12 +429,15 @@
     def part(r):
         return pl.BlockSpec((r, width), lambda j: (0, j))
 
+    def held(low, high):
+        return pl.BlockSpec((dim, width), lambda j: (0, jnp.clip(j - low, 0, high - low - 1)))
+
     return pl.pallas_call(
-        inner_kernel,
+        functools.partial(inner_kernel, tuple(bounds)),
         grid=(channels // width,),
-        in_specs=[
-            fixed(tokens, dim),
-            part(dim),
+        in_specs=[fixed(tokens, dim)]
+        + [held(low, high) for low, high in zip(bounds[:-1], bounds[1:])]
+        + [
             fixed(tokens, mask.shape[1]),
             part(taps),
             part(1),
@@ -440,7 +451,39 @@
         ],
         compiler_params=pltpu.CompilerParams(dimension_semantics=("arbitrary",), vmem_limit_bytes=48 * 2**20),
         cost_estimate=small_cost,
-    )(normed, weight, mask, conv_w, conv_b[None], select)
+    )(normed, *weights, mask, conv_w, conv_b[None], select)
+
+
+def assemble_kernel(outer, places_ref, *refs):
+    *groups, out_ref = refs
+    for i, ref in enumerate(groups):
+
+        @pl.when(lax.div(pl.program_id(0), outer) == i)
+        def _(ref=ref):
+            out_ref[...] = ref[...]
+
+
+def assemble(groups, places):
+    count = places.shape[0]
+    outer = count // len(groups)
+    rows, width = groups[0].shape
+    own = rows // outer
+
+    def held(i):
+        return pl.BlockSpec((own, width), lambda r, _: (jnp.clip(r - i * outer, 0, outer - 1), 0))
+
+    return pl.pallas_call(
+        functools.partial(assemble_kernel, outer),
+        grid_spec=pltpu.PrefetchScalarGridSpec(
+            num_scalar_prefetch=1,
+            grid=(count,),
+            in_specs=[held(i) for i in range(len(groups))],
+            out_specs=pl.BlockSpec((own, width), lambda r, where: (where[r], 0)),
+        ),
+        out_shape=jax.ShapeDtypeStruct((rows * len(groups), width), groups[0].dtype),
+        compiler_params=pltpu.CompilerParams(dimension_semantics=("arbitrary",), vmem_limit_bytes=48 * 2**20),
+        cost_estimate=small_cost,
+    )(places, *groups)
 
 
 def inner_back_kernel(bounds, places_ref, *refs):
@@ -470,9 +513,7 @@
         dinner = dinner + conv_ref[tap : tap + 1, :] * ahead(masked, back)
     low = dinner.astype(bf16)
     dinner_ref[...] = low
-    select_grad_ref[...] = lax.dot_general(
-        dsel, act_ref[...], first_dims, preferred_element_type=f32
-    ).astype(bf16)
+    select_grad_ref[...] = lax.dot_general(dsel, act_ref[...], first_dims, preferred_element_type=f32)
     outer, own = kept_ref.shape[1], kept_ref.shape[3]
     for core, out_ref in ((1, sent_ref), (0, kept_ref)):
         for cross in range(2):
@@ -528,7 +569,7 @@
         out_shape=[
             jax.ShapeDtypeStruct((tokens, channels), bf16),
             jax.ShapeDtypeStruct((8, channels), f32),
-            jax.ShapeDtypeStruct((picked, channels), bf16),
+            jax.ShapeDtypeStruct((picked, channels), f32),
         ]
         + [jax.ShapeDtypeStruct((2, outer, 1, own, channels), bf16)] * 2,
         compiler_params=pltpu.CompilerParams(dimension_semantics=("arbitrary",), vmem_limit_bytes=52 * 2**20),
@@ -536,63 +577,54 @@
     )(places, *dacts, dsel, select, inner, act, mask, conv_w, conv_b[None], left)
 
 
-def project_kernel(micro, count, where_ref, *refs):
-    lefts, rights = refs[:count], refs[count : 2 * count]
-    here_ref, away_ref, total_s = refs[2 * count :]
+def project_kernel(count, where_ref, *refs):
+    lefts, rights, out_ref = refs[:count], refs[count:-1], refs[-1]
     total = None
     for left, right in zip(lefts, rights):
-        part = lax.dot_general(left[...], right[...], last_dims, preferred_element_type=f32)
+        rows = jnp.concatenate([left[m] for m in range(left.shape[0])], axis=0)
+        part = lax.dot_general(rows, right[...], last_dims, preferred_element_type=f32)
         total = part if total is None else total + part
-    total_s[...] = total
-    group = total.shape[0] // micro
-    rows = here_ref.shape[1]
-    here = where_ref[0] * rows
-    for m in range(micro):
-        here_ref[m] = total_s[pl.ds(pl.multiple_of(m * group + here, rows), rows), :]
-        away_ref[m] = total_s[pl.ds(pl.multiple_of(m * group + (group - rows) - here, rows), rows), :].astype(bf16)
-
-
-def project(lefts, rights, places, micro, shard_rows):
-    tokens = lefts[0].shape[0]
-    dim = rights[0].shape[1]
+    rows = out_ref.shape[1]
+    for m in range(out_ref.shape[0]):
+        out_ref[m] = total[m * rows : (m + 1) * rows].astype(out_ref.dtype)
+
+
+def project(terms, where, shard_rows, kind):
+    micro = terms[0][0].shape[0]
+    dim = terms[0][3].shape[1]
     width = min(256, dim)
-    where = lax.axis_index("tensor").astype(jnp.int32)[None]
 
     def column(plane, at, wide):
         return pl.BlockSpec((None, width, wide), lambda i, _: (plane, i, at))
 
+    def left_rows(at, wide):
+        return pl.BlockSpec((micro, shard_rows, wide), lambda i, who: (0, who[0], at))
+
     return pl.pallas_call(
-        functools.partial(project_kernel, micro, len(lefts)),
+        functools.partial(project_kernel, len(terms)),
         grid_spec=pltpu.PrefetchScalarGridSpec(
             num_scalar_prefetch=1,
             grid=(dim // width,),
-            in_specs=[pl.BlockSpec(v.shape, lambda i, _: (0, 0)) for v in lefts]
-            + [column(*at, v.shape[1]) for at, v in zip(places, lefts)],
-            out_specs=[pl.BlockSpec((micro, shard_rows, width), lambda i, _: (0, 0, i))] * 2,
-            scratch_shapes=[pltpu.VMEM((tokens, width), f32)],
+            in_specs=[left_rows(at, wide) for _, at, wide, _, _, _ in terms]
+            + [column(plane, at, wide) for _, _, wide, _, plane, at in terms],
+            out_specs=pl.BlockSpec((micro, shard_rows, width), lambda i, _: (0, 0, i)),
         ),
-        out_shape=[
-            jax.ShapeDtypeStruct((micro, shard_rows, dim), f32),
-            jax.ShapeDtypeStruct((micro, shard_rows, dim), bf16),
-        ],
+        out_shape=jax.ShapeDtypeStruct((micro, shard_rows, dim), kind),
         compiler_params=pltpu.CompilerParams(dimension_semantics=("arbitrary",), vmem_limit_bytes=48 * 2**20),
         cost_estimate=small_cost,
-    )(where, *lefts, *rights)
-
-
-def spread_sum(lefts, rights, places, micro, shard_rows):
-    if lax.axis_size("tensor") == 2:
-        here, away = project(lefts, rights, places, micro, shard_rows)
-        return here, swapped(away, "tensor", 1)
+    )(where, *[t[0] for t in terms], *[t[3] for t in terms])
+
+
+def project_all(terms):
     total = 0.0
-    for left, right, (plane, at) in zip(lefts, rights, places):
-        wide = left.shape[1]
-        total = total + lax.dot_general(
-            left, right[plane, :, at * wide : (at + 1) * wide], last_dims, preferred_element_type=f32
+    for left, left_at, wide, right, plane, at in terms:
+        total = total + jnp.einsum(
+            "mgc,dc->mgd",
+            left[..., left_at * wide : (left_at + 1) * wide],
+            right[plane, :, at * wide : (at + 1) * wide],
+            preferred_element_type=f32,
         )
-    total = total.reshape(micro, -1, total.shape[1])
-    away = lax.psum_scatter(total.astype(bf16), "tensor", scatter_dimension=1, tiled=True)
-    return jnp.zeros(away.shape, f32), away
+    return lax.psum_scatter(total.astype(bf16), "tensor", scatter_dimension=1, tiled=True)
 
 
 def parts_kernel(kinds, outer, places_ref, *refs):
@@ -644,46 +676,58 @@
 
 
 def sums_kernel(crosses, alongs, outer, *refs):
-    given = iter(refs[: 2 * crosses + 3 * alongs])
-    outs = iter(refs[2 * crosses + 3 * alongs :])
-    for _ in range(crosses):
-        kept, got = next(given), next(given)
-        next(outs)[...] = (kept[...].astype(f32) + got[...].astype(f32)).astype(bf16)
-    for _ in range(alongs):
-        kept, got, across = next(given), next(given), next(given)
-        next(outs)[...] = kept[0].astype(f32) + got[0].astype(f32) + across[0].astype(f32)
-        for j in range(1, outer):
-            next(outs)[...] = (kept[j].astype(f32) + got[j].astype(f32) + across[j].astype(f32)).astype(bf16)
+    ins = 2 * sum(crosses) + 3 * sum(alongs)
+    given, outs = iter(refs[:ins]), iter(refs[ins:])
+    for sources in crosses:
+        out, at = next(outs), 0
+        for _ in range(sources):
+            kept, got = next(given), next(given)
+            total = (kept[...].astype(f32) + got[...].astype(f32)).astype(bf16)
+            out[..., at : at + total.shape[-1]] = total
+            at += total.shape[-1]
+    for sources in alongs:
+        out, at = [next(outs) for _ in range(outer)], 0
+        for _ in range(sources):
+            kept, got, across = next(given), next(given), next(given)
+            wide = kept.shape[-1]
+            for j in range(outer):
+                total = kept[j].astype(f32) + got[j].astype(f32) + across[j].astype(f32)
+                out[j][..., at : at + wide] = total.astype(out[j].dtype)
+            at += wide
 
 
 def step_sums(crosses, alongs):
     cuts = 4
     in_specs, out_specs, out_shape, given = [], [], [], []
-    outer = (crosses + alongs)[0][0].shape[1]
+    outer = (crosses + alongs)[0][0][0].shape[1]
 
     def taken(shape, first, at, wide):
         block = (None,) + shape[1:-2] + (shape[-2] // cuts, wide)
         return pl.BlockSpec(block, lambda i: (first,) + (0,) * (len(shape) - 3) + (i, at))
 
-    def plain(shape):
-        return pl.BlockSpec(shape[:-2] + (shape[-2] // cuts, shape[-1]), lambda i: (0,) * (len(shape) - 2) + (i, 0))
-
-    for kept, got, (at, wide) in crosses:
-        shape = kept.shape
-        in_specs += [taken(shape, 1, at, wide)] * 2
-        given += [kept, got]
-        out = shape[1:-1] + (wide,)
+    def plain(shape, at=0):
+        return pl.BlockSpec(
+            shape[:-2] + (shape[-2] // cuts, shape[-1]), lambda i: (0,) * (len(shape) - 2) + (i, at)
+        )
+
+    for sources in crosses:
+        for kept, got, at, wide in sources:
+            in_specs += [taken(kept.shape, 1, at, wide)] * 2
+            given += [kept, got]
+        out = sources[0][0].shape[1:-1] + (sum(v[3] for v in sources),)
         out_specs.append(plain(out))
         out_shape.append(jax.ShapeDtypeStruct(out, bf16))
-    for kept, got, across, (at, wide) in alongs:
-        shape = kept.shape
-        in_specs += [taken(shape, 0, at, wide)] * 2 + [plain(across.shape)]
-        given += [kept, got, across]
-        out = shape[2:-1] + (wide,)
+    for sources in alongs:
+        for kept, got, at, wide, across, across_at in sources:
+            in_specs += [taken(kept.shape, 0, at, wide)] * 2 + [plain(across.shape[:-1] + (wide,), across_at)]
+            given += [kept, got, across]
+        out = sources[0][0].shape[2:-1] + (sum(v[3] for v in sources),)
         out_specs += [plain(out)] * outer
         out_shape += [jax.ShapeDtypeStruct(out, f32 if j == 0 else bf16) for j in range(outer)]
     outs = pl.pallas_call(
-        functools.partial(sums_kernel, len(crosses), len(alongs), outer),
+        functools.partial(
+            sums_kernel, tuple(len(v) for v in crosses), tuple(len(v) for v in alongs), outer
+        ),
         grid=(cuts,),
         in_specs=in_specs,
         out_specs=out_specs,
@@ -704,22 +748,20 @@
     ]
 
 
-def final_kernel(kinds, *refs):
-    *terms, out_ref = refs[: len(refs) - kinds + 1]
-    outs = (out_ref,) + refs[len(refs) - kinds + 1 :]
+def final_kernel(turned, *refs):
+    terms, outs = refs[: len(refs) - len(turned)], refs[len(refs) - len(turned) :]
     total = terms[0][...]
     for ref in terms[1:]:
         total = total + ref[...].astype(f32)
-    outs[0][...] = total[0]
-    if kinds == 2:
-        outs[1][...] = total[1].T
-
-
-def final_sum(terms):
+    for i, turn in enumerate(turned):
+        outs[i][...] = total[i].T if turn else total[i]
+
+
+def final_sum(terms, turned):
     kinds, own, width = terms[0].shape
     return pl.pallas_call(
-        functools.partial(final_kernel, kinds),
-        out_shape=[jax.ShapeDtypeStruct((own, width), f32), jax.ShapeDtypeStruct((width, own), f32)][:kinds],
+        functools.partial(final_kernel, turned),
+        out_shape=[jax.ShapeDtypeStruct((width, own) if turn else (own, width), f32) for turn in turned],
         compiler_params=pltpu.CompilerParams(vmem_limit_bytes=48 * 2**20),
         cost_estimate=small_cost,
     )(*terms)
@@ -736,6 +778,37 @@
         values = jnp.concatenate([jnp.where(low, values, other), jnp.where(low, other, values)], axis=0)
         bit *= 2
     return values
+
+
+def finish_kernel(hidden_ref, cot_ref, gain_ref, layer_ref, layer_away_ref, here_ref, away_ref, layer_out, grad_out):
+    hidden = hidden_ref[...]
+    scale = lax.rsqrt(jnp.mean(hidden * hidden, axis=-1, keepdims=True) + epsilon)
+    normal = hidden * scale
+    layer_out[...] = hidden + (layer_ref[...] + layer_away_ref[...].astype(f32))
+    dnormed = here_ref[...] + away_ref[...].astype(f32)
+    dnormal = dnormed * gain_ref[...]
+    middle = jnp.mean(dnormal * normal, axis=-1, keepdims=True)
+    grad_out[...] = cot_ref[...].astype(f32) + scale * (dnormal - normal * middle)
+
+
+def finish(hidden, cotangent, gain, layer_here, layer_away, here, away):
+    micro, rows, dim = hidden.shape
+    total = micro * rows
+    cut = min(64, total)
+
+    def part():
+        return pl.BlockSpec((cut, dim), lambda i: (i, 0))
+
+    layer, grad = pl.pallas_call(
+        finish_kernel,
+        grid=(total // cut,),
+        in_specs=[part(), part(), pl.BlockSpec((1, dim), lambda i: (0, 0))] + [part()] * 4,
+        out_specs=[part(), part()],
+        out_shape=[jax.ShapeDtypeStruct((total, dim), f32)] * 2,
+        compiler_params=pltpu.CompilerParams(dimension_semantics=("arbitrary",), vmem_limit_bytes=48 * 2**20),
+        cost_estimate=small_cost,
+    )(*[v.reshape(-1, dim) for v in (hidden, cotangent, gain, layer_here, layer_away, here, away)])
+    return layer.reshape(hidden.shape), grad.reshape(hidden.shape)
 
 
 def on_device(
@@ -770,11 +843,19 @@
     ids = jnp.arange(count, dtype=jnp.int32)
     place, cross, core = here // 4, (here // 2) % 2, here % 2
     places = ((place + ids % outer) % outer) * 4 + (cross ^ (ids // outer) % 2) * 2 + (core ^ ids // (2 * outer))
-    places = places.astype(jnp.int32)
+    ranks = ((core ^ ids % 2) * 2 + (cross ^ (ids // 2) % 2)) * outer + (ids // 4 - place) % outer
+    places, ranks = places.astype(jnp.int32), ranks.astype(jnp.int32)
+
+    w_inner = lax.all_gather(input_weight[:, 0], "dp", axis=0, tiled=True)
+    out_shard = output_weight.T
+    weights = []
+    for low, high in ((0, half), (half, channels)):
+        both = jnp.stack([input_weight[:, 1, low:high], out_shard[:, low:high]])
+        both = lax.all_gather(both, "dp", axis=1, tiled=True)
+        weights += [((both, 0, at), (both, 1, at)) for at in range(1 if low == 0 else 2)]
 
     pieces = [norm_gain, conv_weight, conv_bias, step_bias, decay_log, skip_gain]
     packed = doubled(jnp.concatenate([v.reshape(-1) for v in pieces]))
-    picked = select_weight.shape[1]
     narrow, packed = join(jnp.concatenate([select_weight.T, step_weight.reshape(-1, own)], axis=0), packed)
     full = []
     at = 0
@@ -787,17 +868,14 @@
             part = part.reshape(-1)
         full.append(part)
     gain_full, conv_w, conv_b, step_b, decay_lg, skip_g = full
-    narrow = doubled(narrow)
+    picked = select_weight.shape[1]
+    narrow = jnp.stack([narrow] + [moved(narrow, j) for j in range(1, outer)])
+    narrow = jnp.stack([narrow, swapped(narrow, "dp", 2)])
+    narrow = jnp.stack([narrow, swapped(narrow, "dp", 1)]).reshape((count,) + narrow.shape[2:])
+    narrow = jnp.take(narrow, ranks, axis=0)
     w_sel = narrow[:, :picked].transpose(0, 2, 1).reshape(channels, picked)
     w_step = narrow[:, picked:].reshape(-1, channels)
-
-    w_inner = lax.all_gather(input_weight[:, 0], "dp", axis=0, tiled=True)
-    out_shard = output_weight.T
-    weights = []
-    for number in range(2):
-        cut = slice(number * half, (number + 1) * half)
-        both = jnp.stack([input_weight[:, 1, cut], out_shard[:, cut]])
-        weights.append(lax.all_gather(both, "dp", axis=1, tiled=True))
+    rank_dim = w_step.shape[0]
 
     inverse_rms = lax.rsqrt(jnp.mean(hidden * hidden, axis=-1, keepdims=True) + epsilon)
     normal_rows = hidden * inverse_rms
@@ -812,7 +890,7 @@
     def grouped(v):
         return v.reshape(micro, group_tok, v.shape[-1])
 
-    inner, act, selected = inner_forward(normed, w_inner, flat_mask, conv_w, conv_b, w_sel)
+    inner, act, selected = inner_forward(normed, [w_inner], flat_mask, conv_w, conv_b, w_sel)
     selected = tensor_sum(selected)
     lefts = (normed.T, cot_full.T)
     pre_step, rank_low, *tables = middle(selected, w_step, step_b, states)
@@ -820,148 +898,165 @@
     rank_rows = grouped(rank_low)
 
     gated, dgate, dact, step_grads, sums, rank_grads, dins, douts = [[] for _ in range(8)]
-    rows_now = (grouped(normed), grouped(cot_full))
     kept, got, across, total = {}, {}, {}, {}
-    stages = ((0, 2), (2, 1), (3, 1))
-
-    def whole(piece):
-        return kept[piece], got[piece], (0, kept[piece].shape[-1])
-
-    def whole_across(piece):
-        return kept[piece], got[piece], across[piece], (0, kept[piece].shape[-1])
-
-    for number, (start, blocks) in enumerate(stages):
-        cross, along = (), ()
-        if number > 0:
-            cross, along = step_sums(
-                [whole(number - 1)], [whole_across(number - 2)] if number > 1 else []
-            )
-        rows_now, cross, along = join(rows_now, cross, along)
-        cross = [swapped(v, "dp", 2) for v in cross]
-        along = [along_moves(v) for v in along]
-        results = scan_both_ways(
-            start,
-            blocks,
+    rows = (grouped(normed), grouped(cot_full))
+
+    def scanned(number, skip_now):
+        return scan_both_ways(
+            (0, 2, 3)[number],
+            (2, 1, 1)[number],
             quarter,
             grouped(pre_step),
             grouped(act),
-            *rows_now,
-            weights[start // 2],
+            *rows,
+            weights[number],
             rank_rows,
             w_step,
             mask,
             tables,
-            skip_g,
+            skip_now,
             decay_lg,
         )
-        results, cross, along = join(results, cross, along)
-        if number > 0:
-            across[number - 1] = cross[0]
-        if number > 1:
-            total[number - 2] = along[0]
+
+    def hold(results):
         for held, v in zip((gated, dgate, dact), results[:3]):
             held.append(v.reshape(tokens, -1))
         for held, v in zip((step_grads, sums, rank_grads, dins, douts), results[3:]):
             held.append(v)
-        if number == 2:
-            break
-        rights = (dgate[number], gated[number])
-        sent = grad_parts(places, False, lefts, rights)
-        sent, lefts = join(sent, lefts)
-        got[number] = swapped(sent, "dp", 1)
-        kept[number] = grad_parts(places, True, lefts, rights)
-        rows_now, kept[number] = join(rows_now, kept[number])
-
+
+    def source(piece, at=0, wide=None):
+        return kept[piece], got[piece], at, wide or kept[piece].shape[-1]
+
+    hold(scanned(0, skip_g))
+    places_now = places
+    for piece, left, right in (("gate", lefts[0], dgate[0]), ("out", lefts[1], gated[0])):
+        sent = grad_parts(places_now, False, (left,), (right,))
+        sent, places_now = join(sent, places_now)
+        got[piece] = swapped(sent, "dp", 1)
+        kept[piece] = grad_parts(places_now, True, (left,), (right,))
+    cross, _ = step_sums(
+        [[source("gate"), source("out", 0, quarter)], [source("out", 1, quarter)]], []
+    )
+    skip_now, cross = join(skip_g, cross)
+    across["zero"], across["rest"] = [swapped(v, "dp", 2) for v in cross]
+
+    results = scanned(1, skip_now)
+    results, across["zero"] = join(results, across["zero"])
+    hold(results)
+    sent = grad_parts(places_now, False, lefts, (dgate[1], gated[1]))
+    sent, places_now = join(sent, places_now)
+    got["second"] = swapped(sent, "dp", 1)
+    kept["second"] = grad_parts(places_now, True, lefts, (dgate[1], gated[1]))
+    kept["second"], across["rest"], got["second"] = join(kept["second"], across["rest"], got["second"])
+    cross, along = step_sums([[source("second")]], [[source("gate") + (across["zero"], 0)]])
+    skip_now, cross, along = join(skip_now, cross, along)
+    total["gate"] = along_moves(along[0])
+    across["second"] = swapped(cross[0], "dp", 2)
+
+    results = scanned(2, skip_now)
+    results, total["gate"], across["second"] = join(results, total["gate"], across["second"])
+    hold(results)
     rank_grad = sum(v[j] for v in rank_grads for j in range(v.shape[0]))
     select_terms = jnp.concatenate([rank_grad, unblocked(dins, states), unblocked(douts, states)], axis=2)
-    select_terms = select_terms.reshape(tokens, -1)
-    select_terms, gated[2], dgate[2], lefts = join(select_terms, gated[2], dgate[2], lefts)
-    select_terms = tensor_sum(select_terms)
-    sent = grad_parts(places, False, lefts, (dgate[2], gated[2]))
-    sent, lefts = join(sent, lefts)
-    got[2] = swapped(sent, "dp", 1)
-    kept[2] = grad_parts(places, True, lefts, (dgate[2], gated[2]))
-    got[2], kept[2], select_terms = join(got[2], kept[2], select_terms)
+    _, along = step_sums(
+        [], [[source("out", 0, quarter) + (across["zero"], 2), source("out", 1, quarter) + (across["rest"], 0)]]
+    )
+    two = lax.axis_size("tensor") == 2
+    where = lax.axis_index("tensor").astype(jnp.int32)[None]
+    select_terms, places_now, along = join(select_terms.reshape(tokens, -1), places_now, along)
+    select_terms = tensor_sum(select_terms, bf16)
+    total["out"] = along_moves(along[0])
+    sent = grad_parts(places_now, False, lefts, (dgate[2], gated[2]))
+    sent, places_now = join(sent, places_now)
+    got["third"] = swapped(sent, "dp", 1)
+    kept["third"] = grad_parts(places_now, True, lefts, (dgate[2], gated[2]))
+    kept["third"], where = join(kept["third"], where)
+    out_terms = [(grouped(v), 0, v.shape[1]) + w[1] for v, w in zip(gated, weights)]
+    layer_away = project(out_terms, 1 - where, shard_rows, bf16) if two else project_all(out_terms)
+    select_terms, kept["third"], got["third"], total["out"], layer_away = join(
+        select_terms, kept["third"], got["third"], total["out"], layer_away
+    )
     select_low = select_terms.astype(bf16)
-    cross, along = step_sums([whole(2)], [whole_across(1)])
-    cross, along, select_low = join(cross, along, select_low)
-    across[2] = swapped(cross[0], "dp", 2)
-    along = along_moves(along[0])
-    dinner, conv_sums, select_grad, sent, kept[3] = inner_backward(
-        places, dact, select_low, w_sel, inner, act, flat_mask, conv_w, conv_b, lefts[0]
-    )
-    across[2], along, dinner, conv_sums, select_grad, sent, kept[3] = join(
-        across[2], along, dinner, conv_sums, select_grad, sent, kept[3]
-    )
-    total[1] = along
-
-    got[3] = swapped(sent, "dp", 1)
-    mixed_select = select_grad.reshape(-1, count, own).transpose(1, 0, 2).reshape(count, own_dim, -1)
-    mixed_step = jnp.concatenate(step_grads, axis=1).astype(bf16).reshape(count, own_dim, -1)
-    split = mixed_select.shape[2]
-    mixed = jnp.take(jnp.concatenate([mixed_select, mixed_step], axis=2), places, axis=0)
-    mixed = mixed.reshape((2, 2, outer, 1) + mixed.shape[1:])
-    kept[4] = mixed[0]
-    got[4] = swapped(mixed[1], "dp", 1)
-    _, along = step_sums([], [whole_across(2)])
-    got[3], along, kept[4], got[4] = join(got[3], along, kept[4], got[4])
-    along = along_moves(along[0])
-    cross, _ = step_sums([(kept[3], got[3], (0, half)), (kept[3], got[3], (1, half)), whole(4)], [])
-    first, second = swapped(cross[0], "dp", 2), cross[1]
-    across[4] = swapped(cross[2], "dp", 2)
-    norm_here, norm_away = spread_sum(
-        dgate + [dinner],
-        [weights[0], weights[1], weights[1], w_inner[None]],
-        [(0, 0), (0, 0), (0, 1), (0, 0)],
-        micro,
-        shard_rows,
-    )
-    first, across[4], along, second, norm_here = join(first, across[4], along, second, norm_here)
-    total[2] = along
-    _, along = step_sums([], [(kept[3], got[3], first, (0, half)), whole_across(4)])
-    second, along, gated = join(second, along, gated)
-    second = swapped(second, "dp", 2)
-    along = [along_moves(v) for v in along]
-    layer_here, layer_away = spread_sum(
-        gated, [weights[0], weights[1], weights[1]], [(1, 0), (1, 0), (1, 1)], micro, shard_rows
-    )
-    dnormed = norm_here + norm_away.astype(f32)
-    gain_part = jnp.sum(dnormed * normal_rows, axis=(0, 1))
-    vectors = jnp.concatenate([conv_sums[: taps + 1], jnp.concatenate(sums, axis=1)], axis=0)
-    vectors = vectors.reshape(-1, count, own).transpose(1, 0, 2).reshape(count, -1)
-    vectors = jnp.concatenate([gain_part.reshape(count, own_dim), vectors], axis=1)
-    second, along, layer_here, vectors = join(second, along, layer_here, vectors)
-    total[3], total[4] = along
-    _, along = step_sums([], [(kept[3], got[3], second, (1, half))])
-    along, vectors = join(along, vectors)
-    total[5] = along_moves(along[0])
-    vectors = reduce_scatter(vectors)[0]
-    gain_total = tensor_sum(vectors[:own_dim])
-    vectors = vectors[own_dim:].reshape(-1, own)
-
-    layer_rows = hidden + (layer_here + layer_away.astype(f32))
-    dnormal = dnormed * gain_full
-    grad_rows = cotangent.astype(f32) + inverse_rms * (
-        dnormal - normal_rows * jnp.mean(dnormal * normal_rows, axis=-1, keepdims=True)
-    )
-    sums_of = [final_sum(total[n]) for n in range(6)]
-    gate_grad = jnp.concatenate([v[0] for v in sums_of[:3]], axis=1)
-    out_grad = jnp.concatenate([v[1] for v in sums_of[:3]], axis=0)
-    inner_grad = jnp.concatenate([sums_of[3][0], sums_of[5][0]], axis=1)
-    mixed = sums_of[4][0]
+    cross, along = step_sums([[source("third")]], [[source("second") + (across["second"], 0)]])
+    cross, along, select_low, layer_away = join(cross, along, select_low, layer_away)
+    across["third"] = swapped(cross[0], "dp", 2)
+    total["second"] = along_moves(along[0])
+    if two:
+        layer_away = swapped(layer_away, "tensor", 1)
+    dinner, conv_sums, select_grad, sent, kept["inner"] = inner_backward(
+        places_now, dact, select_low, w_sel, inner, act, flat_mask, conv_w, conv_b, lefts[0]
+    )
+    across["third"], total["second"], dinner, conv_sums, select_grad, sent, kept["inner"], where, layer_away = join(
+        across["third"], total["second"], dinner, conv_sums, select_grad, sent, kept["inner"], where, layer_away
+    )
+    norm_terms = [(grouped(v), 0, v.shape[1]) + w[0] for v, w in zip(dgate, weights)]
+    norm_terms.append((grouped(dinner), 0, channels, w_inner[None], 0, 0))
+    got["inner"] = swapped(sent, "dp", 1)
+    if two:
+        norm_away = project(norm_terms, 1 - where, shard_rows, bf16)
+    else:
+        norm_away = project_all(norm_terms)
+    got["inner"], norm_away, where = join(got["inner"], norm_away, where)
+    cross, along = step_sums(
+        [[source("inner", 0, half)], [source("inner", 1, half)]], [[source("third") + (across["third"], 0)]]
+    )
+    cross, along, where, norm_away, select_grad = join(cross, along, where, norm_away, select_grad)
+    across["first"] = swapped(cross[0], "dp", 2)
+    total["third"] = along_moves(along[0])
+    if two:
+        norm_away = swapped(norm_away, "tensor", 1)
+        norm_here = project(norm_terms, where, shard_rows, f32)
+        layer_here = project(out_terms, where, shard_rows, f32)
+    else:
+        norm_here, layer_here = [jnp.zeros(v.shape, f32) for v in (norm_away, layer_away)]
+    across["first"], total["third"], cross[1], norm_here, layer_here, norm_away = join(
+        across["first"], total["third"], cross[1], norm_here, layer_here, norm_away
+    )
+    step_grad = jnp.concatenate(step_grads, axis=1)
+    step_grad = step_grad.reshape(count, rank_dim // count, count, own).transpose(1, 2, 0, 3)
+    small = jnp.concatenate(
+        [select_grad, step_grad.reshape(rank_dim, channels), conv_sums, jnp.concatenate(sums, axis=1)], axis=0
+    )
+    small = lax.psum_scatter(small, "dp", scatter_dimension=1, tiled=True)
+    _, along = step_sums([], [[source("inner", 0, half) + (across["first"], 0)]])
+    cross[1], along, norm_here = join(cross[1], along, norm_here)
+    across["last"] = swapped(cross[1], "dp", 2)
+    total["first"] = along_moves(along[0])
+    norm_here, total["first"][1] = join(norm_here, total["first"][1])
+    layer_rows, grad_rows = finish(hidden, cotangent, gain_full, layer_here, layer_away, norm_here, norm_away)
+    gates, outs = [], []
+    total["gate"], layer_rows = join(total["gate"], layer_rows)
+    gates += final_sum(total["gate"], (False,))
+    outs += final_sum(total["out"], (True,))
+    for name in ("second", "third"):
+        one, other = final_sum(total[name], (False, True))
+        gates.append(one)
+        outs.append(other)
+    across["last"], total["first"], gates, outs, layer_rows, grad_rows = join(
+        across["last"], total["first"], gates, outs, layer_rows, grad_rows
+    )
+    _, along = step_sums([], [[source("inner", 1, half) + (across["last"], 0)]])
+    total["last"] = along_moves(along[0])
+    gate_grad = jnp.concatenate(gates, axis=1)
+    (first,) = final_sum(total["first"], (False,))
+    own_input = input_weight.astype(f32)
+    most = jnp.sum(own_input[:, 0, :half] * first, axis=1) + jnp.sum(own_input[:, 1] * gate_grad, axis=1)
+    (last,) = final_sum(total["last"], (False,))
+    gain_total = tensor_sum(most + jnp.sum(own_input[:, 0, half:] * last, axis=1)) / norm_gain
+    at = picked + rank_dim
     return (
         layer_rows,
         grad_rows,
         gain_total,
-        jnp.stack([inner_grad, gate_grad], axis=1),
-        vectors[:taps],
-        vectors[taps],
-        mixed[:, :split].reshape(-1, own).T,
-        mixed[:, split:].reshape(-1, channels),
-        vectors[taps + 2],
-        vectors[taps + 9 :],
-        vectors[taps + 1],
-        out_grad,
+        jnp.stack([jnp.concatenate([first, last], axis=1), gate_grad], axis=1),
+        small[at : at + taps],
+        small[at + taps],
+        small[:picked].T,
+        small[picked:at].reshape(-1, channels),
+        small[at + 9],
+        small[at + 16 :],
+        small[at + 8],
+        jnp.concatenate(outs, axis=0),
     )
 
 

time: 607 us -> 564 us (0.929)
  waiting for transfers between devices: 156 us -> 138 us
  starting transfers between devices: 81.8 us -> 65.9 us
  local copies, waits for them, and re-layouts: 76.8 us -> 61.3 us
  Pallas kernels: 232 us -> 245 us
  other arithmetic: 33.6 us -> 27.4 us
    ppermute x28 -> x24, waiting for transfers between devices: 106 us -> 42.3 us  [swapped(): return lax.ppermute(values, axis, [(i, i ^ bit) for i in range(count)])]
    ppermute x18, waiting for transfers between devices: 13 us -> 39.8 us  [along_moves(): lax.ppermute(v, 'dp', [(i, (i + 4 * (j + 1)) % count) for i in range(coun...]
    pallas_call x16 -> x19, Pallas kernels: 67 us -> 82.7 us  [the longest x4 38.4 us: project(): pl.pallas_call(functools.partial(project_kernel, len(terms)), grid_spec=p...]
    unnamed x237 -> x209, local copies, waits for them, and re-layouts: 48.3 us -> 34.8 us
    ppermute x18, starting transfers between devices: 46.3 us -> 34.3 us  [along_moves(): lax.ppermute(v, 'dp', [(i, (i + 4 * (j + 1)) % count) for i in range(coun...]
    all_gather x1, waiting for transfers between devices: 0.01 us -> 10.5 us  [on_device(): w_inner = lax.all_gather(input_weight[:, 0], 'dp', axis=0, tiled=True)]
    add x7 -> x4, other arithmetic: 7.79 us -> 1.19 us  [the longest x2 1.17 us: tensor_sum(): return values + swapped(values.astype(kind), 'tensor', 1).astype(f32)]
    all_gather x2, waiting for transfers between devices: 32.6 us -> 39.1 us  [on_device(): both = lax.all_gather(both, 'dp', axis=1, tiled=True)]
  transfers between devices with their start and end apart: 52 -> 49, of which waited for: 21 -> 18; matrix products, arithmetic and copies ran while one was open for 10% -> 8% of each run, Pallas kernels for 35% -> 41%
where the time goes in v3:
time: 564 us; the launch traced here: 555 us
  Pallas kernels  245 us (43%)
  waiting for transfers between devices  138 us (24%)
  starting transfers between devices  65.9 us (12%)
  local copies, waits for them, and re-layouts  61.3 us (11%)
  other arithmetic  27.4 us (5%)
  between operations  15.8 us (3%)
    pallas_call x3, Pallas kernels, scan_both_ways(): pl.pallas_call(functools.partial(scan_kernel, states), grid=(blocks, micr...  117 us
    ppermute x24, waiting for transfers between devices, swapped(): return lax.ppermute(values, axis, [(i, i ^ bit) for i in range(count)])  42.3 us
    ppermute x18, waiting for transfers between devices, along_moves(): lax.ppermute(v, 'dp', [(i, (i + 4 * (j + 1)) % count) for i in range(coun...  39.8 us
    all_gather x2, waiting for transfers between devices, on_device(): both = lax.all_gather(both, 'dp', axis=1, tiled=True)  39.1 us
    pallas_call x4, Pallas kernels, project(): pl.pallas_call(functools.partial(project_kernel, len(terms)), grid_spec=p...  38.4 us
    unnamed x209, local copies, waits for them, and re-layouts  34.8 us
    ppermute x18, starting transfers between devices, along_moves(): lax.ppermute(v, 'dp', [(i, (i + 4 * (j + 1)) % count) for i in range(coun...  34.3 us
    ppermute x24, starting transfers between devices, swapped(): return lax.ppermute(values, axis, [(i, i ^ bit) for i in range(count)])  27.4 us
  transfers between devices with their start and end apart: 49, of which 18 were waited for; matrix products, arithmetic and copies ran while one was open for 8% of the time, Pallas kernels for 41%

profile of v3, /device:TPU:0, one launch (start us, length us, event | category | flops | bytes accessed | tf_op | source)
XLA Modules:
  0.0 555.4 jit_solution(5465548165608589984)
XLA Ops:
  28.5 9.1 %collective-permute-done.3 = f32[8,3072]{1,0:T(8,128)S(1)} collective-permute-done((f32[8,3072]{1,0:T(8,128)S(1)}, f32[8,3072]{1,0:T(8,128)S(1)}, u32[]{:S(2)}, u32[]{:S(2)}) %collective-permute-start.3) | collective-permute-done | bytes 98336 | tf_op jit(solution)/shard_map/ppermute | solution.py:35
  57.1 8.8 %collective-permute-done.8 = bf16[4,288,128]{2,1,0:T(8,128)(2,1)S(1)} collective-permute-done((bf16[4,288,128]{2,1,0:T(8,128)(2,1)S(1)}, bf16[4,288,128]{2,1,0:T(8,128)(2,1)S(1)}, u32[]{:S(2)}, u32[]{:S(2)}) %collective-permute-start.8) | collective-permute-done | bytes 294944 | tf_op jit(solution)/shard_map/ppermute | solution.py:35
  88.8 10.5 %all-gather.9.cloned.1.call-done = bf16[2048,1,2048]{2,0,1:T(8,128)(2,1)} async-done(((bf16[128,1,2048]{2,0,1:T(8,128)(2,1)}), bf16[2048,1,2048]{2,0,1:T(8,128)(2,1)}) %all-gather.9.cloned.1.call-update) | async-done | bytes 8388624 | tf_op jit(solution)/shard_map/all_gather | solution.py:849
  102.1 12.4 %shard_map.229 = (f32[512,2048]{1,0:T(8,128)}, bf16[512,2048]{1,0:T(8,128)(2,1)S(1)}, f32[512,160]{1,0:T(8,128)S(1)}) custom-call(bf16[512,2048]{1,0:T(8,128)(2,1)S(1)} %copy-done.2, bf16[2048,2048]{1,0:T(8,128)(2,1)} %bitcast.264, f32[512,4]{1,0:T(8,128)S(1)} %stack.68.refs_1_.refs_7_, f32[4,2048]{1,0:T(4,128)S(1)} %bitcast.258, f32[1,2048]{1,0:T(1,128)S(1)} %bitcast.260, ...), custom_call_target="tpu_custom_call" | custom-call | flops 1 | bytes 1 | tf_op jit(solution)/shard_map/pallas_call | solution.py:435
  123.3 5.4 collective-permute-done.10
  129.8 5.0 shard_map.230
  138.9 37.0 %all-gather.5.cloned.1.call-done.gate_weight_ref.out_weight_ref.refs_3_.refs_4_ = bf16[2,2048,1024]{2,1,0:T(8,128)(2,1)} async-done(((bf16[2,128,1024]{2,1,0:T(8,128)(2,1)}), bf16[2,2048,1024]{2,1,0:T(8,128)(2,1)}) %all-gather.5.cloned.1.call-update) | async-done | bytes 8388624 | tf_op jit(solution)/shard_map/all_gather | solution.py:854
  175.9 54.5 %shard_map.231 = (bf16[2,256,1024]{2,1,0:T(8,128)(2,1)}, bf16[2,256,1024]{2,1,0:T(8,128)(2,1)}, f32[2,256,1024]{2,1,0:T(8,128)}, f32[128,1024]{1,0:T(8,128)}, f3...) custom-call(f32[2,256,2048]{2,1,0:T(8,128)} %bitcast.222, ...), custom_call_target="tpu_custom_call" | custom-call | flops 1 | bytes 1 | tf_op jit(solution)/shard_map/pallas_call | solution.py:286
  251.3 31.5 %shard_map.237 = (bf16[2,256,512]{2,1,0:T(8,128)(2,1)}, bf16[2,256,512]{2,1,0:T(8,128)(2,1)}, f32[2,256,512]{2,1,0:T(8,128)}, f32[128,512]{1,0:T(8,128)}, f32[24...) custom-call(f32[2,256,2048]{2,1,0:T(8,128)} %bitcast.223, ...), custom_call_target="tpu_custom_call" | custom-call | flops 1 | bytes 1 | tf_op jit(solution)/shard_map/pallas_call | solution.py:286
  294.6 10.4 %collective-permute-done.15.refs_5_ = bf16[4,1,128,512]{3,2,1,0:T(8,128)(2,1)S(1)} collective-permute-done((bf16[4,1,128,512]{3,2,1,0:T(8,128)(2,1)S(1)}, bf16[4,1,128,512]{3,2,1,0:T(8,128)(2,1)S(1)}, u32[]{:S(2)}, u32[]{:S(2)}) %collective-permute-start.15) | collective-permute-done | bytes 524320 | tf_op jit(solution)/shard_map/ppermute | solution.py:35
  321.5 31.2 %shard_map.241 = (bf16[2,256,512]{2,1,0:T(8,128)(2,1)}, bf16[2,256,512]{2,1,0:T(8,128)(2,1)}, f32[2,256,512]{2,1,0:T(8,128)}, f32[128,512]{1,0:T(8,128)}, f32[24...) custom-call(f32[2,256,2048]{2,1,0:T(8,128)} %bitcast.224, ...), custom_call_target="tpu_custom_call" | custom-call | flops 1 | bytes 1 | tf_op jit(solution)/shard_map/pallas_call | solution.py:286
  368.9 8.4 %shard_map.245 = bf16[2,128,2048]{2,1,0:T(8,128)(2,1)S(1)} custom-call(s32[1]{0:T(128)S(6)} %sub.111.where_ref, bf16[2,256,1024]{2,1,0:T(8,128)(2,1)S(1)} %copy-done.12, bf16[2,256,512]{2,1,0:T(8,128)(2,1)S(1)} %copy-done.22, bf16[2,256,512]{2,1,0:T(8,128)(2,1)S(1)} %copy-done.24, ...), custom_call_target="tpu_custom_call" | custom-call | flops 1 | bytes 1 | tf_op jit(solution)/shard_map/pallas_call | solution.py:603
  377.4 5.8 %collective-permute-done.24.refs_2_ = bf16[1,128,1024]{2,1,0:T(8,128)(2,1)S(1)} collective-permute-done((bf16[1,128,1024]{2,1,0:T(8,128)(2,1)}, bf16[1,128,1024]{2,1,0:T(8,128)(2,1)S(1)}, u32[]{:S(2)}, u32[]{:S(2)}) %collective-permute-start.24) | collective-permute-done | bytes 262176 | tf_op jit(solution)/shard_map/ppermute | solution.py:746
  390.5 5.4 collective-permute-start.27
  398.3 19.0 %shard_map.247 = (bf16[512,2048]{1,0:T(8,128)(2,1)}, f32[8,2048]{1,0:T(8,128)S(1)}, f32[160,2048]{1,0:T(8,128)}, bf16[2,4,1,128,2048]{4,3,2,1,0:T(8,128)(2,1)}, bf16[2,4,1,128,2048]{4,3,2,1,0:T(8,128)(2,1)}) custom-call(s32[16]{0:T(128)S(1)} %fusion.44.places_ref, f32[512,1024]{1,0:T(8,128)} %bitcast.285, f32[512,512]{1,0:T(8,128)S(1)} %bitcast.256, ...), custom_call_target="tpu_custom_call" | custom-call | flops 1 | bytes 1 | tf_op jit(solution)/shard_map/pallas_call | solution.py:550
  422.6 11.3 %shard_map.248 = bf16[2,128,2048]{2,1,0:T(8,128)(2,1)} custom-call(s32[1]{0:T(128)S(6)} %sub.112.where_ref, bf16[2,256,1024]{2,1,0:T(8,128)(2,1)S(1)} %copy-done.14, bf16[2,256,512]{2,1,0:T(8,128)(2,1)S(1)} %copy-done.18, bf16[2,256,512]{2,1,0:T(8,128)(2,1)S(1)} %copy-done.19, bf16[2,256,2048]{2,1,0:T(8,128)(2,1)S(1)} %bitcast.245, ...), custom_call_target="tpu_custom_call" | custom-call | flops 1 | bytes 1 | tf_op jit(solution)/shard_map/pallas_call | solution.py:603
  452.3 7.8 %shard_map.251 = f32[2,128,2048]{2,1,0:T(8,128)S(1)} custom-call(s32[1]{0:T(128)} %bitcast.56.where_ref, bf16[2,256,1024]{2,1,0:T(8,128)(2,1)S(1)} %copy-done.12, bf16[2,256,512]{2,1,0:T(8,128)(2,1)S(1)} %copy-done.23, bf16[2,256,512]{2,1,0:T(8,128)(2,1)S(1)} %copy-done.25, ...), custom_call_target="tpu_custom_call" | custom-call | flops 1 | bytes 1 | tf_op jit(solution)/shard_map/pallas_call | solution.py:603
  461.4 11.0 %shard_map.250 = f32[2,128,2048]{2,1,0:T(8,128)S(1)} custom-call(s32[1]{0:T(128)} %bitcast.56.where_ref, bf16[2,256,1024]{2,1,0:T(8,128)(2,1)S(1)} %copy-done.14, bf16[2,256,512]{2,1,0:T(8,128)(2,1)S(1)} %copy-done.18, bf16[2,256,512]{2,1,0:T(8,128)(2,1)S(1)} %copy-done.20, bf16[2,256,2048]{2,1,0:T(8,128)(2,1)} %bitcast.244, ...), custom_call_target="tpu_custom_call" | custom-call | flops 1 | bytes 1 | tf_op jit(solution)/shard_map/pallas_call | solution.py:603
  484.1 7.2 %collective-permute-done.38.refs_1_ = bf16[1,128,1024]{2,1,0:T(8,128)(2,1)S(1)} collective-permute-done((bf16[1,128,1024]{2,1,0:T(8,128)(2,1)S(1)}, bf16[1,128,1024]{2,1,0:T(8,128)(2,1)S(1)}, u32[]{:S(2)}, u32[]{:S(2)}) %collective-permute-start.38) | collective-permute-done | bytes 262176 | tf_op jit(solution)/shard_map/ppermute | solution.py:746
  491.3 5.7 %shard_map.253 = (f32[256,2048]{1,0:T(8,128)}, f32[256,2048]{1,0:T(8,128)}) custom-call(f32[256,2048]{1,0:T(8,128)S(1)} %bitcast.228, bf16[256,2048]{1,0:T(8,128)(2,1)} %bitcast.63.cot_ref, f32[1,2048]{1,0:T(1,128)S(1)} %bitcast.263, f32[256,2048]{1,0:T(8,128)} %bitcast.243, bf16[256,2048]{1,0:T(8,128)(2,1)S(1)} %bitcast.257, f32[256,2048]{1,0:T(8,128)} %bitcast.246, ...), custom_call_target="tpu_custom_call" | custom-call | flops 1 | bytes 1 | tf_op jit(solution)/shard_map/pallas_call | solution.py:802
  497.2 8.6 %collective-permute-done.39.refs_2_ = bf16[1,128,1024]{2,1,0:T(8,128)(2,1)S(1)} collective-permute-done((bf16[1,128,1024]{2,1,0:T(8,128)(2,1)S(1)}, bf16[1,128,1024]{2,1,0:T(8,128)(2,1)S(1)}, u32[]{:S(2)}, u32[]{:S(2)}) %collective-permute-start.39) | collective-permute-done | bytes 262176 | tf_op jit(solution)/shard_map/ppermute | solution.py:746
  508.4 5.9 %collective-permute-start.41 = (bf16[1,128,1024]{2,1,0:T(8,128)(2,1)S(1)}, bf16[1,128,1024]{2,1,0:T(8,128)(2,1)S(1)}, u32[]{:S(2)}, u32[]{:S(2)}) collective-permute-start(bf16[1,128,1024]{2,1,0:T(8,128)(2,1)S(1)} %get-tuple-element.402), channel_id=1, source_target_pairs={{0,8},{2,10},{4,12},{6,14},{8,16},{10,18},{12,20},{14,22},{16,24},... | collective-permute-start | bytes 786440 | tf_op jit(solution)/shard_map/ppermute | solution.py:746
  518.5 7.8 %collective-permute-done.41.refs_1_ = bf16[1,128,1024]{2,1,0:T(8,128)(2,1)S(1)} collective-permute-done((bf16[1,128,1024]{2,1,0:T(8,128)(2,1)S(1)}, bf16[1,128,1024]{2,1,0:T(8,128)(2,1)S(1)}, u32[]{:S(2)}, u32[]{:S(2)}) %collective-permute-start.41) | collective-permute-done | bytes 262176 | tf_op jit(solution)/shard_map/ppermute | solution.py:746
  526.3 10.4 %collective-permute-done.42.refs_2_ = bf16[1,128,1024]{2,1,0:T(8,128)(2,1)S(1)} collective-permute-done((bf16[1,128,1024]{2,1,0:T(8,128)(2,1)S(1)}, bf16[1,128,1024]{2,1,0:T(8,128)(2,1)S(1)}, u32[]{:S(2)}, u32[]{:S(2)}) %collective-permute-start.42) | collective-permute-done | bytes 262176 | tf_op jit(solution)/shard_map/ppermute | solution.py:746
  (403 shorter events, 209.4 us)
Async XLA Ops:
  7.2 92.1 %all-gather.9.cloned.1.call-start = ((), (), s32[]{:S(2)}) async-start(), calls=%async_computation.4 | async-start | bytes 8912896 | tf_op jit(solution)/shard_map/all_gather | solution.py:849
  11.2 164.7 %all-gather.5.cloned.1.call-start = ((), (), s32[]{:S(2)}) async-start(), calls=%async_computation.1 | async-start | bytes 8912896 | tf_op jit(solution)/shard_map/all_gather | solution.py:854
  12.5 238.8 %all-gather.7.cloned.1.call-start = ((), (), s32[]{:S(2)}) async-start(), calls=%async_computation.2 | async-start | bytes 8912896 | tf_op jit(solution)/shard_map/all_gather | solution.py:854
  13.5 528.1 %reduce-scatter.2.cloned.1.call-start = ((), (), s32[]{:S(2)}) async-start(), calls=%async_computation.3 | async-start | bytes 2785280 | tf_op jit(solution)/shard_map/reduce_scatter | solution.py:1020
  39.6 27.4 %collective-permute-start.4 = (bf16[2,128,2048]{2,1,0:T(8,128)(2,1)}, bf16[2,128,2048]{2,1,0:T(8,128)(2,1)}, u32[]{:S(2)}, u32[]{:S(2)}) collective-permute-start(bf16[2,128,2048]{2,1,0:T(8,128)(2,1)} %multiply_convert_fusion), channel_id=1, source_target_pairs={{0,1},{1,0},{2,3},{3,2},{4,5},{5,4},{6,7},{7,6},{8,9},{9,8},{10,11... | collective-permute-start | bytes 3145736 | tf_op jit(solution)/shard_map/ppermute | solution.py:35
  73.4 42.6 %collective-permute-start.11 = (bf16[2,128,2048]{2,1,0:T(8,128)(2,1)}, bf16[2,128,2048]{2,1,0:T(8,128)(2,1)}, u32[]{:S(2)}, u32[]{:S(2)}) collective-permute-start(bf16[2,128,2048]{2,1,0:T(8,128)(2,1)} %param.15), channel_id=1, source_target_pairs={{0,1},{1,0},{2,3},{3,2},{4,5},{5,4},{6,7},{7,6},{8,9},{9,8},{10,11... | collective-permute-start | bytes 3145736 | tf_op jit(solution)/shard_map/ppermute | solution.py:35
  248.6 36.8 %collective-permute-start.14 = (bf16[4,1,128,1536]{3,2,1,0:T(8,128)(2,1)}, bf16[4,1,128,1536]{3,2,1,0:T(8,128)(2,1)}, u32[]{:S(2)}, u32[]{:S(2)}) collective-permute-start(bf16[4,1,128,1536]{3,2,1,0:T(8,128)(2,1)} %get-tuple-element.244), channel_id=1, source_target_pairs={{0,4},{2,6},{4,0},{6,2},{8,12},{10,14},{12,8},{14,10},{16,20},{18,... | collective-permute-start | bytes 4718600 | tf_op jit(solution)/shard_map/ppermute | solution.py:35
  311.6 41.2 %collective-permute-start.20 = (bf16[4,2,128,512]{3,2,1,0:T(8,128)(2,1)}, bf16[4,2,128,512]{3,2,1,0:T(8,128)(2,1)S(1)}, u32[]{:S(2)}, u32[]{:S(2)}) collective-permute-start(bf16[4,2,128,512]{3,2,1,0:T(8,128)(2,1)} %get-tuple-element.272), channel_id=1, source_target_pairs={{0,4},{2,6},{4,0},{6,2},{8,12},{10,14},{12,8},{14,10},{16,20},{18,... | collective-permute-start | bytes 3145736 | tf_op jit(solution)/shard_map/ppermute | solution.py:35
  312.2 40.5 %collective-permute-start.17 = (bf16[1,128,1024]{2,1,0:T(8,128)(2,1)}, bf16[1,128,1024]{2,1,0:T(8,128)(2,1)S(1)}, u32[]{:S(2)}, u32[]{:S(2)}) collective-permute-start(bf16[1,128,1024]{2,1,0:T(8,128)(2,1)} %get-tuple-element.269), channel_id=1, source_target_pairs={{0,8},{2,10},{4,12},{6,14},{8,16},{10,18},{12,20},{14,22},{16,24},... | collective-permute-start | bytes 786440 | tf_op jit(solution)/shard_map/ppermute | solution.py:746
  313.1 39.6 %collective-permute-start.18 = (bf16[1,128,1024]{2,1,0:T(8,128)(2,1)}, bf16[1,128,1024]{2,1,0:T(8,128)(2,1)S(1)}, u32[]{:S(2)}, u32[]{:S(2)}) collective-permute-start(bf16[1,128,1024]{2,1,0:T(8,128)(2,1)} %get-tuple-element.270), channel_id=1, source_target_pairs={{0,16},{2,18},{4,20},{6,22},{8,24},{10,26},{12,28},{14,30},{16,0},... | collective-permute-start | bytes 786440 | tf_op jit(solution)/shard_map/ppermute | solution.py:746
  314.6 38.1 %collective-permute-start.19 = (bf16[1,128,1024]{2,1,0:T(8,128)(2,1)}, bf16[1,128,1024]{2,1,0:T(8,128)(2,1)S(1)}, u32[]{:S(2)}, u32[]{:S(2)}) collective-permute-start(bf16[1,128,1024]{2,1,0:T(8,128)(2,1)} %get-tuple-element.271), channel_id=1, source_target_pairs={{0,24},{2,26},{4,28},{6,30},{8,0},{10,2},{12,4},{14,6},{16,8},{18,... | collective-permute-start | bytes 786440 | tf_op jit(solution)/shard_map/ppermute | solution.py:746
  360.1 23.2 %collective-permute-start.22 = (bf16[2,4,2,128,512]{4,3,2,1,0:T(8,128)(2,1)S(1)}, bf16[2,4,2,128,512]{4,3,2,1,0:T(8,128)(2,1)S(1)}, u32[]{:S(2)}, u32[]{:S(2)}) collective-permute-start(bf16[2,4,2,128,512]{4,3,2,1,0:T(8,128)(2,1)S(1)} %shard_map.243), channel_id=1, source_target_pairs={{0,2},{2,0},{4,6},{6,4},{8,10},{10,8},{12,14},{14,12},{16,18},{18,... | collective-permute-start | bytes 6291464 | tf_op jit(solution)/shard_map/ppermute | solution.py:35
  388.5 31.0 %collective-permute-start.26 = (bf16[4,2,128,512]{3,2,1,0:T(8,128)(2,1)S(1)}, bf16[4,2,128,512]{3,2,1,0:T(8,128)(2,1)S(1)}, u32[]{:S(2)}, u32[]{:S(2)}) collective-permute-start(bf16[4,2,128,512]{3,2,1,0:T(8,128)(2,1)S(1)} %get-tuple-element.307), channel_id=1, source_target_pairs={{0,4},{2,6},{4,0},{6,2},{8,12},{10,14},{12,8},{14,10},{16,20},{18,... | collective-permute-start | bytes 3145736 | tf_op jit(solution)/shard_map/ppermute | solution.py:35
  389.9 29.5 %collective-permute-start.30 = (bf16[2,128,2048]{2,1,0:T(8,128)(2,1)S(1)}, bf16[2,128,2048]{2,1,0:T(8,128)(2,1)S(1)}, u32[]{:S(2)}, u32[]{:S(2)}) collective-permute-start(bf16[2,128,2048]{2,1,0:T(8,128)(2,1)S(1)} %shard_map.245), channel_id=1, source_target_pairs={{0,1},{1,0},{2,3},{3,2},{4,5},{5,4},{6,7},{7,6},{8,9},{9,8},{10,11... | collective-permute-start | bytes 3145736 | tf_op jit(solution)/shard_map/ppermute | solution.py:35
  390.5 26.8 %collective-permute-start.27 = (bf16[2,128,512]{2,1,0:T(8,128)(2,1)S(1)}, bf16[2,128,512]{2,1,0:T(8,128)(2,1)S(1)}, u32[]{:S(2)}, u32[]{:S(2)}) collective-permute-start(bf16[2,128,512]{2,1,0:T(8,128)(2,1)S(1)} %get-tuple-element.309), channel_id=1, source_target_pairs={{0,8},{2,10},{4,12},{6,14},{8,16},{10,18},{12,20},{14,22},{16,24},... | collective-permute-start | bytes 786440 | tf_op jit(solution)/shard_map/ppermute | solution.py:746
  442.4 31.5 %collective-permute-start.32 = (bf16[4,1,128,1024]{3,2,1,0:T(8,128)(2,1)}, bf16[4,1,128,1024]{3,2,1,0:T(8,128)(2,1)}, u32[]{:S(2)}, u32[]{:S(2)}) collective-permute-start(bf16[4,1,128,1024]{3,2,1,0:T(8,128)(2,1)} %get-tuple-element.338), channel_id=1, source_target_pairs={{0,4},{2,6},{4,0},{6,2},{8,12},{10,14},{12,8},{14,10},{16,20},{18,... | collective-permute-start | bytes 3145736 | tf_op jit(solution)/shard_map/ppermute | solution.py:35
  443.0 30.9 %collective-permute-start.36 = (bf16[2,128,2048]{2,1,0:T(8,128)(2,1)}, bf16[2,128,2048]{2,1,0:T(8,128)(2,1)}, u32[]{:S(2)}, u32[]{:S(2)}) collective-permute-start(bf16[2,128,2048]{2,1,0:T(8,128)(2,1)} %shard_map.248), channel_id=1, source_target_pairs={{0,1},{1,0},{2,3},{3,2},{4,5},{5,4},{6,7},{7,6},{8,9},{9,8},{10,11... | collective-permute-start | bytes 3145736 | tf_op jit(solution)/shard_map/ppermute | solution.py:35
  446.3 27.5 %collective-permute-start.33 = (bf16[2,128,512]{2,1,0:T(8,128)(2,1)S(1)}, bf16[2,128,512]{2,1,0:T(8,128)(2,1)S(1)}, u32[]{:S(2)}, u32[]{:S(2)}) collective-permute-start(bf16[2,128,512]{2,1,0:T(8,128)(2,1)S(1)} %get-tuple-element.340), channel_id=1, source_target_pairs={{0,8},{2,10},{4,12},{6,14},{8,16},{10,18},{12,20},{14,22},{16,24},... | collective-permute-start | bytes 786440 | tf_op jit(solution)/shard_map/ppermute | solution.py:746
  447.1 26.8 %collective-permute-start.34 = (bf16[2,128,512]{2,1,0:T(8,128)(2,1)S(1)}, bf16[2,128,512]{2,1,0:T(8,128)(2,1)S(1)}, u32[]{:S(2)}, u32[]{:S(2)}) collective-permute-start(bf16[2,128,512]{2,1,0:T(8,128)(2,1)S(1)} %get-tuple-element.341), channel_id=1, source_target_pairs={{0,16},{2,18},{4,20},{6,22},{8,24},{10,26},{12,28},{14,30},{16,0},... | collective-permute-start | bytes 786440 | tf_op jit(solution)/shard_map/ppermute | solution.py:746
  449.4 24.5 %collective-permute-start.35 = (bf16[2,128,512]{2,1,0:T(8,128)(2,1)S(1)}, bf16[2,128,512]{2,1,0:T(8,128)(2,1)S(1)}, u32[]{:S(2)}, u32[]{:S(2)}) collective-permute-start(bf16[2,128,512]{2,1,0:T(8,128)(2,1)S(1)} %get-tuple-element.342), channel_id=1, source_target_pairs={{0,24},{2,26},{4,28},{6,30},{8,0},{10,2},{12,4},{14,6},{16,8},{18,... | collective-permute-start | bytes 786440 | tf_op jit(solution)/shard_map/ppermute | solution.py:746
  476.9 29.0 %collective-permute-start.37 = (bf16[4,1,128,1024]{3,2,1,0:T(8,128)(2,1)S(1)}, bf16[4,1,128,1024]{3,2,1,0:T(8,128)(2,1)S(1)}, u32[]{:S(2)}, u32[]{:S(2)}) collective-permute-start(bf16[4,1,128,1024]{3,2,1,0:T(8,128)(2,1)S(1)} %copy-done.62), channel_id=1, source_target_pairs={{0,4},{2,6},{4,0},{6,2},{8,12},{10,14},{12,8},{14,10},{16,20},{18,... | collective-permute-start | bytes 3145736 | tf_op jit(solution)/shard_map/ppermute | solution.py:35
  479.7 26.2 %collective-permute-start.39 = (bf16[1,128,1024]{2,1,0:T(8,128)(2,1)S(1)}, bf16[1,128,1024]{2,1,0:T(8,128)(2,1)S(1)}, u32[]{:S(2)}, u32[]{:S(2)}) collective-permute-start(bf16[1,128,1024]{2,1,0:T(8,128)(2,1)S(1)} %get-tuple-element.358), channel_id=1, source_target_pairs={{0,16},{2,18},{4,20},{6,22},{8,24},{10,26},{12,28},{14,30},{16,0},... | collective-permute-start | bytes 786440 | tf_op jit(solution)/shard_map/ppermute | solution.py:746
  480.6 25.3 %collective-permute-start.40 = (bf16[1,128,1024]{2,1,0:T(8,128)(2,1)S(1)}, bf16[1,128,1024]{2,1,0:T(8,128)(2,1)S(1)}, u32[]{:S(2)}, u32[]{:S(2)}) collective-permute-start(bf16[1,128,1024]{2,1,0:T(8,128)(2,1)S(1)} %get-tuple-element.359), channel_id=1, source_target_pairs={{0,24},{2,26},{4,28},{6,30},{8,0},{10,2},{12,4},{14,6},{16,8},{18,... | collective-permute-start | bytes 786440 | tf_op jit(solution)/shard_map/ppermute | solution.py:746
  514.3 22.4 %collective-permute-start.42 = (bf16[1,128,1024]{2,1,0:T(8,128)(2,1)S(1)}, bf16[1,128,1024]{2,1,0:T(8,128)(2,1)S(1)}, u32[]{:S(2)}, u32[]{:S(2)}) collective-permute-start(bf16[1,128,1024]{2,1,0:T(8,128)(2,1)S(1)} %get-tuple-element.403), channel_id=1, source_target_pairs={{0,16},{2,18},{4,20},{6,22},{8,24},{10,26},{12,28},{14,30},{16,0},... | collective-permute-start | bytes 786440 | tf_op jit(solution)/shard_map/ppermute | solution.py:746
  (120 other events, 1197.5 us)
Sparse Core Ops, SparseCore 0:
  11.3 87.9 all-gather.8
  101.5 74.3 all-gather.4
  178.1 73.1 all-gather.6
  446.4 87.6 reduce-scatter.1

commit v4 on v3

--- a/solution.py
+++ b/solution.py
@@ -852,7 +852,7 @@
     for low, high in ((0, half), (half, channels)):
         both = jnp.stack([input_weight[:, 1, low:high], out_shard[:, low:high]])
         both = lax.all_gather(both, "dp", axis=1, tiled=True)
-        weights += [((both, 0, at), (both, 1, at)) for at in range(1 if low == 0 else 2)]
+        weights.append(((both, 0, 0), (both, 1, 0)))
 
     pieces = [norm_gain, conv_weight, conv_bias, step_bias, decay_log, skip_gain]
     packed = doubled(jnp.concatenate([v.reshape(-1) for v in pieces]))
@@ -903,8 +903,8 @@
 
     def scanned(number, skip_now):
         return scan_both_ways(
-            (0, 2, 3)[number],
-            (2, 1, 1)[number],
+            2 * number,
+            2,
             quarter,
             grouped(pre_step),
             grouped(act),
@@ -927,6 +927,9 @@
     def source(piece, at=0, wide=None):
         return kept[piece], got[piece], at, wide or kept[piece].shape[-1]
 
+    def last_step(piece, name, at=0):
+        return [source(piece) + (across[name], at)]
+
     hold(scanned(0, skip_g))
     places_now = places
     for piece, left, right in (("gate", lefts[0], dgate[0]), ("out", lefts[1], gated[0])):
@@ -934,83 +937,88 @@
         sent, places_now = join(sent, places_now)
         got[piece] = swapped(sent, "dp", 1)
         kept[piece] = grad_parts(places_now, True, (left,), (right,))
-    cross, _ = step_sums(
-        [[source("gate"), source("out", 0, quarter)], [source("out", 1, quarter)]], []
-    )
+    cross, _ = step_sums([[source("gate"), source("out")]], [])
     skip_now, cross = join(skip_g, cross)
-    across["zero"], across["rest"] = [swapped(v, "dp", 2) for v in cross]
+    across["early"] = swapped(cross[0], "dp", 2)
 
     results = scanned(1, skip_now)
-    results, across["zero"] = join(results, across["zero"])
+    results, across["early"] = join(results, across["early"])
     hold(results)
-    sent = grad_parts(places_now, False, lefts, (dgate[1], gated[1]))
-    sent, places_now = join(sent, places_now)
-    got["second"] = swapped(sent, "dp", 1)
-    kept["second"] = grad_parts(places_now, True, lefts, (dgate[1], gated[1]))
-    kept["second"], across["rest"], got["second"] = join(kept["second"], across["rest"], got["second"])
-    cross, along = step_sums([[source("second")]], [[source("gate") + (across["zero"], 0)]])
-    skip_now, cross, along = join(skip_now, cross, along)
+    _, along = step_sums([], [last_step("gate", "early"), last_step("out", "early", 1)])
+    along, places_now, rank_grads = join(along, places_now, rank_grads)
     total["gate"] = along_moves(along[0])
-    across["second"] = swapped(cross[0], "dp", 2)
-
-    results = scanned(2, skip_now)
-    results, total["gate"], across["second"] = join(results, total["gate"], across["second"])
-    hold(results)
+    for piece, left, right in (("gate_late", lefts[0], dgate[1]), ("out_late", lefts[1], gated[1])):
+        sent = grad_parts(places_now, False, (left,), (right,))
+        sent, places_now = join(sent, places_now)
+        got[piece] = swapped(sent, "dp", 1)
     rank_grad = sum(v[j] for v in rank_grads for j in range(v.shape[0]))
     select_terms = jnp.concatenate([rank_grad, unblocked(dins, states), unblocked(douts, states)], axis=2)
-    _, along = step_sums(
-        [], [[source("out", 0, quarter) + (across["zero"], 2), source("out", 1, quarter) + (across["rest"], 0)]]
-    )
+    select_terms, places_now = join(select_terms.reshape(tokens, -1), places_now)
+    select_terms = tensor_sum(select_terms, bf16)
+    places_now, total["gate"][1] = join(places_now, total["gate"][1])
+    for piece, left, right in (("gate_late", lefts[0], dgate[1]), ("out_late", lefts[1], gated[1])):
+        kept[piece] = grad_parts(places_now, True, (left,), (right,))
     two = lax.axis_size("tensor") == 2
     where = lax.axis_index("tensor").astype(jnp.int32)[None]
-    select_terms, places_now, along = join(select_terms.reshape(tokens, -1), places_now, along)
-    select_terms = tensor_sum(select_terms, bf16)
-    total["out"] = along_moves(along[0])
-    sent = grad_parts(places_now, False, lefts, (dgate[2], gated[2]))
-    sent, places_now = join(sent, places_now)
-    got["third"] = swapped(sent, "dp", 1)
-    kept["third"] = grad_parts(places_now, True, lefts, (dgate[2], gated[2]))
-    kept["third"], where = join(kept["third"], where)
+    kept["out_late"], where = join(kept["out_late"], where)
     out_terms = [(grouped(v), 0, v.shape[1]) + w[1] for v, w in zip(gated, weights)]
     layer_away = project(out_terms, 1 - where, shard_rows, bf16) if two else project_all(out_terms)
-    select_terms, kept["third"], got["third"], total["out"], layer_away = join(
-        select_terms, kept["third"], got["third"], total["out"], layer_away
-    )
+    names = ("gate_late", "out_late")
+    select_terms, late_kept, late_got, total["gate"], layer_away = join(
+        select_terms, [kept[n] for n in names], [got[n] for n in names], total["gate"], layer_away
+    )
+    for n, one, other in zip(names, late_kept, late_got):
+        kept[n], got[n] = one, other
     select_low = select_terms.astype(bf16)
-    cross, along = step_sums([[source("third")]], [[source("second") + (across["second"], 0)]])
-    cross, along, select_low, layer_away = join(cross, along, select_low, layer_away)
-    across["third"] = swapped(cross[0], "dp", 2)
-    total["second"] = along_moves(along[0])
+    cross, _ = step_sums([[source("gate_late")], [source("out_late")]], [])
+    cross, select_low, layer_away, along[1] = join(cross, select_low, layer_away, along[1])
+    across["gate_late"] = swapped(cross[0], "dp", 2)
+    total["out"] = along_moves(along[1])
     if two:
         layer_away = swapped(layer_away, "tensor", 1)
     dinner, conv_sums, select_grad, sent, kept["inner"] = inner_backward(
         places_now, dact, select_low, w_sel, inner, act, flat_mask, conv_w, conv_b, lefts[0]
     )
-    across["third"], total["second"], dinner, conv_sums, select_grad, sent, kept["inner"], where, layer_away = join(
-        across["third"], total["second"], dinner, conv_sums, select_grad, sent, kept["inner"], where, layer_away
+    across["gate_late"], total["out"], dinner, conv_sums, select_grad, sent, kept["inner"], where, layer_away, cross[1] = join(
+        across["gate_late"],
+        total["out"],
+        dinner,
+        conv_sums,
+        select_grad,
+        sent,
+        kept["inner"],
+        where,
+        layer_away,
+        cross[1],
     )
     norm_terms = [(grouped(v), 0, v.shape[1]) + w[0] for v, w in zip(dgate, weights)]
     norm_terms.append((grouped(dinner), 0, channels, w_inner[None], 0, 0))
     got["inner"] = swapped(sent, "dp", 1)
+    across["out_late"] = swapped(cross[1], "dp", 2)
+    _, along = step_sums([], [last_step("gate_late", "gate_late")])
+    along, where = join(along, where)
+    total["gate_late"] = along_moves(along[0])
     if two:
         norm_away = project(norm_terms, 1 - where, shard_rows, bf16)
     else:
         norm_away = project_all(norm_terms)
-    got["inner"], norm_away, where = join(got["inner"], norm_away, where)
+    got["inner"], norm_away, where, total["gate_late"], across["out_late"] = join(
+        got["inner"], norm_away, where, total["gate_late"], across["out_late"]
+    )
     cross, along = step_sums(
-        [[source("inner", 0, half)], [source("inner", 1, half)]], [[source("third") + (across["third"], 0)]]
+        [[source("inner", 0, half)], [source("inner", 1, half)]], [last_step("out_late", "out_late")]
     )
     cross, along, where, norm_away, select_grad = join(cross, along, where, norm_away, select_grad)
     across["first"] = swapped(cross[0], "dp", 2)
-    total["third"] = along_moves(along[0])
+    total["out_late"] = along_moves(along[0])
     if two:
         norm_away = swapped(norm_away, "tensor", 1)
         norm_here = project(norm_terms, where, shard_rows, f32)
         layer_here = project(out_terms, where, shard_rows, f32)
     else:
         norm_here, layer_here = [jnp.zeros(v.shape, f32) for v in (norm_away, layer_away)]
-    across["first"], total["third"], cross[1], norm_here, layer_here, norm_away = join(
-        across["first"], total["third"], cross[1], norm_here, layer_here, norm_away
+    across["first"], total["out_late"], cross[1], norm_here, layer_here, norm_away = join(
+        across["first"], total["out_late"], cross[1], norm_here, layer_here, norm_away
     )
     step_grad = jnp.concatenate(step_grads, axis=1)
     step_grad = step_grad.reshape(count, rank_dim // count, count, own).transpose(1, 2, 0, 3)
@@ -1024,14 +1032,9 @@
     total["first"] = along_moves(along[0])
     norm_here, total["first"][1] = join(norm_here, total["first"][1])
     layer_rows, grad_rows = finish(hidden, cotangent, gain_full, layer_here, layer_away, norm_here, norm_away)
-    gates, outs = [], []
     total["gate"], layer_rows = join(total["gate"], layer_rows)
-    gates += final_sum(total["gate"], (False,))
-    outs += final_sum(total["out"], (True,))
-    for name in ("second", "third"):
-        one, other = final_sum(total[name], (False, True))
-        gates.append(one)
-        outs.append(other)
+    gates = [final_sum(total[n], (False,))[0] for n in ("gate", "gate_late")]
+    outs = [final_sum(total[n], (True,))[0] for n in ("out", "out_late")]
     across["last"], total["first"], gates, outs, layer_rows, grad_rows = join(
         across["last"], total["first"], gates, outs, layer_rows, grad_rows
     )

time: 564 us -> 534 us (0.947)
  Pallas kernels: 245 us -> 231 us
  local copies, waits for them, and re-layouts: 61.3 us -> 50.4 us
    unnamed x209 -> x188, local copies, waits for them, and re-layouts: 34.8 us -> 21.9 us
    ppermute x24 -> x23, waiting for transfers between devices: 42.3 us -> 32.6 us  [swapped(): return lax.ppermute(values, axis, [(i, i ^ bit) for i in range(count)])]
    pallas_call x3 -> x2, Pallas kernels: 117 us -> 109 us  [scan_both_ways(): pl.pallas_call(functools.partial(scan_kernel, states), grid=(blocks, micr...]
    ppermute x18, waiting for transfers between devices: 39.8 us -> 46.9 us  [along_moves(): lax.ppermute(v, 'dp', [(i, (i + 4 * (j + 1)) % count) for i in range(coun...]
    ppermute x24 -> x23, starting transfers between devices: 27.4 us -> 26 us  [swapped(): return lax.ppermute(values, axis, [(i, i ^ bit) for i in range(count)])]
  transfers between devices with their start and end apart: 49 -> 48, of which waited for: 18 -> 19; matrix products, arithmetic and copies ran while one was open for 8% -> 10% of each run, Pallas kernels for 41% -> 40%
where the time goes in v4:
time: 534 us; the launch traced here: 529 us
  Pallas kernels  231 us (43%)
  waiting for transfers between devices  135 us (25%)
  starting transfers between devices  69.1 us (13%)
  local copies, waits for them, and re-layouts  50.4 us (9%)
  other arithmetic  25.9 us (5%)
  between operations  15.2 us (3%)
    pallas_call x2, Pallas kernels, scan_both_ways(): pl.pallas_call(functools.partial(scan_kernel, states), grid=(blocks, micr...  109 us
    ppermute x18, waiting for transfers between devices, along_moves(): lax.ppermute(v, 'dp', [(i, (i + 4 * (j + 1)) % count) for i in range(coun...  46.9 us
    all_gather x2, waiting for transfers between devices, on_device(): both = lax.all_gather(both, 'dp', axis=1, tiled=True)  40.5 us
    ppermute x18, starting transfers between devices, along_moves(): lax.ppermute(v, 'dp', [(i, (i + 4 * (j + 1)) % count) for i in range(coun...  39 us
    pallas_call x4, Pallas kernels, project(): pl.pallas_call(functools.partial(project_kernel, len(terms)), grid_spec=p...  37.6 us
    ppermute x23, waiting for transfers between devices, swapped(): return lax.ppermute(values, axis, [(i, i ^ bit) for i in range(count)])  32.6 us
    ppermute x23, starting transfers between devices, swapped(): return lax.ppermute(values, axis, [(i, i ^ bit) for i in range(count)])  26 us
    pallas_call x7, Pallas kernels, step_sums(): pl.pallas_call(functools.partial(sums_kernel, tuple((len(v) for v in cros...  24.3 us
  transfers between devices with their start and end apart: 48, of which 19 were waited for; matrix products, arithmetic and copies ran while one was open for 10% of the time, Pallas kernels for 40%

profile of v4, /device:TPU:0, one launch (start us, length us, event | category | flops | bytes accessed | tf_op | source)
XLA Modules:
  0.0 528.8 jit_solution(6980640861111759783)
XLA Ops:
  28.5 9.9 %collective-permute-done.3 = f32[8,3072]{1,0:T(8,128)S(1)} collective-permute-done((f32[8,3072]{1,0:T(8,128)S(1)}, f32[8,3072]{1,0:T(8,128)S(1)}, u32[]{:S(2)}, u32[]{:S(2)}) %collective-permute-start.3) | collective-permute-done | bytes 98336 | tf_op jit(solution)/shard_map/ppermute | solution.py:35
  48.5 5.0 collective-permute-done.6
  57.1 9.6 %collective-permute-done.8 = bf16[4,288,128]{2,1,0:T(8,128)(2,1)S(1)} collective-permute-done((bf16[4,288,128]{2,1,0:T(8,128)(2,1)S(1)}, bf16[4,288,128]{2,1,0:T(8,128)(2,1)S(1)}, u32[]{:S(2)}, u32[]{:S(2)}) %collective-permute-start.8) | collective-permute-done | bytes 294944 | tf_op jit(solution)/shard_map/ppermute | solution.py:35
  90.7 8.6 %all-gather.9.cloned.1.call-done = bf16[2048,1,2048]{2,0,1:T(8,128)(2,1)} async-done(((bf16[128,1,2048]{2,0,1:T(8,128)(2,1)}), bf16[2048,1,2048]{2,0,1:T(8,128)(2,1)}) %all-gather.9.cloned.1.call-update) | async-done | bytes 8388624 | tf_op jit(solution)/shard_map/all_gather | solution.py:849
  100.8 12.5 %shard_map.229 = (f32[512,2048]{1,0:T(8,128)}, bf16[512,2048]{1,0:T(8,128)(2,1)S(1)}, f32[512,160]{1,0:T(8,128)}) custom-call(bf16[512,2048]{1,0:T(8,128)(2,1)S(1)} %copy-done.3, bf16[2048,2048]{1,0:T(8,128)(2,1)} %bitcast.233, f32[512,4]{1,0:T(8,128)S(1)} %stack.68.refs_1_.refs_6_, f32[4,2048]{1,0:T(4,128)S(1)} %bitcast.227, f32[1,2048]{1,0:T(1,128)S(1)} %bitcast.229, ...), custom_call_target="tpu_custom_call" | custom-call | flops 1 | bytes 1 | tf_op jit(solution)/shard_map/pallas_call | solution.py:435
  122.0 5.8 %collective-permute-done.10 = f32[512,160]{1,0:T(8,128)} collective-permute-done((f32[512,160]{1,0:T(8,128)}, f32[512,160]{1,0:T(8,128)}, u32[]{:S(2)}, u32[]{:S(2)}) %collective-permute-start.10) | collective-permute-done | bytes 327712 | tf_op jit(solution)/shard_map/ppermute | solution.py:35
  129.1 5.0 shard_map.230
  138.4 37.5 %all-gather.5.cloned.1.call-done.gate_weight_ref.out_weight_ref.refs_2_.refs_3_ = bf16[2,2048,1024]{2,1,0:T(8,128)(2,1)} async-done(((bf16[2,128,1024]{2,1,0:T(8,128)(2,1)}), bf16[2,2048,1024]{2,1,0:T(8,128)(2,1)}) %all-gather.5.cloned.1.call-update) | async-done | bytes 8388624 | tf_op jit(solution)/shard_map/all_gather | solution.py:854
  175.9 54.4 %shard_map.231 = (bf16[2,256,1024]{2,1,0:T(8,128)(2,1)}, bf16[2,256,1024]{2,1,0:T(8,128)(2,1)}, f32[2,256,1024]{2,1,0:T(8,128)}, f32[128,1024]{1,0:T(8,128)}, f3...) custom-call(f32[2,256,2048]{2,1,0:T(8,128)} %bitcast.204, ...), custom_call_target="tpu_custom_call" | custom-call | flops 1 | bytes 1 | tf_op jit(solution)/shard_map/pallas_call | solution.py:286
  251.4 54.9 %shard_map.237 = (bf16[2,256,1024]{2,1,0:T(8,128)(2,1)}, bf16[2,256,1024]{2,1,0:T(8,128)(2,1)}, f32[2,256,1024]{2,1,0:T(8,128)}, f32[128,1024]{1,0:T(8,128)}, f3...) custom-call(f32[2,256,2048]{2,1,0:T(8,128)} %bitcast.205, ...), custom_call_target="tpu_custom_call" | custom-call | flops 1 | bytes 1 | tf_op jit(solution)/shard_map/pallas_call | solution.py:286
  333.0 7.6 %shard_map.243 = bf16[2,128,2048]{2,1,0:T(8,128)(2,1)S(1)} custom-call(s32[1]{0:T(128)S(6)} %sub.105.where_ref, bf16[2,256,1024]{2,1,0:T(8,128)(2,1)S(1)} %copy-done.15, bf16[2,256,1024]{2,1,0:T(8,128)(2,1)S(1)} %copy-done.19, bf16[2,2048,1024]{2,1,0:T(8,128)(2,1)} %all-gather.5.cloned.1.call-done.gate_weight_ref.out_weight_ref.refs_2_.refs_3_, ...), custom_call_target="tpu_custom_call" | custom-call | flops 1 | bytes 1 | tf_op jit(solution)/shard_map/pallas_call | solution.py:603
  349.3 9.4 %collective-permute-start.23 = (bf16[1,128,1024]{2,1,0:T(8,128)(2,1)}, bf16[1,128,1024]{2,1,0:T(8,128)(2,1)S(1)}, u32[]{:S(2)}, u32[]{:S(2)}) collective-permute-start(bf16[1,128,1024]{2,1,0:T(8,128)(2,1)} %get-tuple-element.275), channel_id=1, source_target_pairs={{0,16},{2,18},{4,20},{6,22},{8,24},{10,26},{12,28},{14,30},{16,0},... | collective-permute-start | bytes 786440 | tf_op jit(solution)/shard_map/ppermute | solution.py:746
  359.7 18.5 %shard_map.245 = (bf16[512,2048]{1,0:T(8,128)(2,1)}, f32[8,2048]{1,0:T(8,128)S(1)}, f32[160,2048]{1,0:T(8,128)}, bf16[2,4,1,128,2048]{4,3,2,1,0:T(8,128)(2,1)}, bf16[2,4,1,128,2048]{4,3,2,1,0:T(8,128)(2,1)}) custom-call(s32[16]{0:T(128)S(1)} %fusion.40.places_ref, f32[512,1024]{1,0:T(8,128)} %bitcast.249, f32[512,1024]{1,0:T(8,128)} %bitcast.250, ...), custom_call_target="tpu_custom_call" | custom-call | flops 1 | bytes 1 | tf_op jit(solution)/shard_map/pallas_call | solution.py:550
  389.9 11.2 %shard_map.247 = bf16[2,128,2048]{2,1,0:T(8,128)(2,1)} custom-call(s32[1]{0:T(128)S(6)} %sub.106.where_ref, bf16[2,256,1024]{2,1,0:T(8,128)(2,1)S(1)} %copy-done.13, bf16[2,256,1024]{2,1,0:T(8,128)(2,1)S(1)} %copy-done.17, bf16[2,256,2048]{2,1,0:T(8,128)(2,1)S(1)} %bitcast.217, ...), custom_call_target="tpu_custom_call" | custom-call | flops 1 | bytes 1 | tf_op jit(solution)/shard_map/pallas_call | solution.py:603
  401.2 4.8 collective-permute-done.28.refs_2_
  415.8 5.5 %collective-permute-start.32 = (bf16[1,128,1024]{2,1,0:T(8,128)(2,1)}, bf16[1,128,1024]{2,1,0:T(8,128)(2,1)S(1)}, u32[]{:S(2)}, u32[]{:S(2)}) collective-permute-start(bf16[1,128,1024]{2,1,0:T(8,128)(2,1)} %copy-done.60), channel_id=1, source_target_pairs={{0,8},{2,10},{4,12},{6,14},{8,16},{10,18},{12,20},{14,22},{16,24},... | collective-permute-start | bytes 786440 | tf_op jit(solution)/shard_map/ppermute | solution.py:746
  423.7 7.7 %shard_map.250 = f32[2,128,2048]{2,1,0:T(8,128)S(1)} custom-call(s32[1]{0:T(128)} %bitcast.53.where_ref, bf16[2,256,1024]{2,1,0:T(8,128)(2,1)S(1)} %copy-done.16, bf16[2,256,1024]{2,1,0:T(8,128)(2,1)S(1)} %copy-done.20, bf16[2,2048,1024]{2,1,0:T(8,128)(2,1)} %all-gather.5.cloned.1.call-done.gate_weight_ref.out_weight_ref.refs_2_.refs_3_, ...), custom_call_target="tpu_custom_call" | custom-call | flops 1 | bytes 1 | tf_op jit(solution)/shard_map/pallas_call | solution.py:603
  432.8 11.0 %shard_map.249 = f32[2,128,2048]{2,1,0:T(8,128)S(1)} custom-call(s32[1]{0:T(128)} %bitcast.53.where_ref, bf16[2,256,1024]{2,1,0:T(8,128)(2,1)S(1)} %copy-done.13, bf16[2,256,1024]{2,1,0:T(8,128)(2,1)S(1)} %copy-done.18, bf16[2,256,2048]{2,1,0:T(8,128)(2,1)} %bitcast.216, ...), custom_call_target="tpu_custom_call" | custom-call | flops 1 | bytes 1 | tf_op jit(solution)/shard_map/pallas_call | solution.py:603
  453.8 9.0 %collective-permute-done.37.refs_1_ = bf16[1,128,1024]{2,1,0:T(8,128)(2,1)S(1)} collective-permute-done((bf16[1,128,1024]{2,1,0:T(8,128)(2,1)S(1)}, bf16[1,128,1024]{2,1,0:T(8,128)(2,1)S(1)}, u32[]{:S(2)}, u32[]{:S(2)}) %collective-permute-start.37) | collective-permute-done | bytes 262176 | tf_op jit(solution)/shard_map/ppermute | solution.py:746
  462.8 5.7 %shard_map.252 = (f32[256,2048]{1,0:T(8,128)}, f32[256,2048]{1,0:T(8,128)}) custom-call(f32[256,2048]{1,0:T(8,128)S(1)} %bitcast.201, bf16[256,2048]{1,0:T(8,128)(2,1)} %bitcast.59.cot_ref, f32[1,2048]{1,0:T(1,128)S(1)} %bitcast.232, f32[256,2048]{1,0:T(8,128)} %bitcast.218, bf16[256,2048]{1,0:T(8,128)(2,1)S(1)} %bitcast.224, f32[256,2048]{1,0:T(8,128)} %bitcast.219, ...), custom_call_target="tpu_custom_call" | custom-call | flops 1 | bytes 1 | tf_op jit(solution)/shard_map/pallas_call | solution.py:802
  468.7 8.9 %collective-permute-done.38.refs_2_ = bf16[1,128,1024]{2,1,0:T(8,128)(2,1)S(1)} collective-permute-done((bf16[1,128,1024]{2,1,0:T(8,128)(2,1)S(1)}, bf16[1,128,1024]{2,1,0:T(8,128)(2,1)S(1)}, u32[]{:S(2)}, u32[]{:S(2)}) %collective-permute-start.38) | collective-permute-done | bytes 262176 | tf_op jit(solution)/shard_map/ppermute | solution.py:746
  481.4 5.1 collective-permute-start.40
  490.3 8.2 %collective-permute-done.40.refs_1_ = bf16[1,128,1024]{2,1,0:T(8,128)(2,1)S(1)} collective-permute-done((bf16[1,128,1024]{2,1,0:T(8,128)(2,1)S(1)}, bf16[1,128,1024]{2,1,0:T(8,128)(2,1)S(1)}, u32[]{:S(2)}, u32[]{:S(2)}) %collective-permute-start.40) | collective-permute-done | bytes 262176 | tf_op jit(solution)/shard_map/ppermute | solution.py:746
  498.5 11.3 %collective-permute-done.41.refs_2_ = bf16[1,128,1024]{2,1,0:T(8,128)(2,1)S(1)} collective-permute-done((bf16[1,128,1024]{2,1,0:T(8,128)(2,1)S(1)}, bf16[1,128,1024]{2,1,0:T(8,128)(2,1)S(1)}, u32[]{:S(2)}, u32[]{:S(2)}) %collective-permute-start.41) | collective-permute-done | bytes 262176 | tf_op jit(solution)/shard_map/ppermute | solution.py:746
  (379 shorter events, 186.4 us)
Async XLA Ops:
  7.2 92.1 %all-gather.9.cloned.1.call-start = ((), (), s32[]{:S(2)}) async-start(), calls=%async_computation.4 | async-start | bytes 8912896 | tf_op jit(solution)/shard_map/all_gather | solution.py:849
  11.2 164.8 %all-gather.5.cloned.1.call-start = ((), (), s32[]{:S(2)}) async-start(), calls=%async_computation.1 | async-start | bytes 8912896 | tf_op jit(solution)/shard_map/all_gather | solution.py:854
  12.5 238.8 %all-gather.7.cloned.1.call-start = ((), (), s32[]{:S(2)}) async-start(), calls=%async_computation.2 | async-start | bytes 8912896 | tf_op jit(solution)/shard_map/all_gather | solution.py:854
  13.5 501.9 %reduce-scatter.2.cloned.1.call-start = ((), (), s32[]{:S(2)}) async-start(), calls=%async_computation.3 | async-start | bytes 2785280 | tf_op jit(solution)/shard_map/reduce_scatter | solution.py:1028
  40.3 27.5 %collective-permute-start.4 = (bf16[2,128,2048]{2,1,0:T(8,128)(2,1)}, bf16[2,128,2048]{2,1,0:T(8,128)(2,1)}, u32[]{:S(2)}, u32[]{:S(2)}) collective-permute-start(bf16[2,128,2048]{2,1,0:T(8,128)(2,1)} %multiply_convert_fusion), channel_id=1, source_target_pairs={{0,1},{1,0},{2,3},{3,2},{4,5},{5,4},{6,7},{7,6},{8,9},{9,8},{10,11... | collective-permute-start | bytes 3145736 | tf_op jit(solution)/shard_map/ppermute | solution.py:35
  74.0 40.8 %collective-permute-start.11 = (bf16[2,128,2048]{2,1,0:T(8,128)(2,1)}, bf16[2,128,2048]{2,1,0:T(8,128)(2,1)}, u32[]{:S(2)}, u32[]{:S(2)}) collective-permute-start(bf16[2,128,2048]{2,1,0:T(8,128)(2,1)} %param.15), channel_id=1, source_target_pairs={{0,1},{1,0},{2,3},{3,2},{4,5},{5,4},{6,7},{7,6},{8,9},{9,8},{10,11... | collective-permute-start | bytes 3145736 | tf_op jit(solution)/shard_map/ppermute | solution.py:35
  247.8 58.5 %collective-permute-start.14 = (bf16[4,1,128,2048]{3,2,1,0:T(8,128)(2,1)}, bf16[4,1,128,2048]{3,2,1,0:T(8,128)(2,1)}, u32[]{:S(2)}, u32[]{:S(2)}) collective-permute-start(bf16[4,1,128,2048]{3,2,1,0:T(8,128)(2,1)} %shard_map.236), channel_id=1, source_target_pairs={{0,4},{2,6},{4,0},{6,2},{8,12},{10,14},{12,8},{14,10},{16,20},{18,... | collective-permute-start | bytes 6291464 | tf_op jit(solution)/shard_map/ppermute | solution.py:35
  315.9 24.8 %collective-permute-start.18 = (bf16[2,4,1,128,1024]{4,3,2,1,0:T(8,128)(2,1)}, bf16[2,4,1,128,1024]{4,3,2,1,0:T(8,128)(2,1)}, u32[]{:S(2)}, u32[]{:S(2)}) collective-permute-start(bf16[2,4,1,128,1024]{4,3,2,1,0:T(8,128)(2,1)} %shard_map.240), channel_id=1, source_target_pairs={{0,2},{2,0},{4,6},{6,4},{8,10},{10,8},{12,14},{14,12},{16,18},{18,... | collective-permute-start | bytes 6291464 | tf_op jit(solution)/shard_map/ppermute | solution.py:35
  316.1 24.5 %collective-permute-start.17 = (bf16[2,4,1,128,1024]{4,3,2,1,0:T(8,128)(2,1)S(1)}, bf16[2,4,1,128,1024]{4,3,2,1,0:T(8,128)(2,1)}, u32[]{:S(2)}, u32[]{:S(2)}) collective-permute-start(bf16[2,4,1,128,1024]{4,3,2,1,0:T(8,128)(2,1)S(1)} %shard_map.239), channel_id=1, source_target_pairs={{0,2},{2,0},{4,6},{6,4},{8,10},{10,8},{12,14},{14,12},{16,18},{18,... | collective-permute-start | bytes 6291464 | tf_op jit(solution)/shard_map/ppermute | solution.py:35
  343.8 36.5 %collective-permute-start.21 = (bf16[4,1,128,1024]{3,2,1,0:T(8,128)(2,1)S(1)}, bf16[4,1,128,1024]{3,2,1,0:T(8,128)(2,1)S(1)}, u32[]{:S(2)}, u32[]{:S(2)}) collective-permute-start(bf16[4,1,128,1024]{3,2,1,0:T(8,128)(2,1)S(1)} %get-tuple-element.272), channel_id=1, source_target_pairs={{0,4},{2,6},{4,0},{6,2},{8,12},{10,14},{12,8},{14,10},{16,20},{18,... | collective-permute-start | bytes 3145736 | tf_op jit(solution)/shard_map/ppermute | solution.py:35
  344.4 35.9 %collective-permute-start.25 = (bf16[2,128,2048]{2,1,0:T(8,128)(2,1)S(1)}, bf16[2,128,2048]{2,1,0:T(8,128)(2,1)S(1)}, u32[]{:S(2)}, u32[]{:S(2)}) collective-permute-start(bf16[2,128,2048]{2,1,0:T(8,128)(2,1)S(1)} %shard_map.243), channel_id=1, source_target_pairs={{0,1},{1,0},{2,3},{3,2},{4,5},{5,4},{6,7},{7,6},{8,9},{9,8},{10,11... | collective-permute-start | bytes 3145736 | tf_op jit(solution)/shard_map/ppermute | solution.py:35
  345.9 32.3 %collective-permute-start.22 = (bf16[1,128,1024]{2,1,0:T(8,128)(2,1)}, bf16[1,128,1024]{2,1,0:T(8,128)(2,1)S(1)}, u32[]{:S(2)}, u32[]{:S(2)}) collective-permute-start(bf16[1,128,1024]{2,1,0:T(8,128)(2,1)} %get-tuple-element.274), channel_id=1, source_target_pairs={{0,8},{2,10},{4,12},{6,14},{8,16},{10,18},{12,20},{14,22},{16,24},... | collective-permute-start | bytes 786440 | tf_op jit(solution)/shard_map/ppermute | solution.py:746
  349.3 29.6 %collective-permute-start.23 = (bf16[1,128,1024]{2,1,0:T(8,128)(2,1)}, bf16[1,128,1024]{2,1,0:T(8,128)(2,1)S(1)}, u32[]{:S(2)}, u32[]{:S(2)}) collective-permute-start(bf16[1,128,1024]{2,1,0:T(8,128)(2,1)} %get-tuple-element.275), channel_id=1, source_target_pairs={{0,16},{2,18},{4,20},{6,22},{8,24},{10,26},{12,28},{14,30},{16,0},... | collective-permute-start | bytes 786440 | tf_op jit(solution)/shard_map/ppermute | solution.py:746
  380.4 25.7 %collective-permute-start.26 = (bf16[2,4,1,128,2048]{4,3,2,1,0:T(8,128)(2,1)}, bf16[2,4,1,128,2048]{4,3,2,1,0:T(8,128)(2,1)}, u32[]{:S(2)}, u32[]{:S(2)}) collective-permute-start(bf16[2,4,1,128,2048]{4,3,2,1,0:T(8,128)(2,1)} %get-tuple-element.289), channel_id=1, source_target_pairs={{0,2},{2,0},{4,6},{6,4},{8,10},{10,8},{12,14},{14,12},{16,18},{18,... | collective-permute-start | bytes 12582920 | tf_op jit(solution)/shard_map/ppermute | solution.py:35
  380.5 25.6 %collective-permute-start.30 = (bf16[4,1,128,1024]{3,2,1,0:T(8,128)(2,1)S(1)}, bf16[4,1,128,1024]{3,2,1,0:T(8,128)(2,1)S(1)}, u32[]{:S(2)}, u32[]{:S(2)}) collective-permute-start(bf16[4,1,128,1024]{3,2,1,0:T(8,128)(2,1)S(1)} %get-tuple-element.302), channel_id=1, source_target_pairs={{0,4},{2,6},{4,0},{6,2},{8,12},{10,14},{12,8},{14,10},{16,20},{18,... | collective-permute-start | bytes 3145736 | tf_op jit(solution)/shard_map/ppermute | solution.py:35
  412.6 32.6 %collective-permute-start.31 = (bf16[4,1,128,1024]{3,2,1,0:T(8,128)(2,1)}, bf16[4,1,128,1024]{3,2,1,0:T(8,128)(2,1)}, u32[]{:S(2)}, u32[]{:S(2)}) collective-permute-start(bf16[4,1,128,1024]{3,2,1,0:T(8,128)(2,1)} %get-tuple-element.314), channel_id=1, source_target_pairs={{0,4},{2,6},{4,0},{6,2},{8,12},{10,14},{12,8},{14,10},{16,20},{18,... | collective-permute-start | bytes 3145736 | tf_op jit(solution)/shard_map/ppermute | solution.py:35
  413.9 31.3 %collective-permute-start.35 = (bf16[2,128,2048]{2,1,0:T(8,128)(2,1)}, bf16[2,128,2048]{2,1,0:T(8,128)(2,1)}, u32[]{:S(2)}, u32[]{:S(2)}) collective-permute-start(bf16[2,128,2048]{2,1,0:T(8,128)(2,1)} %shard_map.247), channel_id=1, source_target_pairs={{0,1},{1,0},{2,3},{3,2},{4,5},{5,4},{6,7},{7,6},{8,9},{9,8},{10,11... | collective-permute-start | bytes 3145736 | tf_op jit(solution)/shard_map/ppermute | solution.py:35
  415.8 29.4 %collective-permute-start.32 = (bf16[1,128,1024]{2,1,0:T(8,128)(2,1)}, bf16[1,128,1024]{2,1,0:T(8,128)(2,1)S(1)}, u32[]{:S(2)}, u32[]{:S(2)}) collective-permute-start(bf16[1,128,1024]{2,1,0:T(8,128)(2,1)} %copy-done.60), channel_id=1, source_target_pairs={{0,8},{2,10},{4,12},{6,14},{8,16},{10,18},{12,20},{14,22},{16,24},... | collective-permute-start | bytes 786440 | tf_op jit(solution)/shard_map/ppermute | solution.py:746
  421.3 23.9 %collective-permute-start.33 = (bf16[1,128,1024]{2,1,0:T(8,128)(2,1)}, bf16[1,128,1024]{2,1,0:T(8,128)(2,1)S(1)}, u32[]{:S(2)}, u32[]{:S(2)}) collective-permute-start(bf16[1,128,1024]{2,1,0:T(8,128)(2,1)} %copy-done.59), channel_id=1, source_target_pairs={{0,16},{2,18},{4,20},{6,22},{8,24},{10,26},{12,28},{14,30},{16,0},... | collective-permute-start | bytes 786440 | tf_op jit(solution)/shard_map/ppermute | solution.py:746
  421.3 23.9 %collective-permute-start.34 = (bf16[1,128,1024]{2,1,0:T(8,128)(2,1)}, bf16[1,128,1024]{2,1,0:T(8,128)(2,1)S(1)}, u32[]{:S(2)}, u32[]{:S(2)}) collective-permute-start(bf16[1,128,1024]{2,1,0:T(8,128)(2,1)} %copy-done.58), channel_id=1, source_target_pairs={{0,24},{2,26},{4,28},{6,30},{8,0},{10,2},{12,4},{14,6},{16,8},{18,... | collective-permute-start | bytes 786440 | tf_op jit(solution)/shard_map/ppermute | solution.py:746
  448.4 30.5 %collective-permute-start.36 = (bf16[4,1,128,1024]{3,2,1,0:T(8,128)(2,1)S(1)}, bf16[4,1,128,1024]{3,2,1,0:T(8,128)(2,1)S(1)}, u32[]{:S(2)}, u32[]{:S(2)}) collective-permute-start(bf16[4,1,128,1024]{3,2,1,0:T(8,128)(2,1)S(1)} %copy-done.57), channel_id=1, source_target_pairs={{0,4},{2,6},{4,0},{6,2},{8,12},{10,14},{12,8},{14,10},{16,20},{18,... | collective-permute-start | bytes 3145736 | tf_op jit(solution)/shard_map/ppermute | solution.py:35
  449.3 28.3 %collective-permute-start.38 = (bf16[1,128,1024]{2,1,0:T(8,128)(2,1)S(1)}, bf16[1,128,1024]{2,1,0:T(8,128)(2,1)S(1)}, u32[]{:S(2)}, u32[]{:S(2)}) collective-permute-start(bf16[1,128,1024]{2,1,0:T(8,128)(2,1)S(1)} %get-tuple-element.334), channel_id=1, source_target_pairs={{0,16},{2,18},{4,20},{6,22},{8,24},{10,26},{12,28},{14,30},{16,0},... | collective-permute-start | bytes 786440 | tf_op jit(solution)/shard_map/ppermute | solution.py:746
  451.9 25.7 %collective-permute-start.39 = (bf16[1,128,1024]{2,1,0:T(8,128)(2,1)S(1)}, bf16[1,128,1024]{2,1,0:T(8,128)(2,1)S(1)}, u32[]{:S(2)}, u32[]{:S(2)}) collective-permute-start(bf16[1,128,1024]{2,1,0:T(8,128)(2,1)S(1)} %get-tuple-element.335), channel_id=1, source_target_pairs={{0,24},{2,26},{4,28},{6,30},{8,0},{10,2},{12,4},{14,6},{16,8},{18,... | collective-permute-start | bytes 786440 | tf_op jit(solution)/shard_map/ppermute | solution.py:746
  486.5 23.4 %collective-permute-start.41 = (bf16[1,128,1024]{2,1,0:T(8,128)(2,1)S(1)}, bf16[1,128,1024]{2,1,0:T(8,128)(2,1)S(1)}, u32[]{:S(2)}, u32[]{:S(2)}) collective-permute-start(bf16[1,128,1024]{2,1,0:T(8,128)(2,1)S(1)} %get-tuple-element.374), channel_id=1, source_target_pairs={{0,16},{2,18},{4,20},{6,22},{8,24},{10,26},{12,28},{14,30},{16,0},... | collective-permute-start | bytes 786440 | tf_op jit(solution)/shard_map/ppermute | solution.py:746
  (109 other events, 1010.5 us)
Sparse Core Ops, SparseCore 0:
  11.3 87.9 all-gather.8
  101.4 74.4 all-gather.4
  178.1 73.1 all-gather.6
  415.9 91.9 reduce-scatter.1

commit v5 on v4

--- a/solution.py
+++ b/solution.py
@@ -398,7 +398,7 @@
 
 
 def inner_kernel(bounds, normed_ref, *refs):
-    *weight_refs, mask_ref, conv_ref, bias_ref, select_ref, inner_ref, act_ref, selected_ref = refs
+    *weight_refs, mask_ref, conv_ref, bias_ref, select_ref, inner_ref, convolved_ref, act_ref, selected_ref = refs
     tile = pl.program_id(0)
     for ref, low, high in zip(weight_refs, bounds[:-1], bounds[1:]):
 
@@ -407,6 +407,7 @@
             inner_ref[...] = jnp.dot(normed_ref[...], ref[...], preferred_element_type=f32)
 
     convolved = convolve(inner_ref[...], mask_ref, conv_ref, bias_ref)
+    convolved_ref[...] = convolved
     act = (convolved * jax.nn.sigmoid(convolved)).astype(bf16)
     act_ref[...] = act
     part = jnp.dot(act, select_ref[...], preferred_element_type=f32)
@@ -443,8 +444,9 @@
             part(1),
             pl.BlockSpec((width, picked), lambda j: (j, 0)),
         ],
-        out_specs=[part(tokens), part(tokens), fixed(tokens, picked)],
+        out_specs=[part(tokens)] * 3 + [fixed(tokens, picked)],
         out_shape=[
+            jax.ShapeDtypeStruct((tokens, channels), f32),
             jax.ShapeDtypeStruct((tokens, channels), f32),
             jax.ShapeDtypeStruct((tokens, channels), bf16),
             jax.ShapeDtypeStruct((tokens, picked), f32),
@@ -487,7 +489,7 @@
 
 
 def inner_back_kernel(bounds, places_ref, *refs):
-    *dact_refs, dsel_ref, select_ref, inner_ref, act_ref, mask_ref, conv_ref, bias_ref, left_ref = refs[:-6]
+    *dact_refs, dsel_ref, select_ref, inner_ref, convolved_ref, act_ref, mask_ref, conv_ref, left_ref = refs[:-6]
     dinner_ref, sums_ref, select_grad_ref, sent_ref, kept_ref, dact_s = refs[-6:]
     taps = conv_ref.shape[0]
     tile = pl.program_id(0)
@@ -499,7 +501,7 @@
 
     inner = inner_ref[...]
     dsel = dsel_ref[...]
-    convolved = convolve(inner, mask_ref, conv_ref, bias_ref)
+    convolved = convolved_ref[...]
     sig = jax.nn.sigmoid(convolved)
     dact = dact_s[...] + lax.dot_general(dsel, select_ref[...], last_dims, preferred_element_type=f32)
     dconv = dact * sig * (1.0 + convolved * (1.0 - sig))
@@ -508,9 +510,9 @@
     sums_ref[taps - 1 : taps, :] = jnp.sum(dconv * inner, axis=0, keepdims=True)
     for back in range(1, taps):
         tap = taps - 1 - back
-        masked = dconv * mask_ref[:, back : back + 1]
-        sums_ref[tap : tap + 1, :] = jnp.sum(masked * behind(inner, back), axis=0, keepdims=True)
-        dinner = dinner + conv_ref[tap : tap + 1, :] * ahead(masked, back)
+        moved = ahead(dconv * mask_ref[:, back : back + 1], back)
+        sums_ref[tap : tap + 1, :] = jnp.sum(moved * inner, axis=0, keepdims=True)
+        dinner = dinner + conv_ref[tap : tap + 1, :] * moved
     low = dinner.astype(bf16)
     dinner_ref[...] = low
     select_grad_ref[...] = lax.dot_general(dsel, act_ref[...], first_dims, preferred_element_type=f32)
@@ -526,7 +528,7 @@
                 out_ref[cross, j, 0] = full[j * own : (j + 1) * own]
 
 
-def inner_backward(places, dacts, dsel, select, inner, act, mask, conv_w, conv_b, left):
+def inner_backward(places, dacts, dsel, select, inner, convolved, act, mask, conv_w, left):
     tokens, channels = inner.shape
     count = places.shape[0]
     outer, own = count // 4, left.shape[0] // count
@@ -558,9 +560,9 @@
                 pl.BlockSpec((width, picked), lambda j, _: (j, 0)),
                 part(tokens),
                 part(tokens),
+                part(tokens),
                 fixed(tokens, mask.shape[1]),
                 part(taps),
-                part(1),
                 fixed(*left.shape),
             ],
             out_specs=[part(tokens), part(8), part(picked), parts, parts],
@@ -574,7 +576,7 @@
         + [jax.ShapeDtypeStruct((2, outer, 1, own, channels), bf16)] * 2,
         compiler_params=pltpu.CompilerParams(dimension_semantics=("arbitrary",), vmem_limit_bytes=52 * 2**20),
         cost_estimate=small_cost,
-    )(places, *dacts, dsel, select, inner, act, mask, conv_w, conv_b[None], left)
+    )(places, *dacts, dsel, select, inner, convolved, act, mask, conv_w, left)
 
 
 def project_kernel(count, where_ref, *refs):
@@ -697,7 +699,7 @@
 
 
 def step_sums(crosses, alongs):
-    cuts = 4
+    cuts = 2
     in_specs, out_specs, out_shape, given = [], [], [], []
     outer = (crosses + alongs)[0][0][0].shape[1]
 
@@ -890,7 +892,7 @@
     def grouped(v):
         return v.reshape(micro, group_tok, v.shape[-1])
 
-    inner, act, selected = inner_forward(normed, [w_inner], flat_mask, conv_w, conv_b, w_sel)
+    inner, convolved, act, selected = inner_forward(normed, [w_inner], flat_mask, conv_w, conv_b, w_sel)
     selected = tensor_sum(selected)
     lefts = (normed.T, cot_full.T)
     pre_step, rank_low, *tables = middle(selected, w_step, step_b, states)
@@ -971,25 +973,14 @@
         kept[n], got[n] = one, other
     select_low = select_terms.astype(bf16)
     cross, _ = step_sums([[source("gate_late")], [source("out_late")]], [])
-    cross, select_low, layer_away, along[1] = join(cross, select_low, layer_away, along[1])
+    cross, select_low, along[1] = join(cross, select_low, along[1])
     across["gate_late"] = swapped(cross[0], "dp", 2)
     total["out"] = along_moves(along[1])
-    if two:
-        layer_away = swapped(layer_away, "tensor", 1)
     dinner, conv_sums, select_grad, sent, kept["inner"] = inner_backward(
-        places_now, dact, select_low, w_sel, inner, act, flat_mask, conv_w, conv_b, lefts[0]
-    )
-    across["gate_late"], total["out"], dinner, conv_sums, select_grad, sent, kept["inner"], where, layer_away, cross[1] = join(
-        across["gate_late"],
-        total["out"],
-        dinner,
-        conv_sums,
-        select_grad,
-        sent,
-        kept["inner"],
-        where,
-        layer_away,
-        cross[1],
+        places_now, dact, select_low, w_sel, inner, convolved, act, flat_mask, conv_w, lefts[0]
+    )
+    across["gate_late"], total["out"], dinner, conv_sums, select_grad, sent, kept["inner"], where, cross[1] = join(
+        across["gate_late"], total["out"], dinner, conv_sums, select_grad, sent, kept["inner"], where, cross[1]
     )
     norm_terms = [(grouped(v), 0, v.shape[1]) + w[0] for v, w in zip(dgate, weights)]
     norm_terms.append((grouped(dinner), 0, channels, w_inner[None], 0, 0))
@@ -1027,19 +1018,21 @@
     )
     small = lax.psum_scatter(small, "dp", scatter_dimension=1, tiled=True)
     _, along = step_sums([], [[source("inner", 0, half) + (across["first"], 0)]])
-    cross[1], along, norm_here = join(cross[1], along, norm_here)
+    cross[1], along, layer_away = join(cross[1], along, layer_away)
     across["last"] = swapped(cross[1], "dp", 2)
     total["first"] = along_moves(along[0])
-    norm_here, total["first"][1] = join(norm_here, total["first"][1])
-    layer_rows, grad_rows = finish(hidden, cotangent, gain_full, layer_here, layer_away, norm_here, norm_away)
-    total["gate"], layer_rows = join(total["gate"], layer_rows)
+    if two:
+        layer_away = swapped(layer_away, "tensor", 1)
+    total["gate"], total["first"][1] = join(total["gate"], total["first"][1])
     gates = [final_sum(total[n], (False,))[0] for n in ("gate", "gate_late")]
     outs = [final_sum(total[n], (True,))[0] for n in ("out", "out_late")]
-    across["last"], total["first"], gates, outs, layer_rows, grad_rows = join(
-        across["last"], total["first"], gates, outs, layer_rows, grad_rows
+    across["last"], total["first"], gates, outs, layer_away, norm_here = join(
+        across["last"], total["first"], gates, outs, layer_away, norm_here
     )
     _, along = step_sums([], [[source("inner", 1, half) + (across["last"], 0)]])
+    along, norm_here = join(along, norm_here)
     total["last"] = along_moves(along[0])
+    layer_rows, grad_rows = finish(hidden, cotangent, gain_full, layer_here, layer_away, norm_here, norm_away)
     gate_grad = jnp.concatenate(gates, axis=1)
     (first,) = final_sum(total["first"], (False,))
     own_input = input_weight.astype(f32)

time: 534 us -> 528 us (0.989)
  Pallas kernels: 231 us -> 225 us
  transfers between devices with their start and end apart: 48 -> 48, of which waited for: 19 -> 20; matrix products, arithmetic and copies ran while one was open for 10% -> 9% of each run, Pallas kernels for 40% -> 40%
where the time goes in v5:
time: 528 us; the launch traced here: 523 us
  Pallas kernels  225 us (43%)
  waiting for transfers between devices  135 us (26%)
  starting transfers between devices  68.5 us (13%)
  local copies, waits for them, and re-layouts  51.5 us (10%)
  other arithmetic  26 us (5%)
  between operations  15.2 us (3%)
    pallas_call x2, Pallas kernels, scan_both_ways(): pl.pallas_call(functools.partial(scan_kernel, states), grid=(blocks, micr...  109 us
    ppermute x18, waiting for transfers between devices, along_moves(): lax.ppermute(v, 'dp', [(i, (i + 4 * (j + 1)) % count) for i in range(coun...  45.7 us
    all_gather x2, waiting for transfers between devices, on_device(): both = lax.all_gather(both, 'dp', axis=1, tiled=True)  43.1 us
    ppermute x18, starting transfers between devices, along_moves(): lax.ppermute(v, 'dp', [(i, (i + 4 * (j + 1)) % count) for i in range(coun...  37.9 us
    pallas_call x4, Pallas kernels, project(): pl.pallas_call(functools.partial(project_kernel, len(terms)), grid_spec=p...  37.5 us
    ppermute x23, waiting for transfers between devices, swapped(): return lax.ppermute(values, axis, [(i, i ^ bit) for i in range(count)])  28.8 us
    ppermute x23, starting transfers between devices, swapped(): return lax.ppermute(values, axis, [(i, i ^ bit) for i in range(count)])  26.6 us
    unnamed x188, local copies, waits for them, and re-layouts  22.9 us
  transfers between devices with their start and end apart: 48, of which 20 were waited for; matrix products, arithmetic and copies ran while one was open for 9% of the time, Pallas kernels for 40%

profile of v5, /device:TPU:0, one launch (start us, length us, event | category | flops | bytes accessed | tf_op | source)
XLA Modules:
  0.0 522.5 jit_solution(14541854751297565265)
XLA Ops:
  28.5 9.8 %collective-permute-done.3 = f32[8,3072]{1,0:T(8,128)S(1)} collective-permute-done((f32[8,3072]{1,0:T(8,128)S(1)}, f32[8,3072]{1,0:T(8,128)S(1)}, u32[]{:S(2)}, u32[]{:S(2)}) %collective-permute-start.3) | collective-permute-done | bytes 98336 | tf_op jit(solution)/shard_map/ppermute | solution.py:35
  56.3 7.2 %collective-permute-done.8 = bf16[4,288,128]{2,1,0:T(8,128)(2,1)S(1)} collective-permute-done((bf16[4,288,128]{2,1,0:T(8,128)(2,1)S(1)}, bf16[4,288,128]{2,1,0:T(8,128)(2,1)S(1)}, u32[]{:S(2)}, u32[]{:S(2)}) %collective-permute-start.8) | collective-permute-done | bytes 294944 | tf_op jit(solution)/shard_map/ppermute | solution.py:35
  86.9 11.9 %all-gather.9.cloned.1.call-done = bf16[2048,1,2048]{2,0,1:T(8,128)(2,1)} async-done(((bf16[128,1,2048]{2,0,1:T(8,128)(2,1)}), bf16[2048,1,2048]{2,0,1:T(8,128)(2,1)}) %all-gather.9.cloned.1.call-update) | async-done | bytes 8388624 | tf_op jit(solution)/shard_map/all_gather | solution.py:851
  100.4 13.2 %shard_map.229 = (f32[512,2048]{1,0:T(8,128)}, f32[512,2048]{1,0:T(8,128)}, bf16[512,2048]{1,0:T(8,128)(2,1)S(1)}, f32[512,160]{1,0:T(8,128)}) custom-call(bf16[512,2048]{1,0:T(8,128)(2,1)S(1)} %copy-done.3, bf16[2048,2048]{1,0:T(8,128)(2,1)} %bitcast.232, f32[512,4]{1,0:T(8,128)S(1)} %stack.68.refs_1_.refs_7_, f32[4,2048]{1,0:T(4,128)S(1)} %bitcast.227, ...), custom_call_target="tpu_custom_call" | custom-call | flops 1 | bytes 1 | tf_op jit(solution)/shard_map/pallas_call | solution.py:436
  122.3 5.7 %collective-permute-done.10 = f32[512,160]{1,0:T(8,128)} collective-permute-done((f32[512,160]{1,0:T(8,128)}, f32[512,160]{1,0:T(8,128)}, u32[]{:S(2)}, u32[]{:S(2)}) %collective-permute-start.10) | collective-permute-done | bytes 327712 | tf_op jit(solution)/shard_map/ppermute | solution.py:35
  129.3 5.1 shard_map.230
  138.6 37.4 %all-gather.5.cloned.1.call-done.gate_weight_ref.out_weight_ref.refs_2_.refs_3_ = bf16[2,2048,1024]{2,1,0:T(8,128)(2,1)} async-done(((bf16[2,128,1024]{2,1,0:T(8,128)(2,1)}), bf16[2,2048,1024]{2,1,0:T(8,128)(2,1)}) %all-gather.5.cloned.1.call-update) | async-done | bytes 8388624 | tf_op jit(solution)/shard_map/all_gather | solution.py:856
  176.0 54.5 %shard_map.231 = (bf16[2,256,1024]{2,1,0:T(8,128)(2,1)}, bf16[2,256,1024]{2,1,0:T(8,128)(2,1)}, f32[2,256,1024]{2,1,0:T(8,128)}, f32[128,1024]{1,0:T(8,128)}, f3...) custom-call(f32[2,256,2048]{2,1,0:T(8,128)} %bitcast.204, ...), custom_call_target="tpu_custom_call" | custom-call | flops 1 | bytes 1 | tf_op jit(solution)/shard_map/pallas_call | solution.py:286
  245.7 5.7 %all-gather.7.cloned.1.call-done.gate_weight_ref.out_weight_ref.refs_3_.refs_4_ = bf16[2,2048,1024]{2,1,0:T(8,128)(2,1)} async-done(((bf16[2,128,1024]{2,1,0:T(8,128)(2,1)}), bf16[2,2048,1024]{2,1,0:T(8,128)(2,1)}) %all-gather.7.cloned.1.call-update) | async-done | bytes 8388624 | tf_op jit(solution)/shard_map/all_gather | solution.py:856
  251.4 54.9 %shard_map.237 = (bf16[2,256,1024]{2,1,0:T(8,128)(2,1)}, bf16[2,256,1024]{2,1,0:T(8,128)(2,1)}, f32[2,256,1024]{2,1,0:T(8,128)}, f32[128,1024]{1,0:T(8,128)}, f3...) custom-call(f32[2,256,2048]{2,1,0:T(8,128)} %bitcast.205, ...), custom_call_target="tpu_custom_call" | custom-call | flops 1 | bytes 1 | tf_op jit(solution)/shard_map/pallas_call | solution.py:286
  321.4 6.1 %collective-permute-done.16.refs_1_ = bf16[1,128,1024]{2,1,0:T(8,128)(2,1)S(1)} collective-permute-done((bf16[1,128,1024]{2,1,0:T(8,128)(2,1)S(1)}, bf16[1,128,1024]{2,1,0:T(8,128)(2,1)S(1)}, u32[]{:S(2)}, u32[]{:S(2)}) %collective-permute-start.16) | collective-permute-done | bytes 262176 | tf_op jit(solution)/shard_map/ppermute | solution.py:748
  333.0 7.6 %shard_map.243 = bf16[2,128,2048]{2,1,0:T(8,128)(2,1)S(1)} custom-call(s32[1]{0:T(128)S(6)} %sub.105.where_ref, bf16[2,256,1024]{2,1,0:T(8,128)(2,1)S(1)} %copy-done.12, bf16[2,256,1024]{2,1,0:T(8,128)(2,1)S(1)} %copy-done.15, bf16[2,2048,1024]{2,1,0:T(8,128)(2,1)} %all-gather.5.cloned.1.call-done.gate_weight_ref.out_weight_ref.refs_2_.refs_3_, ...), custom_call_target="tpu_custom_call" | custom-call | flops 1 | bytes 1 | tf_op jit(solution)/shard_map/pallas_call | solution.py:605
  345.5 8.8 %collective-permute-start.22 = (bf16[1,128,1024]{2,1,0:T(8,128)(2,1)}, bf16[1,128,1024]{2,1,0:T(8,128)(2,1)S(1)}, u32[]{:S(2)}, u32[]{:S(2)}) collective-permute-start(bf16[1,128,1024]{2,1,0:T(8,128)(2,1)} %get-tuple-element.275), channel_id=1, source_target_pairs={{0,8},{2,10},{4,12},{6,14},{8,16},{10,18},{12,20},{14,22},{16,24},... | collective-permute-start | bytes 786440 | tf_op jit(solution)/shard_map/ppermute | solution.py:748
  359.3 16.9 %shard_map.245 = (bf16[512,2048]{1,0:T(8,128)(2,1)}, f32[8,2048]{1,0:T(8,128)S(1)}, f32[160,2048]{1,0:T(8,128)}, bf16[2,4,1,128,2048]{4,3,2,1,0:T(8,128)(2,1)}, bf16[2,4,1,128,2048]{4,3,2,1,0:T(8,128)(2,1)}) custom-call(s32[16]{0:T(128)S(1)} %fusion.40.places_ref, f32[512,1024]{1,0:T(8,128)} %bitcast.248, f32[512,1024]{1,0:T(8,128)} %bitcast.249, ...), custom_call_target="tpu_custom_call" | custom-call | flops 1 | bytes 1 | tf_op jit(solution)/shard_map/pallas_call | solution.py:552
  385.3 11.2 %shard_map.247 = bf16[2,128,2048]{2,1,0:T(8,128)(2,1)} custom-call(s32[1]{0:T(128)S(6)} %sub.106.where_ref, bf16[2,256,1024]{2,1,0:T(8,128)(2,1)S(1)} %copy-done.14, bf16[2,256,1024]{2,1,0:T(8,128)(2,1)S(1)} %copy-done.17, bf16[2,256,2048]{2,1,0:T(8,128)(2,1)S(1)} %bitcast.217, ...), custom_call_target="tpu_custom_call" | custom-call | flops 1 | bytes 1 | tf_op jit(solution)/shard_map/pallas_call | solution.py:605
  396.6 4.5 collective-permute-done.27.refs_2_
  412.7 4.1 collective-permute-start.31
  419.3 11.2 %shard_map.249 = f32[2,128,2048]{2,1,0:T(8,128)S(1)} custom-call(s32[1]{0:T(128)} %bitcast.56.where_ref, bf16[2,256,1024]{2,1,0:T(8,128)(2,1)S(1)} %copy-done.14, bf16[2,256,1024]{2,1,0:T(8,128)(2,1)S(1)} %copy-done.18, bf16[2,256,2048]{2,1,0:T(8,128)(2,1)} %bitcast.216, ...), custom_call_target="tpu_custom_call" | custom-call | flops 1 | bytes 1 | tf_op jit(solution)/shard_map/pallas_call | solution.py:605
  431.8 7.5 %shard_map.250 = f32[2,128,2048]{2,1,0:T(8,128)S(1)} custom-call(s32[1]{0:T(128)} %bitcast.56.where_ref, bf16[2,256,1024]{2,1,0:T(8,128)(2,1)S(1)} %copy-done.12, bf16[2,256,1024]{2,1,0:T(8,128)(2,1)S(1)} %copy-done.16, bf16[2,2048,1024]{2,1,0:T(8,128)(2,1)} %all-gather.5.cloned.1.call-done.gate_weight_ref.out_weight_ref.refs_2_.refs_3_, ...), custom_call_target="tpu_custom_call" | custom-call | flops 1 | bytes 1 | tf_op jit(solution)/shard_map/pallas_call | solution.py:605
  449.6 8.3 %collective-permute-done.36.refs_1_ = bf16[1,128,1024]{2,1,0:T(8,128)(2,1)S(1)} collective-permute-done((bf16[1,128,1024]{2,1,0:T(8,128)(2,1)S(1)}, bf16[1,128,1024]{2,1,0:T(8,128)(2,1)S(1)}, u32[]{:S(2)}, u32[]{:S(2)}) %collective-permute-start.36) | collective-permute-done | bytes 262176 | tf_op jit(solution)/shard_map/ppermute | solution.py:748
  458.1 14.4 %collective-permute-done.37.refs_2_ = bf16[1,128,1024]{2,1,0:T(8,128)(2,1)S(1)} collective-permute-done((bf16[1,128,1024]{2,1,0:T(8,128)(2,1)S(1)}, bf16[1,128,1024]{2,1,0:T(8,128)(2,1)S(1)}, u32[]{:S(2)}, u32[]{:S(2)}) %collective-permute-start.37) | collective-permute-done | bytes 262176 | tf_op jit(solution)/shard_map/ppermute | solution.py:748
  475.1 5.1 collective-permute-start.40
  484.3 5.6 %shard_map.257 = (f32[256,2048]{1,0:T(8,128)}, f32[256,2048]{1,0:T(8,128)}) custom-call(f32[256,2048]{1,0:T(8,128)S(1)} %bitcast.201, bf16[256,2048]{1,0:T(8,128)(2,1)} %bitcast.1.cot_ref, f32[1,2048]{1,0:T(1,128)S(1)} %bitcast.231, f32[256,2048]{1,0:T(8,128)} %bitcast.219, bf16[256,2048]{1,0:T(8,128)(2,1)S(1)} %bitcast.224, f32[256,2048]{1,0:T(8,128)} %bitcast.218, ...), custom_call_target="tpu_custom_call" | custom-call | flops 1 | bytes 1 | tf_op jit(solution)/shard_map/pallas_call | solution.py:804
  491.6 11.8 %collective-permute-done.41.refs_2_ = bf16[1,128,1024]{2,1,0:T(8,128)(2,1)S(1)} collective-permute-done((bf16[1,128,1024]{2,1,0:T(8,128)(2,1)S(1)}, bf16[1,128,1024]{2,1,0:T(8,128)(2,1)S(1)}, u32[]{:S(2)}, u32[]{:S(2)}) %collective-permute-start.41) | collective-permute-done | bytes 262176 | tf_op jit(solution)/shard_map/ppermute | solution.py:748
  (379 shorter events, 178.8 us)
Async XLA Ops:
  7.2 91.6 %all-gather.9.cloned.1.call-start = ((), (), s32[]{:S(2)}) async-start(), calls=%async_computation.4 | async-start | bytes 8912896 | tf_op jit(solution)/shard_map/all_gather | solution.py:851
  11.2 164.8 %all-gather.5.cloned.1.call-start = ((), (), s32[]{:S(2)}) async-start(), calls=%async_computation.1 | async-start | bytes 8912896 | tf_op jit(solution)/shard_map/all_gather | solution.py:856
  12.6 238.8 %all-gather.7.cloned.1.call-start = ((), (), s32[]{:S(2)}) async-start(), calls=%async_computation.2 | async-start | bytes 8912896 | tf_op jit(solution)/shard_map/all_gather | solution.py:856
  13.5 495.7 %reduce-scatter.2.cloned.1.call-start = ((), (), s32[]{:S(2)}) async-start(), calls=%async_computation.3 | async-start | bytes 2785280 | tf_op jit(solution)/shard_map/reduce_scatter | solution.py:1019
  40.3 24.3 %collective-permute-start.4 = (bf16[2,128,2048]{2,1,0:T(8,128)(2,1)}, bf16[2,128,2048]{2,1,0:T(8,128)(2,1)}, u32[]{:S(2)}, u32[]{:S(2)}) collective-permute-start(bf16[2,128,2048]{2,1,0:T(8,128)(2,1)} %multiply_convert_fusion), channel_id=1, source_target_pairs={{0,1},{1,0},{2,3},{3,2},{4,5},{5,4},{6,7},{7,6},{8,9},{9,8},{10,11... | collective-permute-start | bytes 3145736 | tf_op jit(solution)/shard_map/ppermute | solution.py:35
  70.9 44.2 %collective-permute-start.11 = (bf16[2,128,2048]{2,1,0:T(8,128)(2,1)}, bf16[2,128,2048]{2,1,0:T(8,128)(2,1)}, u32[]{:S(2)}, u32[]{:S(2)}) collective-permute-start(bf16[2,128,2048]{2,1,0:T(8,128)(2,1)} %param.15), channel_id=1, source_target_pairs={{0,1},{1,0},{2,3},{3,2},{4,5},{5,4},{6,7},{7,6},{8,9},{9,8},{10,11... | collective-permute-start | bytes 3145736 | tf_op jit(solution)/shard_map/ppermute | solution.py:35
  245.2 61.1 %collective-permute-start.14 = (bf16[4,1,128,2048]{3,2,1,0:T(8,128)(2,1)}, bf16[4,1,128,2048]{3,2,1,0:T(8,128)(2,1)}, u32[]{:S(2)}, u32[]{:S(2)}) collective-permute-start(bf16[4,1,128,2048]{3,2,1,0:T(8,128)(2,1)} %shard_map.236), channel_id=1, source_target_pairs={{0,4},{2,6},{4,0},{6,2},{8,12},{10,14},{12,8},{14,10},{16,20},{18,... | collective-permute-start | bytes 6291464 | tf_op jit(solution)/shard_map/ppermute | solution.py:35
  315.8 25.8 %collective-permute-start.17 = (bf16[2,4,1,128,1024]{4,3,2,1,0:T(8,128)(2,1)}, bf16[2,4,1,128,1024]{4,3,2,1,0:T(8,128)(2,1)}, u32[]{:S(2)}, u32[]{:S(2)}) collective-permute-start(bf16[2,4,1,128,1024]{4,3,2,1,0:T(8,128)(2,1)} %shard_map.239), channel_id=1, source_target_pairs={{0,2},{2,0},{4,6},{6,4},{8,10},{10,8},{12,14},{14,12},{16,18},{18,... | collective-permute-start | bytes 6291464 | tf_op jit(solution)/shard_map/ppermute | solution.py:35
  316.1 25.5 %collective-permute-start.18 = (bf16[2,4,1,128,1024]{4,3,2,1,0:T(8,128)(2,1)S(1)}, bf16[2,4,1,128,1024]{4,3,2,1,0:T(8,128)(2,1)}, u32[]{:S(2)}, u32[]{:S(2)}) collective-permute-start(bf16[2,4,1,128,1024]{4,3,2,1,0:T(8,128)(2,1)S(1)} %shard_map.240), channel_id=1, source_target_pairs={{0,2},{2,0},{4,6},{6,4},{8,10},{10,8},{12,14},{14,12},{16,18},{18,... | collective-permute-start | bytes 6291464 | tf_op jit(solution)/shard_map/ppermute | solution.py:35
  344.8 31.4 %collective-permute-start.21 = (bf16[4,1,128,1024]{3,2,1,0:T(8,128)(2,1)S(1)}, bf16[4,1,128,1024]{3,2,1,0:T(8,128)(2,1)S(1)}, u32[]{:S(2)}, u32[]{:S(2)}) collective-permute-start(bf16[4,1,128,1024]{3,2,1,0:T(8,128)(2,1)S(1)} %get-tuple-element.273), channel_id=1, source_target_pairs={{0,4},{2,6},{4,0},{6,2},{8,12},{10,14},{12,8},{14,10},{16,20},{18,... | collective-permute-start | bytes 3145736 | tf_op jit(solution)/shard_map/ppermute | solution.py:35
  345.5 30.7 %collective-permute-start.22 = (bf16[1,128,1024]{2,1,0:T(8,128)(2,1)}, bf16[1,128,1024]{2,1,0:T(8,128)(2,1)S(1)}, u32[]{:S(2)}, u32[]{:S(2)}) collective-permute-start(bf16[1,128,1024]{2,1,0:T(8,128)(2,1)} %get-tuple-element.275), channel_id=1, source_target_pairs={{0,8},{2,10},{4,12},{6,14},{8,16},{10,18},{12,20},{14,22},{16,24},... | collective-permute-start | bytes 786440 | tf_op jit(solution)/shard_map/ppermute | solution.py:748
  376.3 25.9 %collective-permute-start.25 = (bf16[2,4,1,128,2048]{4,3,2,1,0:T(8,128)(2,1)}, bf16[2,4,1,128,2048]{4,3,2,1,0:T(8,128)(2,1)}, u32[]{:S(2)}, u32[]{:S(2)}) collective-permute-start(bf16[2,4,1,128,2048]{4,3,2,1,0:T(8,128)(2,1)} %get-tuple-element.290), channel_id=1, source_target_pairs={{0,2},{2,0},{4,6},{6,4},{8,10},{10,8},{12,14},{14,12},{16,18},{18,... | collective-permute-start | bytes 12582920 | tf_op jit(solution)/shard_map/ppermute | solution.py:35
  376.3 25.8 %collective-permute-start.29 = (bf16[4,1,128,1024]{3,2,1,0:T(8,128)(2,1)}, bf16[4,1,128,1024]{3,2,1,0:T(8,128)(2,1)S(1)}, u32[]{:S(2)}, u32[]{:S(2)}) collective-permute-start(bf16[4,1,128,1024]{3,2,1,0:T(8,128)(2,1)} %get-tuple-element.303), channel_id=1, source_target_pairs={{0,4},{2,6},{4,0},{6,2},{8,12},{10,14},{12,8},{14,10},{16,20},{18,... | collective-permute-start | bytes 3145736 | tf_op jit(solution)/shard_map/ppermute | solution.py:35
  407.9 32.8 %collective-permute-start.30 = (bf16[4,1,128,1024]{3,2,1,0:T(8,128)(2,1)}, bf16[4,1,128,1024]{3,2,1,0:T(8,128)(2,1)}, u32[]{:S(2)}, u32[]{:S(2)}) collective-permute-start(bf16[4,1,128,1024]{3,2,1,0:T(8,128)(2,1)} %get-tuple-element.315), channel_id=1, source_target_pairs={{0,4},{2,6},{4,0},{6,2},{8,12},{10,14},{12,8},{14,10},{16,20},{18,... | collective-permute-start | bytes 3145736 | tf_op jit(solution)/shard_map/ppermute | solution.py:35
  409.4 31.4 %collective-permute-start.34 = (bf16[2,128,2048]{2,1,0:T(8,128)(2,1)}, bf16[2,128,2048]{2,1,0:T(8,128)(2,1)}, u32[]{:S(2)}, u32[]{:S(2)}) collective-permute-start(bf16[2,128,2048]{2,1,0:T(8,128)(2,1)} %shard_map.247), channel_id=1, source_target_pairs={{0,1},{1,0},{2,3},{3,2},{4,5},{5,4},{6,7},{7,6},{8,9},{9,8},{10,11... | collective-permute-start | bytes 3145736 | tf_op jit(solution)/shard_map/ppermute | solution.py:35
  412.7 28.0 %collective-permute-start.31 = (bf16[1,128,1024]{2,1,0:T(8,128)(2,1)}, bf16[1,128,1024]{2,1,0:T(8,128)(2,1)S(1)}, u32[]{:S(2)}, u32[]{:S(2)}) collective-permute-start(bf16[1,128,1024]{2,1,0:T(8,128)(2,1)} %copy-done.58), channel_id=1, source_target_pairs={{0,8},{2,10},{4,12},{6,14},{8,16},{10,18},{12,20},{14,22},{16,24},... | collective-permute-start | bytes 786440 | tf_op jit(solution)/shard_map/ppermute | solution.py:748
  416.9 23.9 %collective-permute-start.32 = (bf16[1,128,1024]{2,1,0:T(8,128)(2,1)}, bf16[1,128,1024]{2,1,0:T(8,128)(2,1)S(1)}, u32[]{:S(2)}, u32[]{:S(2)}) collective-permute-start(bf16[1,128,1024]{2,1,0:T(8,128)(2,1)} %copy-done.57), channel_id=1, source_target_pairs={{0,16},{2,18},{4,20},{6,22},{8,24},{10,26},{12,28},{14,30},{16,0},... | collective-permute-start | bytes 786440 | tf_op jit(solution)/shard_map/ppermute | solution.py:748
  416.9 23.9 %collective-permute-start.33 = (bf16[1,128,1024]{2,1,0:T(8,128)(2,1)}, bf16[1,128,1024]{2,1,0:T(8,128)(2,1)S(1)}, u32[]{:S(2)}, u32[]{:S(2)}) collective-permute-start(bf16[1,128,1024]{2,1,0:T(8,128)(2,1)} %copy-done.56), channel_id=1, source_target_pairs={{0,24},{2,26},{4,28},{6,30},{8,0},{10,2},{12,4},{14,6},{16,8},{18,... | collective-permute-start | bytes 786440 | tf_op jit(solution)/shard_map/ppermute | solution.py:748
  443.4 30.0 %collective-permute-start.35 = (bf16[4,1,128,1024]{3,2,1,0:T(8,128)(2,1)S(1)}, bf16[4,1,128,1024]{3,2,1,0:T(8,128)(2,1)S(1)}, u32[]{:S(2)}, u32[]{:S(2)}) collective-permute-start(bf16[4,1,128,1024]{3,2,1,0:T(8,128)(2,1)S(1)} %copy-done.55), channel_id=1, source_target_pairs={{0,4},{2,6},{4,0},{6,2},{8,12},{10,14},{12,8},{14,10},{16,20},{18,... | collective-permute-start | bytes 3145736 | tf_op jit(solution)/shard_map/ppermute | solution.py:35
  444.9 28.4 %collective-permute-start.39 = (bf16[2,128,2048]{2,1,0:T(8,128)(2,1)S(1)}, bf16[2,128,2048]{2,1,0:T(8,128)(2,1)S(1)}, u32[]{:S(2)}, u32[]{:S(2)}) collective-permute-start(bf16[2,128,2048]{2,1,0:T(8,128)(2,1)S(1)} %copy-done.28), channel_id=1, source_target_pairs={{0,1},{1,0},{2,3},{3,2},{4,5},{5,4},{6,7},{7,6},{8,9},{9,8},{10,11... | collective-permute-start | bytes 3145736 | tf_op jit(solution)/shard_map/ppermute | solution.py:35
  445.2 27.3 %collective-permute-start.37 = (bf16[1,128,1024]{2,1,0:T(8,128)(2,1)S(1)}, bf16[1,128,1024]{2,1,0:T(8,128)(2,1)S(1)}, u32[]{:S(2)}, u32[]{:S(2)}) collective-permute-start(bf16[1,128,1024]{2,1,0:T(8,128)(2,1)S(1)} %get-tuple-element.339), channel_id=1, source_target_pairs={{0,16},{2,18},{4,20},{6,22},{8,24},{10,26},{12,28},{14,30},{16,0},... | collective-permute-start | bytes 786440 | tf_op jit(solution)/shard_map/ppermute | solution.py:748
  447.6 24.9 %collective-permute-start.38 = (bf16[1,128,1024]{2,1,0:T(8,128)(2,1)S(1)}, bf16[1,128,1024]{2,1,0:T(8,128)(2,1)S(1)}, u32[]{:S(2)}, u32[]{:S(2)}) collective-permute-start(bf16[1,128,1024]{2,1,0:T(8,128)(2,1)S(1)} %get-tuple-element.340), channel_id=1, source_target_pairs={{0,24},{2,26},{4,28},{6,30},{8,0},{10,2},{12,4},{14,6},{16,8},{18,... | collective-permute-start | bytes 786440 | tf_op jit(solution)/shard_map/ppermute | solution.py:748
  480.2 23.2 %collective-permute-start.41 = (bf16[1,128,1024]{2,1,0:T(8,128)(2,1)S(1)}, bf16[1,128,1024]{2,1,0:T(8,128)(2,1)S(1)}, u32[]{:S(2)}, u32[]{:S(2)}) collective-permute-start(bf16[1,128,1024]{2,1,0:T(8,128)(2,1)S(1)} %get-tuple-element.378), channel_id=1, source_target_pairs={{0,16},{2,18},{4,20},{6,22},{8,24},{10,26},{12,28},{14,30},{16,0},... | collective-permute-start | bytes 786440 | tf_op jit(solution)/shard_map/ppermute | solution.py:748
  481.4 22.0 %collective-permute-start.42 = (bf16[1,128,1024]{2,1,0:T(8,128)(2,1)S(1)}, bf16[1,128,1024]{2,1,0:T(8,128)(2,1)S(1)}, u32[]{:S(2)}, u32[]{:S(2)}) collective-permute-start(bf16[1,128,1024]{2,1,0:T(8,128)(2,1)S(1)} %get-tuple-element.379), channel_id=1, source_target_pairs={{0,24},{2,26},{4,28},{6,30},{8,0},{10,2},{12,4},{14,6},{16,8},{18,... | collective-permute-start | bytes 786440 | tf_op jit(solution)/shard_map/ppermute | solution.py:748
  (109 other events, 1020.2 us)
Sparse Core Ops, SparseCore 0:
  11.3 87.4 all-gather.8
  101.0 74.9 all-gather.4
  178.2 73.1 all-gather.6
  412.8 88.5 reduce-scatter.1

commit v6 on v5

--- a/solution.py
+++ b/solution.py
@@ -949,15 +949,15 @@
     _, along = step_sums([], [last_step("gate", "early"), last_step("out", "early", 1)])
     along, places_now, rank_grads = join(along, places_now, rank_grads)
     total["gate"] = along_moves(along[0])
-    for piece, left, right in (("gate_late", lefts[0], dgate[1]), ("out_late", lefts[1], gated[1])):
-        sent = grad_parts(places_now, False, (left,), (right,))
-        sent, places_now = join(sent, places_now)
-        got[piece] = swapped(sent, "dp", 1)
     rank_grad = sum(v[j] for v in rank_grads for j in range(v.shape[0]))
     select_terms = jnp.concatenate([rank_grad, unblocked(dins, states), unblocked(douts, states)], axis=2)
     select_terms, places_now = join(select_terms.reshape(tokens, -1), places_now)
     select_terms = tensor_sum(select_terms, bf16)
     places_now, total["gate"][1] = join(places_now, total["gate"][1])
+    for piece, left, right in (("gate_late", lefts[0], dgate[1]), ("out_late", lefts[1], gated[1])):
+        sent = grad_parts(places_now, False, (left,), (right,))
+        sent, places_now = join(sent, places_now)
+        got[piece] = swapped(sent, "dp", 1)
     for piece, left, right in (("gate_late", lefts[0], dgate[1]), ("out_late", lefts[1], gated[1])):
         kept[piece] = grad_parts(places_now, True, (left,), (right,))
     two = lax.axis_size("tensor") == 2

time: 528 us -> 525 us (level)
  starting transfers between devices: 68.5 us -> 60.9 us
  waiting for transfers between devices: 135 us -> 141 us
    ppermute x18, starting transfers between devices: 37.9 us -> 32.1 us  [along_moves(): lax.ppermute(v, 'dp', [(i, (i + 4 * (j + 1)) % count) for i in range(coun...]
  transfers between devices with their start and end apart: 48 -> 48, of which waited for: 20 -> 22; matrix products, arithmetic and copies ran while one was open for 9% -> 9% of each run, Pallas kernels for 40% -> 40%
where the time goes in v6:
time: 525 us; the launch traced here: 520 us
  Pallas kernels  225 us (43%)
  waiting for transfers between devices  141 us (27%)
  starting transfers between devices  60.9 us (12%)
  local copies, waits for them, and re-layouts  50.7 us (10%)
  other arithmetic  26 us (5%)
  between operations  15.2 us (3%)
    pallas_call x2, Pallas kernels, scan_both_ways(): pl.pallas_call(functools.partial(scan_kernel, states), grid=(blocks, micr...  109 us
    ppermute x18, waiting for transfers between devices, along_moves(): lax.ppermute(v, 'dp', [(i, (i + 4 * (j + 1)) % count) for i in range(coun...  47.5 us
    all_gather x2, waiting for transfers between devices, on_device(): both = lax.all_gather(both, 'dp', axis=1, tiled=True)  43 us
    pallas_call x4, Pallas kernels, project(): pl.pallas_call(functools.partial(project_kernel, len(terms)), grid_spec=p...  37.5 us
    ppermute x23, waiting for transfers between devices, swapped(): return lax.ppermute(values, axis, [(i, i ^ bit) for i in range(count)])  33.5 us
    ppermute x18, starting transfers between devices, along_moves(): lax.ppermute(v, 'dp', [(i, (i + 4 * (j + 1)) % count) for i in range(coun...  32.1 us
    ppermute x23, starting transfers between devices, swapped(): return lax.ppermute(values, axis, [(i, i ^ bit) for i in range(count)])  24.8 us
    unnamed x188, local copies, waits for them, and re-layouts  22.2 us
  transfers between devices with their start and end apart: 48, of which 22 were waited for; matrix products, arithmetic and copies ran while one was open for 9% of the time, Pallas kernels for 40%

profile of v6, /device:TPU:0, one launch (start us, length us, event | category | flops | bytes accessed | tf_op | source)
XLA Modules:
  0.0 520.3 jit_solution(7014378591268997606)
XLA Ops:
  28.5 9.8 %collective-permute-done.3 = f32[8,3072]{1,0:T(8,128)S(1)} collective-permute-done((f32[8,3072]{1,0:T(8,128)S(1)}, f32[8,3072]{1,0:T(8,128)S(1)}, u32[]{:S(2)}, u32[]{:S(2)}) %collective-permute-start.3) | collective-permute-done | bytes 98336 | tf_op jit(solution)/shard_map/ppermute | solution.py:35
  56.3 7.2 %collective-permute-done.8 = bf16[4,288,128]{2,1,0:T(8,128)(2,1)S(1)} collective-permute-done((bf16[4,288,128]{2,1,0:T(8,128)(2,1)S(1)}, bf16[4,288,128]{2,1,0:T(8,128)(2,1)S(1)}, u32[]{:S(2)}, u32[]{:S(2)}) %collective-permute-start.8) | collective-permute-done | bytes 294944 | tf_op jit(solution)/shard_map/ppermute | solution.py:35
  86.9 11.9 %all-gather.9.cloned.1.call-done = bf16[2048,1,2048]{2,0,1:T(8,128)(2,1)} async-done(((bf16[128,1,2048]{2,0,1:T(8,128)(2,1)}), bf16[2048,1,2048]{2,0,1:T(8,128)(2,1)}) %all-gather.9.cloned.1.call-update) | async-done | bytes 8388624 | tf_op jit(solution)/shard_map/all_gather | solution.py:851
  100.4 13.2 %shard_map.229 = (f32[512,2048]{1,0:T(8,128)}, f32[512,2048]{1,0:T(8,128)}, bf16[512,2048]{1,0:T(8,128)(2,1)S(1)}, f32[512,160]{1,0:T(8,128)}) custom-call(bf16[512,2048]{1,0:T(8,128)(2,1)S(1)} %copy-done.3, bf16[2048,2048]{1,0:T(8,128)(2,1)} %bitcast.232, f32[512,4]{1,0:T(8,128)S(1)} %stack.68.refs_1_.refs_7_, f32[4,2048]{1,0:T(4,128)S(1)} %bitcast.227, ...), custom_call_target="tpu_custom_call" | custom-call | flops 1 | bytes 1 | tf_op jit(solution)/shard_map/pallas_call | solution.py:436
  118.3 4.0 copy.158
  122.3 5.7 %collective-permute-done.10 = f32[512,160]{1,0:T(8,128)} collective-permute-done((f32[512,160]{1,0:T(8,128)}, f32[512,160]{1,0:T(8,128)}, u32[]{:S(2)}, u32[]{:S(2)}) %collective-permute-start.10) | collective-permute-done | bytes 327712 | tf_op jit(solution)/shard_map/ppermute | solution.py:35
  129.3 5.1 shard_map.230
  138.6 37.4 %all-gather.5.cloned.1.call-done.gate_weight_ref.out_weight_ref.refs_2_.refs_3_ = bf16[2,2048,1024]{2,1,0:T(8,128)(2,1)} async-done(((bf16[2,128,1024]{2,1,0:T(8,128)(2,1)}), bf16[2,2048,1024]{2,1,0:T(8,128)(2,1)}) %all-gather.5.cloned.1.call-update) | async-done | bytes 8388624 | tf_op jit(solution)/shard_map/all_gather | solution.py:856
  176.0 54.5 %shard_map.231 = (bf16[2,256,1024]{2,1,0:T(8,128)(2,1)}, bf16[2,256,1024]{2,1,0:T(8,128)(2,1)}, f32[2,256,1024]{2,1,0:T(8,128)}, f32[128,1024]{1,0:T(8,128)}, f3...) custom-call(f32[2,256,2048]{2,1,0:T(8,128)} %bitcast.204, ...), custom_call_target="tpu_custom_call" | custom-call | flops 1 | bytes 1 | tf_op jit(solution)/shard_map/pallas_call | solution.py:286
  245.8 5.5 %all-gather.7.cloned.1.call-done.gate_weight_ref.out_weight_ref.refs_3_.refs_4_ = bf16[2,2048,1024]{2,1,0:T(8,128)(2,1)} async-done(((bf16[2,128,1024]{2,1,0:T(8,128)(2,1)}), bf16[2,2048,1024]{2,1,0:T(8,128)(2,1)}) %all-gather.7.cloned.1.call-update) | async-done | bytes 8388624 | tf_op jit(solution)/shard_map/all_gather | solution.py:856
  251.4 54.9 %shard_map.237 = (bf16[2,256,1024]{2,1,0:T(8,128)(2,1)}, bf16[2,256,1024]{2,1,0:T(8,128)(2,1)}, f32[2,256,1024]{2,1,0:T(8,128)}, f32[128,1024]{1,0:T(8,128)}, f3...) custom-call(f32[2,256,2048]{2,1,0:T(8,128)} %bitcast.205, ...), custom_call_target="tpu_custom_call" | custom-call | flops 1 | bytes 1 | tf_op jit(solution)/shard_map/pallas_call | solution.py:286
  312.1 8.2 %collective-permute-done.16.refs_1_ = bf16[1,128,1024]{2,1,0:T(8,128)(2,1)S(1)} collective-permute-done((bf16[1,128,1024]{2,1,0:T(8,128)(2,1)S(1)}, bf16[1,128,1024]{2,1,0:T(8,128)(2,1)S(1)}, u32[]{:S(2)}, u32[]{:S(2)}) %collective-permute-start.16) | collective-permute-done | bytes 262176 | tf_op jit(solution)/shard_map/ppermute | solution.py:748
  336.4 7.6 %shard_map.243 = bf16[2,128,2048]{2,1,0:T(8,128)(2,1)S(1)} custom-call(s32[1]{0:T(128)S(6)} %sub.105.where_ref, bf16[2,256,1024]{2,1,0:T(8,128)(2,1)S(1)} %copy-done.12, bf16[2,256,1024]{2,1,0:T(8,128)(2,1)S(1)} %copy-done.15, bf16[2,2048,1024]{2,1,0:T(8,128)(2,1)} %all-gather.5.cloned.1.call-done.gate_weight_ref.out_weight_ref.refs_2_.refs_3_, ...), custom_call_target="tpu_custom_call" | custom-call | flops 1 | bytes 1 | tf_op jit(solution)/shard_map/pallas_call | solution.py:605
  352.8 16.9 %shard_map.245 = (bf16[512,2048]{1,0:T(8,128)(2,1)}, f32[8,2048]{1,0:T(8,128)S(1)}, f32[160,2048]{1,0:T(8,128)}, bf16[2,4,1,128,2048]{4,3,2,1,0:T(8,128)(2,1)}, bf16[2,4,1,128,2048]{4,3,2,1,0:T(8,128)(2,1)}) custom-call(s32[16]{0:T(128)S(1)} %fusion.40.places_ref, f32[512,1024]{1,0:T(8,128)} %bitcast.248, f32[512,1024]{1,0:T(8,128)} %bitcast.249, ...), custom_call_target="tpu_custom_call" | custom-call | flops 1 | bytes 1 | tf_op jit(solution)/shard_map/pallas_call | solution.py:552
  383.2 11.2 %shard_map.247 = bf16[2,128,2048]{2,1,0:T(8,128)(2,1)} custom-call(s32[1]{0:T(128)S(6)} %sub.106.where_ref, bf16[2,256,1024]{2,1,0:T(8,128)(2,1)S(1)} %copy-done.14, bf16[2,256,1024]{2,1,0:T(8,128)(2,1)S(1)} %copy-done.17, bf16[2,256,2048]{2,1,0:T(8,128)(2,1)S(1)} %bitcast.217, ...), custom_call_target="tpu_custom_call" | custom-call | flops 1 | bytes 1 | tf_op jit(solution)/shard_map/pallas_call | solution.py:605
  398.4 4.1 shard_map.248
  408.1 5.1 collective-permute-start.31
  415.7 11.2 %shard_map.249 = f32[2,128,2048]{2,1,0:T(8,128)S(1)} custom-call(s32[1]{0:T(128)} %bitcast.56.where_ref, bf16[2,256,1024]{2,1,0:T(8,128)(2,1)S(1)} %copy-done.14, bf16[2,256,1024]{2,1,0:T(8,128)(2,1)S(1)} %copy-done.18, bf16[2,256,2048]{2,1,0:T(8,128)(2,1)} %bitcast.216, ...), custom_call_target="tpu_custom_call" | custom-call | flops 1 | bytes 1 | tf_op jit(solution)/shard_map/pallas_call | solution.py:605
  428.2 7.6 %shard_map.250 = f32[2,128,2048]{2,1,0:T(8,128)S(1)} custom-call(s32[1]{0:T(128)} %bitcast.56.where_ref, bf16[2,256,1024]{2,1,0:T(8,128)(2,1)S(1)} %copy-done.12, bf16[2,256,1024]{2,1,0:T(8,128)(2,1)S(1)} %copy-done.16, bf16[2,2048,1024]{2,1,0:T(8,128)(2,1)} %all-gather.5.cloned.1.call-done.gate_weight_ref.out_weight_ref.refs_2_.refs_3_, ...), custom_call_target="tpu_custom_call" | custom-call | flops 1 | bytes 1 | tf_op jit(solution)/shard_map/pallas_call | solution.py:605
  445.9 9.3 %collective-permute-done.36.refs_1_ = bf16[1,128,1024]{2,1,0:T(8,128)(2,1)S(1)} collective-permute-done((bf16[1,128,1024]{2,1,0:T(8,128)(2,1)S(1)}, bf16[1,128,1024]{2,1,0:T(8,128)(2,1)S(1)}, u32[]{:S(2)}, u32[]{:S(2)}) %collective-permute-start.36) | collective-permute-done | bytes 262176 | tf_op jit(solution)/shard_map/ppermute | solution.py:748
  455.4 14.6 %collective-permute-done.37.refs_2_ = bf16[1,128,1024]{2,1,0:T(8,128)(2,1)S(1)} collective-permute-done((bf16[1,128,1024]{2,1,0:T(8,128)(2,1)S(1)}, bf16[1,128,1024]{2,1,0:T(8,128)(2,1)S(1)}, u32[]{:S(2)}, u32[]{:S(2)}) %collective-permute-start.37) | collective-permute-done | bytes 262176 | tf_op jit(solution)/shard_map/ppermute | solution.py:748
  472.2 5.7 %collective-permute-start.40 = (bf16[1,128,1024]{2,1,0:T(8,128)(2,1)S(1)}, bf16[1,128,1024]{2,1,0:T(8,128)(2,1)S(1)}, u32[]{:S(2)}, u32[]{:S(2)}) collective-permute-start(bf16[1,128,1024]{2,1,0:T(8,128)(2,1)S(1)} %get-tuple-element.377), channel_id=1, source_target_pairs={{0,8},{2,10},{4,12},{6,14},{8,16},{10,18},{12,20},{14,22},{16,24},... | collective-permute-start | bytes 786440 | tf_op jit(solution)/shard_map/ppermute | solution.py:748
  482.0 5.6 %shard_map.257 = (f32[256,2048]{1,0:T(8,128)}, f32[256,2048]{1,0:T(8,128)}) custom-call(f32[256,2048]{1,0:T(8,128)S(1)} %bitcast.201, bf16[256,2048]{1,0:T(8,128)(2,1)} %bitcast.1.cot_ref, f32[1,2048]{1,0:T(1,128)S(1)} %bitcast.231, f32[256,2048]{1,0:T(8,128)} %bitcast.219, bf16[256,2048]{1,0:T(8,128)(2,1)S(1)} %bitcast.224, f32[256,2048]{1,0:T(8,128)} %bitcast.218, ...), custom_call_target="tpu_custom_call" | custom-call | flops 1 | bytes 1 | tf_op jit(solution)/shard_map/pallas_call | solution.py:804
  489.3 11.9 %collective-permute-done.41.refs_2_ = bf16[1,128,1024]{2,1,0:T(8,128)(2,1)S(1)} collective-permute-done((bf16[1,128,1024]{2,1,0:T(8,128)(2,1)S(1)}, bf16[1,128,1024]{2,1,0:T(8,128)(2,1)S(1)}, u32[]{:S(2)}, u32[]{:S(2)}) %collective-permute-start.41) | collective-permute-done | bytes 262176 | tf_op jit(solution)/shard_map/ppermute | solution.py:748
  (379 shorter events, 177.0 us)
Async XLA Ops:
  7.2 91.6 %all-gather.9.cloned.1.call-start = ((), (), s32[]{:S(2)}) async-start(), calls=%async_computation.4 | async-start | bytes 8912896 | tf_op jit(solution)/shard_map/all_gather | solution.py:851
  11.2 164.8 %all-gather.5.cloned.1.call-start = ((), (), s32[]{:S(2)}) async-start(), calls=%async_computation.1 | async-start | bytes 8912896 | tf_op jit(solution)/shard_map/all_gather | solution.py:856
  12.6 238.8 %all-gather.7.cloned.1.call-start = ((), (), s32[]{:S(2)}) async-start(), calls=%async_computation.2 | async-start | bytes 8912896 | tf_op jit(solution)/shard_map/all_gather | solution.py:856
  13.5 493.4 %reduce-scatter.2.cloned.1.call-start = ((), (), s32[]{:S(2)}) async-start(), calls=%async_computation.3 | async-start | bytes 2785280 | tf_op jit(solution)/shard_map/reduce_scatter | solution.py:1019
  40.3 24.3 %collective-permute-start.4 = (bf16[2,128,2048]{2,1,0:T(8,128)(2,1)}, bf16[2,128,2048]{2,1,0:T(8,128)(2,1)}, u32[]{:S(2)}, u32[]{:S(2)}) collective-permute-start(bf16[2,128,2048]{2,1,0:T(8,128)(2,1)} %multiply_convert_fusion), channel_id=1, source_target_pairs={{0,1},{1,0},{2,3},{3,2},{4,5},{5,4},{6,7},{7,6},{8,9},{9,8},{10,11... | collective-permute-start | bytes 3145736 | tf_op jit(solution)/shard_map/ppermute | solution.py:35
  70.9 44.2 %collective-permute-start.11 = (bf16[2,128,2048]{2,1,0:T(8,128)(2,1)}, bf16[2,128,2048]{2,1,0:T(8,128)(2,1)}, u32[]{:S(2)}, u32[]{:S(2)}) collective-permute-start(bf16[2,128,2048]{2,1,0:T(8,128)(2,1)} %param.15), channel_id=1, source_target_pairs={{0,1},{1,0},{2,3},{3,2},{4,5},{5,4},{6,7},{7,6},{8,9},{9,8},{10,11... | collective-permute-start | bytes 3145736 | tf_op jit(solution)/shard_map/ppermute | solution.py:35
  245.2 61.1 %collective-permute-start.14 = (bf16[4,1,128,2048]{3,2,1,0:T(8,128)(2,1)}, bf16[4,1,128,2048]{3,2,1,0:T(8,128)(2,1)}, u32[]{:S(2)}, u32[]{:S(2)}) collective-permute-start(bf16[4,1,128,2048]{3,2,1,0:T(8,128)(2,1)} %shard_map.236), channel_id=1, source_target_pairs={{0,4},{2,6},{4,0},{6,2},{8,12},{10,14},{12,8},{14,10},{16,20},{18,... | collective-permute-start | bytes 6291464 | tf_op jit(solution)/shard_map/ppermute | solution.py:35
  325.4 19.7 %collective-permute-start.17 = (bf16[2,4,1,128,1024]{4,3,2,1,0:T(8,128)(2,1)}, bf16[2,4,1,128,1024]{4,3,2,1,0:T(8,128)(2,1)}, u32[]{:S(2)}, u32[]{:S(2)}) collective-permute-start(bf16[2,4,1,128,1024]{4,3,2,1,0:T(8,128)(2,1)} %shard_map.239), channel_id=1, source_target_pairs={{0,2},{2,0},{4,6},{6,4},{8,10},{10,8},{12,14},{14,12},{16,18},{18,... | collective-permute-start | bytes 6291464 | tf_op jit(solution)/shard_map/ppermute | solution.py:35
  348.3 24.4 %collective-permute-start.21 = (bf16[4,1,128,1024]{3,2,1,0:T(8,128)(2,1)S(1)}, bf16[4,1,128,1024]{3,2,1,0:T(8,128)(2,1)S(1)}, u32[]{:S(2)}, u32[]{:S(2)}) collective-permute-start(bf16[4,1,128,1024]{3,2,1,0:T(8,128)(2,1)S(1)} %get-tuple-element.273), channel_id=1, source_target_pairs={{0,4},{2,6},{4,0},{6,2},{8,12},{10,14},{12,8},{14,10},{16,20},{18,... | collective-permute-start | bytes 3145736 | tf_op jit(solution)/shard_map/ppermute | solution.py:35
  348.9 20.8 %collective-permute-start.22 = (bf16[1,128,1024]{2,1,0:T(8,128)(2,1)}, bf16[1,128,1024]{2,1,0:T(8,128)(2,1)S(1)}, u32[]{:S(2)}, u32[]{:S(2)}) collective-permute-start(bf16[1,128,1024]{2,1,0:T(8,128)(2,1)} %get-tuple-element.275), channel_id=1, source_target_pairs={{0,8},{2,10},{4,12},{6,14},{8,16},{10,18},{12,20},{14,22},{16,24},... | collective-permute-start | bytes 786440 | tf_op jit(solution)/shard_map/ppermute | solution.py:748
  372.7 25.8 %collective-permute-start.25 = (bf16[2,4,1,128,2048]{4,3,2,1,0:T(8,128)(2,1)}, bf16[2,4,1,128,2048]{4,3,2,1,0:T(8,128)(2,1)}, u32[]{:S(2)}, u32[]{:S(2)}) collective-permute-start(bf16[2,4,1,128,2048]{4,3,2,1,0:T(8,128)(2,1)} %get-tuple-element.290), channel_id=1, source_target_pairs={{0,2},{2,0},{4,6},{6,4},{8,10},{10,8},{12,14},{14,12},{16,18},{18,... | collective-permute-start | bytes 12582920 | tf_op jit(solution)/shard_map/ppermute | solution.py:35
  372.7 25.8 %collective-permute-start.29 = (bf16[4,1,128,1024]{3,2,1,0:T(8,128)(2,1)}, bf16[4,1,128,1024]{3,2,1,0:T(8,128)(2,1)S(1)}, u32[]{:S(2)}, u32[]{:S(2)}) collective-permute-start(bf16[4,1,128,1024]{3,2,1,0:T(8,128)(2,1)} %get-tuple-element.303), channel_id=1, source_target_pairs={{0,4},{2,6},{4,0},{6,2},{8,12},{10,14},{12,8},{14,10},{16,20},{18,... | collective-permute-start | bytes 3145736 | tf_op jit(solution)/shard_map/ppermute | solution.py:35
  374.8 19.7 %collective-permute-start.26 = (bf16[1,128,1024]{2,1,0:T(8,128)(2,1)S(1)}, bf16[1,128,1024]{2,1,0:T(8,128)(2,1)S(1)}, u32[]{:S(2)}, u32[]{:S(2)}) collective-permute-start(bf16[1,128,1024]{2,1,0:T(8,128)(2,1)S(1)} %get-tuple-element.300), channel_id=1, source_target_pairs={{0,8},{2,10},{4,12},{6,14},{8,16},{10,18},{12,20},{14,22},{16,24},... | collective-permute-start | bytes 786440 | tf_op jit(solution)/shard_map/ppermute | solution.py:748
  404.3 32.9 %collective-permute-start.30 = (bf16[4,1,128,1024]{3,2,1,0:T(8,128)(2,1)}, bf16[4,1,128,1024]{3,2,1,0:T(8,128)(2,1)}, u32[]{:S(2)}, u32[]{:S(2)}) collective-permute-start(bf16[4,1,128,1024]{3,2,1,0:T(8,128)(2,1)} %get-tuple-element.315), channel_id=1, source_target_pairs={{0,4},{2,6},{4,0},{6,2},{8,12},{10,14},{12,8},{14,10},{16,20},{18,... | collective-permute-start | bytes 3145736 | tf_op jit(solution)/shard_map/ppermute | solution.py:35
  404.8 32.4 %collective-permute-start.34 = (bf16[2,128,2048]{2,1,0:T(8,128)(2,1)}, bf16[2,128,2048]{2,1,0:T(8,128)(2,1)}, u32[]{:S(2)}, u32[]{:S(2)}) collective-permute-start(bf16[2,128,2048]{2,1,0:T(8,128)(2,1)} %shard_map.247), channel_id=1, source_target_pairs={{0,1},{1,0},{2,3},{3,2},{4,5},{5,4},{6,7},{7,6},{8,9},{9,8},{10,11... | collective-permute-start | bytes 3145736 | tf_op jit(solution)/shard_map/ppermute | solution.py:35
  408.1 29.0 %collective-permute-start.31 = (bf16[1,128,1024]{2,1,0:T(8,128)(2,1)}, bf16[1,128,1024]{2,1,0:T(8,128)(2,1)S(1)}, u32[]{:S(2)}, u32[]{:S(2)}) collective-permute-start(bf16[1,128,1024]{2,1,0:T(8,128)(2,1)} %copy-done.58), channel_id=1, source_target_pairs={{0,8},{2,10},{4,12},{6,14},{8,16},{10,18},{12,20},{14,22},{16,24},... | collective-permute-start | bytes 786440 | tf_op jit(solution)/shard_map/ppermute | solution.py:748
  413.2 23.9 %collective-permute-start.32 = (bf16[1,128,1024]{2,1,0:T(8,128)(2,1)}, bf16[1,128,1024]{2,1,0:T(8,128)(2,1)S(1)}, u32[]{:S(2)}, u32[]{:S(2)}) collective-permute-start(bf16[1,128,1024]{2,1,0:T(8,128)(2,1)} %copy-done.57), channel_id=1, source_target_pairs={{0,16},{2,18},{4,20},{6,22},{8,24},{10,26},{12,28},{14,30},{16,0},... | collective-permute-start | bytes 786440 | tf_op jit(solution)/shard_map/ppermute | solution.py:748
  415.1 22.1 %collective-permute-start.33 = (bf16[1,128,1024]{2,1,0:T(8,128)(2,1)}, bf16[1,128,1024]{2,1,0:T(8,128)(2,1)S(1)}, u32[]{:S(2)}, u32[]{:S(2)}) collective-permute-start(bf16[1,128,1024]{2,1,0:T(8,128)(2,1)} %copy-done.56), channel_id=1, source_target_pairs={{0,24},{2,26},{4,28},{6,30},{8,0},{10,2},{12,4},{14,6},{16,8},{18,... | collective-permute-start | bytes 786440 | tf_op jit(solution)/shard_map/ppermute | solution.py:748
  439.5 31.0 %collective-permute-start.35 = (bf16[4,1,128,1024]{3,2,1,0:T(8,128)(2,1)S(1)}, bf16[4,1,128,1024]{3,2,1,0:T(8,128)(2,1)S(1)}, u32[]{:S(2)}, u32[]{:S(2)}) collective-permute-start(bf16[4,1,128,1024]{3,2,1,0:T(8,128)(2,1)S(1)} %copy-done.55), channel_id=1, source_target_pairs={{0,4},{2,6},{4,0},{6,2},{8,12},{10,14},{12,8},{14,10},{16,20},{18,... | collective-permute-start | bytes 3145736 | tf_op jit(solution)/shard_map/ppermute | solution.py:35
  440.3 30.1 %collective-permute-start.39 = (bf16[2,128,2048]{2,1,0:T(8,128)(2,1)S(1)}, bf16[2,128,2048]{2,1,0:T(8,128)(2,1)S(1)}, u32[]{:S(2)}, u32[]{:S(2)}) collective-permute-start(bf16[2,128,2048]{2,1,0:T(8,128)(2,1)S(1)} %copy-done.28), channel_id=1, source_target_pairs={{0,1},{1,0},{2,3},{3,2},{4,5},{5,4},{6,7},{7,6},{8,9},{9,8},{10,11... | collective-permute-start | bytes 3145736 | tf_op jit(solution)/shard_map/ppermute | solution.py:35
  442.9 27.0 %collective-permute-start.37 = (bf16[1,128,1024]{2,1,0:T(8,128)(2,1)S(1)}, bf16[1,128,1024]{2,1,0:T(8,128)(2,1)S(1)}, u32[]{:S(2)}, u32[]{:S(2)}) collective-permute-start(bf16[1,128,1024]{2,1,0:T(8,128)(2,1)S(1)} %get-tuple-element.339), channel_id=1, source_target_pairs={{0,16},{2,18},{4,20},{6,22},{8,24},{10,26},{12,28},{14,30},{16,0},... | collective-permute-start | bytes 786440 | tf_op jit(solution)/shard_map/ppermute | solution.py:748
  443.9 26.1 %collective-permute-start.38 = (bf16[1,128,1024]{2,1,0:T(8,128)(2,1)S(1)}, bf16[1,128,1024]{2,1,0:T(8,128)(2,1)S(1)}, u32[]{:S(2)}, u32[]{:S(2)}) collective-permute-start(bf16[1,128,1024]{2,1,0:T(8,128)(2,1)S(1)} %get-tuple-element.340), channel_id=1, source_target_pairs={{0,24},{2,26},{4,28},{6,30},{8,0},{10,2},{12,4},{14,6},{16,8},{18,... | collective-permute-start | bytes 786440 | tf_op jit(solution)/shard_map/ppermute | solution.py:748
  477.9 23.3 %collective-permute-start.41 = (bf16[1,128,1024]{2,1,0:T(8,128)(2,1)S(1)}, bf16[1,128,1024]{2,1,0:T(8,128)(2,1)S(1)}, u32[]{:S(2)}, u32[]{:S(2)}) collective-permute-start(bf16[1,128,1024]{2,1,0:T(8,128)(2,1)S(1)} %get-tuple-element.378), channel_id=1, source_target_pairs={{0,16},{2,18},{4,20},{6,22},{8,24},{10,26},{12,28},{14,30},{16,0},... | collective-permute-start | bytes 786440 | tf_op jit(solution)/shard_map/ppermute | solution.py:748
  479.1 22.1 %collective-permute-start.42 = (bf16[1,128,1024]{2,1,0:T(8,128)(2,1)S(1)}, bf16[1,128,1024]{2,1,0:T(8,128)(2,1)S(1)}, u32[]{:S(2)}, u32[]{:S(2)}) collective-permute-start(bf16[1,128,1024]{2,1,0:T(8,128)(2,1)S(1)} %get-tuple-element.379), channel_id=1, source_target_pairs={{0,24},{2,26},{4,28},{6,30},{8,0},{10,2},{12,4},{14,6},{16,8},{18,... | collective-permute-start | bytes 786440 | tf_op jit(solution)/shard_map/ppermute | solution.py:748
  (109 other events, 1021.5 us)
Sparse Core Ops, SparseCore 0:
  11.3 87.4 all-gather.8
  101.0 74.9 all-gather.4
  178.2 73.1 all-gather.6
  408.3 91.1 reduce-scatter.1
